TPU v7x, 128 devices: a whole 4x4x4 slice. The times are simulated.
128 devices in a mesh: clus: 32 (over z, x, core), grp: 4 (over y).
Axes of the slice: x: 4, y: 4, z: 4, core: 2. Of those that a mesh axis runs over, the one named last changes fastest.
Arguments:
- right_sides: float32 [1024, 16, 256], P(('clus', 'grp')), may hold values from -6 to 6
- diag_shift: float32 [1024, 256], P(('clus', 'grp')), may hold values from 2 to 4
- self_blocks: bfloat16 [1024, 256, 256], P(('clus', 'grp')), may hold values from -0.03125 to 0.03125
- near_blocks: bfloat16 [3072, 256, 256], P(('clus', 'grp')), may hold values from -0.03125 to 0.03125
- far_left: bfloat16 [12288, 32, 256], P(('clus', 'grp')), may hold values from -0.0625 to 0.0625
- far_right: bfloat16 [12288, 32, 256], P(('clus', 'grp')), may hold values from -0.0625 to 0.0625
- far_rank: int32 [12288], P(('clus', 'grp')), may hold values from 8 to 32
- send_leaf: int32 [128, 128, 1], P(('clus', 'grp')), may hold values from 0 to 7, as said below
- block_pos: int32 [2, 15360], P(None, ('clus', 'grp')), may hold values from 0 to 127, as said below
Outputs:
- solution: float32 [1024, 16, 256], P(('clus', 'grp'))
- residual: float32 [1024, 16, 256], P(('clus', 'grp'))
Inputs may be any that keep to these rules, and one draw needn't show every extreme that they name: For each sender s and owner o the 1 entries send_leaf[s, o, :] are distinct leaves of s. `block_pos`: each owner's block positions name every one of its 32 * 4 * 1 slot positions at least once.
All inputs are finite; a program needn't handle non-finite values.
Results may differ from a plain program's by a relative error of at most 0.0019.
Values may be sent and summed in bfloat16 or wider, within the bound.
No kernel may reach another device: no remote copies, remote signals or barrier semaphores. Data moves between devices by JAX's collectives and lax.ppermute only.
A program may use at most 64 MiB of HBM per device.

v0:
```python
import jax
import jax.numpy as jnp
from jax import lax
from jax.sharding import PartitionSpec as P

ITERS = 2


def inner_gram(left_field, right_field):
    return jnp.einsum("lri,lsi->rs", left_field, right_field, precision=lax.Precision.HIGHEST)


def combine_cols(field, coefs):
    return jnp.einsum("lri,rs->lsi", field, coefs, precision=lax.Precision.HIGHEST)


def small_solve(matrix, target):
    factor = jnp.linalg.cholesky(matrix)
    return jax.scipy.linalg.cho_solve((factor, True), target)


def shards(
    right_sides,
    diag_shift,
    self_blocks,
    near_blocks,
    far_left,
    far_right,
    far_rank,
    send_leaf,
    block_pos,
):
    leaf_dev, rhs_count, leaf_size = right_sides.shape
    near_count = near_blocks.shape[0]
    devices = lax.axis_size(("clus", "grp"))
    targets = send_leaf[0]
    slot_count = targets.shape[1]
    flat_targets = targets.reshape(-1)
    rows_at = block_pos[0]
    cols_at = block_pos[1]
    rank_mask = (
        jnp.arange(far_left.shape[1], dtype=jnp.int32)[None, :] < far_rank[:, None]
    ).astype(jnp.float32)
    positions = devices * slot_count
    solution = jnp.zeros_like(right_sides)
    residual = right_sides
    direction = right_sides
    res_gram = lax.psum(inner_gram(residual, residual), ("clus", "grp"))
    for iteration in range(ITERS):
        halved = direction.astype(jnp.bfloat16)
        outgoing = halved[flat_targets].reshape(devices, slot_count, rhs_count, leaf_size)
        incoming = lax.all_to_all(
            outgoing, ("clus", "grp"), split_axis=0, concat_axis=0, tiled=True
        )
        base = diag_shift[:, None, :] * direction
        base = base + jnp.einsum(
            "lij,lrj->lri", self_blocks, halved, preferred_element_type=jnp.float32
        )
        base = base + jnp.einsum(
            "lij,lri->lrj", self_blocks, halved, preferred_element_type=jnp.float32
        )
        received = incoming.reshape(positions, rhs_count, leaf_size)
        x_row = received[rows_at]
        x_col = received[cols_at]
        rows_near = jnp.einsum(
            "bij,brj->bri", near_blocks, x_col[:near_count], preferred_element_type=jnp.float32
        )
        cols_near = jnp.einsum(
            "bij,bri->brj", near_blocks, x_row[:near_count], preferred_element_type=jnp.float32
        )
        right_proj = (
            jnp.einsum(
                "bkj,brj->bkr", far_right, x_col[near_count:], preferred_element_type=jnp.float32
            )
            * rank_mask[:, :, None]
        ).astype(jnp.bfloat16)
        left_proj = (
            jnp.einsum(
                "bki,bri->bkr", far_left, x_row[near_count:], preferred_element_type=jnp.float32
            )
            * rank_mask[:, :, None]
        ).astype(jnp.bfloat16)
        rows_far = jnp.einsum(
            "bki,bkr->bri", far_left, right_proj, preferred_element_type=jnp.float32
        )
        cols_far = jnp.einsum(
            "bkj,bkr->brj", far_right, left_proj, preferred_element_type=jnp.float32
        )
        summed = jax.ops.segment_sum(
            jnp.concatenate([rows_near, rows_far], axis=0), rows_at, num_segments=positions
        )
        summed = summed + jax.ops.segment_sum(
            jnp.concatenate([cols_near, cols_far], axis=0), cols_at, num_segments=positions
        )
        returned = lax.all_to_all(
            summed.reshape(devices, slot_count, rhs_count, leaf_size),
            ("clus", "grp"),
            split_axis=0,
            concat_axis=0,
            tiled=True,
        )
        gathered = jax.ops.segment_sum(
            returned.reshape(positions, rhs_count, leaf_size), flat_targets, num_segments=leaf_dev
        )
        product = base + gathered
        curvature = lax.psum(inner_gram(direction, product), ("clus", "grp"))
        step_coef = small_solve(curvature, res_gram)
        solution = solution + combine_cols(direction, step_coef)
        residual = residual - combine_cols(product, step_coef)
        if iteration + 1 < ITERS:
            next_gram = lax.psum(inner_gram(residual, residual), ("clus", "grp"))
            dir_coef = small_solve(res_gram, next_gram)
            direction = residual + combine_cols(direction, dir_coef)
            res_gram = next_gram
    return (solution, residual)


def solution(mesh):
    placed = (
        P(("clus", "grp"), None, None),
        P(("clus", "grp"), None),
        P(("clus", "grp"), None, None),
        P(("clus", "grp"), None, None),
        P(("clus", "grp"), None, None),
        P(("clus", "grp"), None, None),
        P(("clus", "grp")),
        P(("clus", "grp"), None, None),
        P(None, ("clus", "grp")),
    )
    return jax.shard_map(
        shards,
        mesh=mesh,
        in_specs=placed,
        out_specs=(P(("clus", "grp"), None, None), P(("clus", "grp"), None, None)),
        check_vma=False,
    )
```

profile of v0, /device:TPU:1, one launch (start us, length us, event | category | flops | bytes accessed | tf_op | source)
XLA Modules:
  0.0 485.7 jit_solution(15078852858996218079)
XLA Ops:
  2.5 1.7 gather_fusion
  4.2 12.0 %all-to-all-start = ((bf16[128,1,16,256]{3,2,1,0:T(8,128)(2,1)}), bf16[128,1,16,256]{3,2,1,0:T(8,128)(2,1)}, u32[]{:S(2)}, u32[]{:S(2)}) async-start(bf16[128,1,16,256]{3,2,1,0:T(8,128)(2,1)} %bitcast.152), calls=%async_computation | async-start | bytes 2097152 | tf_op jit(solution)/shard_map/all_to_all | solution.py:52
  16.4 18.9 %all-to-all-done = bf16[128,1,16,256]{3,2,1,0:T(8,128)(2,1)} async-done(((bf16[128,1,16,256]{3,2,1,0:T(8,128)(2,1)}), bf16[128,1,16,256]{3,2,1,0:T(8,128)(2,1)}, u32[]{:S(2)}, u32[]{:S(2)}) %all-to-all-start) | async-done | bytes 1048608 | tf_op jit(solution)/shard_map/all_to_all | solution.py:52
  35.3 2.9 gather_fusion.2
  38.2 2.9 gather_fusion.1
  41.1 1.5 fusion.36
  46.9 1.4 pad_maximum_fusion.1
  48.4 1.4 pad_maximum_fusion
  49.8 1.6 broadcast.125.clone.1
  51.4 17.3 %scatter_fusion.1 = f32[128,16,256]{2,1,0:T(8,128)} fusion(f32[128,16,256]{2,1,0:T(8,128)} %broadcast.125.clone.1, s32[120]{0:T(128)S(1)} %get-tuple-element.8, f32[120,16,256]{2,1,0:T(8,128)} %pad_maximum_fusion.1), kind=kCustom, calls=%fused_computation.7 | custom fusion | flops 491520 | bytes 5898720 | tf_op jit(solution)/shard_map/scatter-add | solution.py:92
  68.7 1.6 broadcast.125.clone
  70.3 17.3 %scatter_fusion = f32[128,16,256]{2,1,0:T(8,128)} fusion(f32[128,16,256]{2,1,0:T(8,128)} %broadcast.125.clone, s32[120]{0:T(128)S(1)} %get-tuple-element.9, f32[120,16,256]{2,1,0:T(8,128)} %pad_maximum_fusion), kind=kCustom, calls=%fused_computation.6 | custom fusion | flops 491520 | bytes 5898720 | tf_op jit(solution)/shard_map/scatter-add | solution.py:89
  87.5 4.0 add_bitcast_fusion.1
  91.6 5.0 %all-to-all-start.1 = ((f32[128,1,16,256]{3,2,1,0:T(8,128)}), f32[128,1,16,256]{3,2,1,0:T(8,128)}, u32[]{:S(2)}, u32[]{:S(2)}) async-start(f32[128,1,16,256]{3,2,1,0:T(8,128)} %add_bitcast_fusion.1), calls=%async_computation.1 | async-start | bytes 4194304 | tf_op jit(solution)/shard_map/all_to_all | solution.py:95
  96.9 1.7 convolution_add_fusion.4
  98.5 1.5 convolution_add_fusion.3
  100.0 26.9 %all-to-all-done.1 = f32[128,1,16,256]{3,2,1,0:T(8,128)} async-done(((f32[128,1,16,256]{3,2,1,0:T(8,128)}), f32[128,1,16,256]{3,2,1,0:T(8,128)}, u32[]{:S(2)}, u32[]{:S(2)}) %all-to-all-start.1) | async-done | bytes 2097184 | tf_op jit(solution)/shard_map/all_to_all | solution.py:95
  126.9 11.8 %scatter_fusion.2 = f32[8,16,256]{2,1,0:T(8,128)S(1)} fusion(f32[8,16,256]{2,1,0:T(8,128)S(1)} %convolution_add_fusion.3, s32[128]{0:T(128)S(1)} %bitcast.154, f32[128,16,256]{2,1,0:T(8,128)} %bitcast.12), kind=kCustom, calls=%fused_computation.8 | custom fusion | flops 524288 | bytes 6291968 | tf_op jit(solution)/shard_map/scatter-add | solution.py:102
  139.0 62.9 %all-reduce = (f32[16,16]{0,1:T(8,128)S(1)}, f32[16,16]{0,1:T(8,128)S(1)}) all-reduce(f32[16,16]{0,1:T(8,128)S(1)} %convolution_bitcast_fusion.8, f32[16,16]{0,1:T(8,128)S(1)} %convolution_bitcast_fusion.9), channel_id=1, replica_groups=mesh['clus'=32,'grp'=4] {'clus','grp'}, use_global_device_ids=true, to_apply=%region_6.8 | all-reduce | flops 512 | bytes 4096 | tf_op jit(solution)/shard_map/psum | solution.py:48
  202.0 1.5 cholesky.70
  204.8 1.8 custom-call.10
  206.7 1.5 cholesky.59
  209.5 1.2 custom-call.9
  211.6 62.8 %psum.30 = f32[16,16]{1,0:T(8,128)S(1)} all-reduce(f32[16,16]{1,0:T(8,128)S(1)} %convolution_bitcast_fusion.6), channel_id=1, replica_groups=mesh['clus'=32,'grp'=4] {'clus','grp'}, use_global_device_ids=true, to_apply=%region_7.0 | all-reduce | flops 256 | bytes 2048 | tf_op jit(solution)/shard_map/psum | solution.py:111
  277.1 1.8 gather_fusion.3
  278.9 24.9 %all_to_all.20 = bf16[128,1,16,256]{3,2,1,0:T(8,128)(2,1)} all-to-all(bf16[128,1,16,256]{3,2,1,0:T(8,128)(2,1)} %bitcast.153), channel_id=1, replica_groups=mesh['clus'=32,'grp'=4] {'clus','grp'}, dimensions={0} | all-to-all | bytes 2097152 | tf_op jit(solution)/shard_map/all_to_all | solution.py:52
  303.8 3.1 gather_fusion.5
  306.8 3.0 fusion.3
  309.9 1.3 fusion.38
  311.1 3.1 gather_fusion.4
  314.2 2.3 fusion.2
  316.5 1.7 fusion.37
  319.6 1.5 fusion.33
  321.1 1.4 pad_maximum_fusion.3
  322.5 1.6 broadcast.125.clone.3
  324.1 17.3 %scatter_fusion.4 = f32[128,16,256]{2,1,0:T(8,128)} fusion(f32[128,16,256]{2,1,0:T(8,128)} %broadcast.125.clone.3, s32[120]{0:T(128)S(1)} %copy-done.22, f32[120,16,256]{2,1,0:T(8,128)} %pad_maximum_fusion.3), kind=kCustom, calls=%fused_computation.10 | custom fusion | flops 491520 | bytes 5898720 | tf_op jit(solution)/shard_map/scatter-add | solution.py:92
  341.4 2.9 pad_maximum_fusion.2
  344.3 1.6 broadcast.125.clone.2
  345.9 17.2 %scatter_fusion.3 = f32[128,16,256]{2,1,0:T(8,128)} fusion(f32[128,16,256]{2,1,0:T(8,128)} %broadcast.125.clone.2, s32[120]{0:T(128)S(1)} %copy-done.20, f32[120,16,256]{2,1,0:T(8,128)} %pad_maximum_fusion.2), kind=kCustom, calls=%fused_computation.9 | custom fusion | flops 491520 | bytes 5898720 | tf_op jit(solution)/shard_map/scatter-add | solution.py:89
  363.2 4.0 add_bitcast_fusion
  367.2 5.1 %all-to-all-start.3 = ((f32[128,1,16,256]{3,2,1,0:T(8,128)}), f32[128,1,16,256]{3,2,1,0:T(8,128)}, u32[]{:S(2)}, u32[]{:S(2)}) async-start(f32[128,1,16,256]{3,2,1,0:T(8,128)} %add_bitcast_fusion), calls=%async_computation.3 | async-start | bytes 4194304 | tf_op jit(solution)/shard_map/all_to_all | solution.py:95
  373.2 1.6 convolution_add_fusion.2
  374.8 1.5 convolution_add_fusion.1
  376.3 26.3 %all-to-all-done.3 = f32[128,1,16,256]{3,2,1,0:T(8,128)} async-done(((f32[128,1,16,256]{3,2,1,0:T(8,128)}), f32[128,1,16,256]{3,2,1,0:T(8,128)}, u32[]{:S(2)}, u32[]{:S(2)}) %all-to-all-start.3) | async-done | bytes 2097184 | tf_op jit(solution)/shard_map/all_to_all | solution.py:95
  402.6 11.8 %scatter_fusion.5 = f32[8,16,256]{2,1,0:T(8,128)S(1)} fusion(f32[8,16,256]{2,1,0:T(8,128)S(1)} %convolution_add_fusion.1, s32[128]{0:T(128)S(1)} %bitcast.155, f32[128,16,256]{2,1,0:T(8,128)} %bitcast.33), kind=kCustom, calls=%fused_computation.11 | custom fusion | flops 524288 | bytes 6291968 | tf_op jit(solution)/shard_map/scatter-add | solution.py:102
  415.6 62.8 %psum.31 = f32[16,16]{0,1:T(8,128)S(1)} all-reduce(f32[16,16]{0,1:T(8,128)S(1)} %convolution_bitcast_fusion.4), channel_id=1, replica_groups=mesh['clus'=32,'grp'=4] {'clus','grp'}, use_global_device_ids=true, to_apply=%region_11.14 | all-reduce | flops 256 | bytes 2048 | tf_op jit(solution)/shard_map/psum | solution.py:106
  478.4 1.5 cholesky.81
  483.8 1.9 fusion.5
  (97 shorter events, 20.7 us)
Async XLA Ops:
  0.6 40.4 %copy-start = (bf16[24,256,256]{2,1,0:T(8,128)(2,1)S(1)}, bf16[24,256,256]{2,1,0:T(8,128)(2,1)}, u32[]{:S(2)}) copy-start(bf16[24,256,256]{2,1,0:T(8,128)(2,1)} %param.15) | copy-start | bytes 9437188
  1.5 2.8 copy-start.16
  2.5 13.7 %copy-start.23 = (s32[2,120]{1,0:T(2,128)S(1)}, s32[2,120]{1,0:T(2,128)}, u32[]{:S(2)}) copy-start(s32[2,120]{1,0:T(2,128)} %param.20) | copy-start | bytes 2884
  2.5 13.7 %copy-start.26 = (s32[96]{0:T(128)S(1)}, s32[96]{0:T(128)}, u32[]{:S(2)}) copy-start(s32[96]{0:T(128)} %param.18) | copy-start | bytes 1156
  4.2 31.0 %all-to-all-start = ((bf16[128,1,16,256]{3,2,1,0:T(8,128)(2,1)}), bf16[128,1,16,256]{3,2,1,0:T(8,128)(2,1)}, u32[]{:S(2)}, u32[]{:S(2)}) async-start(bf16[128,1,16,256]{3,2,1,0:T(8,128)(2,1)} %bitcast.152), calls=%async_computation | async-start | bytes 2097152 | tf_op jit(solution)/shard_map/all_to_all | solution.py:52
  16.2 24.8 %copy-start.17 = (s32[1024]{0:T(1024)}, s32[1024]{0:T(1024)S(1)}, u32[]{:S(2)}) copy-start(s32[1024]{0:T(1024)S(1)} %get-tuple-element.13) | copy-start | bytes 12292
  16.2 24.8 %copy-start.18 = (s32[1024]{0:T(1024)}, s32[1024]{0:T(1024)S(1)}, u32[]{:S(2)}) copy-start(s32[1024]{0:T(1024)S(1)} %get-tuple-element.12) | copy-start | bytes 12292
  16.3 35.1 %copy-start.21 = (s32[120]{0:T(128)}, s32[120]{0:T(128)S(1)}, u32[]{:S(2)}) copy-start(s32[120]{0:T(128)S(1)} %get-tuple-element.8) | copy-start | bytes 1444
  16.3 54.0 %copy-start.19 = (s32[120]{0:T(128)}, s32[120]{0:T(128)S(1)}, u32[]{:S(2)}) copy-start(s32[120]{0:T(128)S(1)} %get-tuple-element.9) | copy-start | bytes 1444
  16.4 28.5 %copy-start.12 = (f32[96,32]{1,0:T(8,128)}, f32[96,32]{1,0:T(8,128)S(1)}, u32[]{:S(2)}) copy-start(f32[96,32]{1,0:T(8,128)S(1)} %fusion.8) | copy-start | bytes 36868
  41.1 1.5 copy-start.7
  42.6 1.4 copy-start.4
  42.6 1.7 copy-start.6
  44.3 1.4 copy-start.2
  91.6 5.0 %copy-start.1 = (f32[8,16,256]{2,1,0:T(8,128)S(1)}, f32[8,16,256]{2,1,0:T(8,128)}, u32[]{:S(2)}) copy-start(f32[8,16,256]{2,1,0:T(8,128)} %param.12) | copy-start | bytes 393220
  91.6 5.3 %copy-start.14 = (f32[8,256]{1,0:T(8,128)S(1)}, f32[8,256]{1,0:T(8,128)}, u32[]{:S(2)}) copy-start(f32[8,256]{1,0:T(8,128)} %param.13) | copy-start | bytes 24580
  91.6 35.4 %all-to-all-start.1 = ((f32[128,1,16,256]{3,2,1,0:T(8,128)}), f32[128,1,16,256]{3,2,1,0:T(8,128)}, u32[]{:S(2)}, u32[]{:S(2)}) async-start(f32[128,1,16,256]{3,2,1,0:T(8,128)} %add_bitcast_fusion.1), calls=%async_computation.1 | async-start | bytes 4194304 | tf_op jit(solution)/shard_map/all_to_all | solution.py:95
  96.6 30.3 %copy-start.24 = (s32[1,128,1]{1,2,0:T(1,128)S(1)}, s32[1,128,1]{1,2,0:T(1,128)}, u32[]{:S(2)}) copy-start(s32[1,128,1]{1,2,0:T(1,128)} %param.19) | copy-start | bytes 1540
  278.9 27.9 %copy-start.13 = (f32[96,32]{1,0:T(8,128)S(1)}, f32[96,32]{1,0:T(8,128)}, u32[]{:S(2)}) copy-start(f32[96,32]{1,0:T(8,128)} %copy-done.12) | copy-start | bytes 36868
  306.8 3.1 copy-start.9
  314.2 2.3 copy-start.8
  316.5 1.7 copy-start.3
  316.5 1.7 copy-start.10
  318.2 1.4 copy-start.5
  319.6 1.5 copy-start.11
  322.5 1.6 copy-start.22
  344.3 1.6 copy-start.20
  367.2 6.0 %copy-start.15 = (f32[8,256]{1,0:T(8,128)S(1)}, f32[8,256]{1,0:T(8,128)}, u32[]{:S(2)}) copy-start(f32[8,256]{1,0:T(8,128)} %param.13) | copy-start | bytes 24580
  367.2 35.4 %all-to-all-start.3 = ((f32[128,1,16,256]{3,2,1,0:T(8,128)}), f32[128,1,16,256]{3,2,1,0:T(8,128)}, u32[]{:S(2)}, u32[]{:S(2)}) async-start(f32[128,1,16,256]{3,2,1,0:T(8,128)} %add_bitcast_fusion), calls=%async_computation.3 | async-start | bytes 4194304 | tf_op jit(solution)/shard_map/all_to_all | solution.py:95
  373.2 29.4 %copy-start.25 = (s32[1,128,1]{1,2,0:T(1,128)S(1)}, s32[1,128,1]{1,2,0:T(1,128)}, u32[]{:S(2)}) copy-start(s32[1,128,1]{1,2,0:T(1,128)} %param.19) | copy-start | bytes 1540
where the time goes:
time: 488 us; the launch traced here: 486 us
  blocking collectives  213 us (44%)
  other arithmetic  123 us (25%)
  waiting for transfers between devices  72.1 us (15%)
  matrix products  29.9 us (6%)
  local copies, waits for them, and re-layouts  24.7 us (5%)
  starting transfers between devices  22 us (5%)
    psum x1, blocking collectives, shards(): res_gram = lax.psum(inner_gram(residual, residual), ('clus', 'grp'))  62.9 us
    psum x1, blocking collectives, shards(): curvature = lax.psum(inner_gram(direction, product), ('clus', 'grp'))  62.8 us
    psum x1, blocking collectives, shards(): next_gram = lax.psum(inner_gram(residual, residual), ('clus', 'grp'))  62.8 us
    all_to_all x2, waiting for transfers between devices, shards(): lax.all_to_all(summed.reshape(devices, slot_count, rhs_count, leaf_size),...  53.3 us
    scatter-add x2, other arithmetic, shards(): jax.ops.segment_sum(jnp.concatenate([cols_near, cols_far], axis=0), cols_...  34.6 us
    scatter-add x2, other arithmetic, shards(): jax.ops.segment_sum(jnp.concatenate([rows_near, rows_far], axis=0), rows_...  34.5 us
    all_to_all x1, blocking collectives, shards(): lax.all_to_all(outgoing, ('clus', 'grp'), split_axis=0, concat_axis=0, ti...  24.9 us
    scatter-add x2, other arithmetic, shards(): jax.ops.segment_sum(returned.reshape(positions, rhs_count, leaf_size), fl...  23.6 us
  transfers between devices with their start and end apart: 3, of which 3 were waited for; matrix products, arithmetic and copies ran while one was open for 2% of the time, Pallas kernels for 0%

commit v1 on v0

v1 whole, which is shorter than its diff:
```python
import jax
import jax.numpy as jnp
from jax import lax
from jax.experimental import pallas as pl
from jax.experimental.pallas import tpu as pltpu
from jax.sharding import PartitionSpec as P

AXES = ("clus", "grp")
HIGHEST = lax.Precision.HIGHEST
NT = (((1,), (1,)), ((), ()))
F32 = jnp.float32
BF16 = jnp.bfloat16

VMEM = pl.BlockSpec(memory_space=pltpu.VMEM)
SMEM = pl.BlockSpec(memory_space=pltpu.SMEM)


def iota(shape, dim):
    return lax.broadcasted_iota(jnp.int32, shape, dim)


def spread(values):
    values = values + pltpu.roll(values, 64, 1)
    values = values + pltpu.roll(values, 32, 1)
    return values + pltpu.roll(values, 16, 1)


def block_mask():
    return iota((128, 128), 0) // 16 == iota((128, 128), 1) // 16


def fold(products):
    kept = jnp.where(block_mask(), products, 0.0)
    total = kept[0:16]
    for part in range(1, 8):
        total = total + kept[16 * part : 16 * part + 16]
    return spread(total)


def kron_rows(coefs):
    tiled = jnp.concatenate([coefs] * 8, axis=0)
    return jnp.where(block_mask(), tiled, 0.0).T


def combine(field, kron):
    return jnp.dot(kron, field, precision=HIGHEST, preferred_element_type=F32)


def gram(left, right):
    return fold(lax.dot_general(left, right, NT, precision=HIGHEST, preferred_element_type=F32))


def solve(matrix, target):
    group = iota((16, 128), 1) // 16
    row_at = iota((16, 128), 0)
    work = jnp.where(group == 0, matrix, target)
    for step in range(16):
        column = jnp.broadcast_to(work[:, step : step + 1], (16, 128))
        pivot = column[step : step + 1, :]
        scaled = work[step : step + 1, :] * jnp.where(pivot > 0, 1.0 / pivot, jnp.nan)
        work = jnp.where(row_at == step, scaled, work - column * scaled)
    return jnp.where(group == 0, pltpu.roll(work, 16, 1), work)


def pack(first, second):
    group = iota((8, 128), 1) // 16
    tile = jnp.zeros((8, 128), F32)
    at = 0
    for matrix in (first, second):
        high = matrix.astype(BF16).astype(F32)
        low = matrix - high
        for piece in (high, low):
            for half in (piece[0:8], piece[8:16]):
                tile = jnp.where(group == at, half, tile)
                at += 1
    return tile.astype(BF16)


def unpack(tile):
    group = iota((8, 128), 1) // 16
    joined = tile + pltpu.roll(tile, 128 - 32, 1)
    halves = [spread(jnp.where(group == at, joined, 0.0)) for at in (0, 1, 4, 5)]
    return jnp.concatenate(halves[0:2], axis=0), jnp.concatenate(halves[2:4], axis=0)


def send_kernel(leaf_ref, field_ref, message_ref, half_ref):
    half_ref[...] = field_ref[...].astype(BF16)

    def some(at, carry):
        for part in range(8):
            owner = at * 8 + part
            message_ref[owner] = half_ref[leaf_ref[owner]]
        return carry

    lax.fori_loop(0, message_ref.shape[0] // 8, some, 0)


def base_kernel(field_ref, shift_ref, self_ref, base_ref, curve_ref, norm_ref):
    leaves = field_ref.shape[0]
    for leaf in range(leaves):
        field = field_ref[leaf]
        half = field.astype(BF16)
        block = self_ref[leaf]
        total = shift_ref[leaf : leaf + 1, :] * field
        total = total + lax.dot_general(half, block, NT, preferred_element_type=F32)
        base_ref[leaf] = total + jnp.dot(half, block, preferred_element_type=F32)
    fields = field_ref[...].reshape(128, 256)
    curve_ref[...] = gram(fields, base_ref[...].reshape(128, 256))
    norm_ref[...] = gram(fields, fields)


def owner_kernel(
    rank_ref, at_ref, x_ref, near_ref, left_ref, right_ref, curve_ref, norm_ref, out_ref, acc_ref
):
    slots = x_ref.shape[0]
    near = near_ref.shape[0]
    far = left_ref.shape[0]

    def clear(at, carry):
        acc_ref[pl.ds(at * 8, 8)] = jnp.zeros((8, 16, 256), F32)
        return carry

    lax.fori_loop(0, slots // 8, clear, 0)

    def near_some(at, carry):
        sums = []
        for part in range(4):
            which = at * 4 + part
            row, col = at_ref[0, which], at_ref[1, which]
            block = near_ref[which]
            sums.append(
                (row, lax.dot_general(x_ref[col], block, NT, preferred_element_type=F32))
            )
            sums.append((col, jnp.dot(x_ref[row], block, preferred_element_type=F32)))
        for slot, value in sums:
            acc_ref[slot] += value
        return carry

    lax.fori_loop(0, near // 4, near_some, 0)

    lane = iota((16, 256), 1)

    def far_some(at, carry):
        first = at * 8
        left = left_ref[pl.ds(first, 8)].reshape(256, 256)
        right = right_ref[pl.ds(first, 8)].reshape(256, 256)
        rows = [at_ref[0, near + first + part] for part in range(8)]
        cols = [at_ref[1, near + first + part] for part in range(8)]
        x_row = jnp.concatenate([x_ref[slot] for slot in rows], axis=0)
        x_col = jnp.concatenate([x_ref[slot] for slot in cols], axis=0)
        kept = jnp.concatenate(
            [
                (lane >= 32 * part) & (lane < 32 * part + rank_ref[first + part])
                for part in range(8)
            ],
            axis=0,
        )
        right_proj = lax.dot_general(x_col, right, NT, preferred_element_type=F32)
        left_proj = lax.dot_general(x_row, left, NT, preferred_element_type=F32)
        right_proj = jnp.where(kept, right_proj, 0.0).astype(BF16)
        left_proj = jnp.where(kept, left_proj, 0.0).astype(BF16)
        to_row = jnp.dot(right_proj, left, preferred_element_type=F32)
        to_col = jnp.dot(left_proj, right, preferred_element_type=F32)
        for part in range(8):
            acc_ref[rows[part]] += to_row[16 * part : 16 * part + 16]
            acc_ref[cols[part]] += to_col[16 * part : 16 * part + 16]
        return carry

    lax.fori_loop(0, far // 8, far_some, 0)

    def finish(at, products):
        here = pl.ds(at * 8, 8)
        sums = acc_ref[here].astype(BF16)
        out_ref[here, 0:16, :] = sums[:, :, 0:128]
        out_ref[here, 16:32, :] = sums[:, :, 128:256]
        return products + lax.dot_general(
            x_ref[here].reshape(128, 256),
            sums.reshape(128, 256),
            NT,
            preferred_element_type=F32,
        )

    products = lax.fori_loop(0, slots // 8, finish, jnp.zeros((128, 128), F32))
    tile = pack(fold(products) + curve_ref[...], norm_ref[...])

    def attach(at, carry):
        out_ref[pl.ds(at * 8, 8), 32:40, :] = jnp.broadcast_to(tile[None], (8, 8, 128))
        return carry

    lax.fori_loop(0, slots // 8, attach, 0)


def add_returned(leaf_ref, sums_ref, acc_ref):
    def some(at, tiles):
        for part in range(8):
            owner = at * 8 + part
            leaf = leaf_ref[owner]
            acc_ref[leaf, :, 0:128] += sums_ref[owner, 0:16, :].astype(F32)
            acc_ref[leaf, :, 128:256] += sums_ref[owner, 16:32, :].astype(F32)
            tiles = tiles + sums_ref[owner, 32:40, :].astype(F32)
        return tiles

    return lax.fori_loop(0, sums_ref.shape[0] // 8, some, jnp.zeros((8, 128), F32))


def leaf_kernel(
    leaf_ref, sums_ref, base_ref, field_ref,
    residual_ref, image_ref, message_ref, curve_ref, norm_ref, step_ref, half_ref,
):
    image_ref[...] = base_ref[...]
    curve, norm = unpack(add_returned(leaf_ref, sums_ref, image_ref))
    step = solve(curve, norm)
    curve_ref[...] = curve
    norm_ref[...] = norm
    step_ref[...] = step
    image = image_ref[...].reshape(128, 256)
    residual = field_ref[...].reshape(128, 256) - combine(image, kron_rows(step))
    residual_ref[...] = residual.reshape(residual_ref.shape)
    half_ref[...] = residual.reshape(residual_ref.shape).astype(BF16)

    def some(at, carry):
        for part in range(8):
            owner = at * 8 + part
            message_ref[owner] = half_ref[leaf_ref[owner]]
        return carry

    lax.fori_loop(0, message_ref.shape[0] // 8, some, 0)


def final_kernel(
    leaf_ref, sums_ref, base_ref, field_ref, residual_ref, image_ref,
    curve_ref, norm_ref, step_ref, solution_ref, out_ref, acc_ref,
):
    acc_ref[...] = base_ref[...]
    curve, next_norm = unpack(add_returned(leaf_ref, sums_ref, acc_ref))
    coef = solve(norm_ref[...], next_norm)
    narrow = coef[:, 0:16]
    moved = jnp.dot(curve_ref[:, 0:16], coef, precision=HIGHEST, preferred_element_type=F32)
    moved = lax.dot_general(
        narrow, moved, (((0,), (0,)), ((), ())), precision=HIGHEST, preferred_element_type=F32
    )
    step = solve(curve - moved, next_norm)
    kron_step = kron_rows(step)
    kron_coef = kron_rows(coef)
    field = field_ref[...].reshape(128, 256)
    residual = residual_ref[...].reshape(128, 256)
    direction = residual + combine(field, kron_coef)
    product = acc_ref[...].reshape(128, 256) + combine(
        image_ref[...].reshape(128, 256), kron_coef
    )
    answer = combine(field, kron_rows(step_ref[...])) + combine(direction, kron_step)
    solution_ref[...] = answer.reshape(solution_ref.shape)
    out_ref[...] = (residual - combine(product, kron_step)).reshape(out_ref.shape)


def call(kernel, ins, outs, scratch=(), cost=None):
    return pl.pallas_call(
        kernel,
        out_shape=[jax.ShapeDtypeStruct(shape, kind) for shape, kind in outs],
        in_specs=list(ins),
        out_specs=[VMEM] * len(outs),
        scratch_shapes=[pltpu.VMEM(shape, kind) for shape, kind in scratch],
        compiler_params=pltpu.CompilerParams(vmem_limit_bytes=32 * 1024 * 1024),
        cost_estimate=cost,
    )


def swap(values):
    return lax.all_to_all(values, AXES, split_axis=0, concat_axis=0, tiled=True)


def shards(
    right_sides,
    diag_shift,
    self_blocks,
    near_blocks,
    far_left,
    far_right,
    far_rank,
    send_leaf,
    block_pos,
):
    leaves, rhs, size = right_sides.shape
    slots = send_leaf.shape[1]
    targets = send_leaf.reshape(slots)
    whole = ((leaves, rhs, size), F32)
    small = ((rhs, 128), F32)
    message = ((slots, rhs, size), BF16)
    returned = ((slots, 40, 128), BF16)
    local_cost = pl.CostEstimate(
        flops=4 * leaves * rhs * size * size, bytes_accessed=2 * leaves * size * size, transcendentals=0
    )
    send = call(send_kernel, [SMEM, VMEM], [message], [((leaves, rhs, size), BF16)])
    base = call(base_kernel, [VMEM] * 3, [whole, small, small], cost=local_cost)
    owner = call(
        owner_kernel, [SMEM, SMEM] + [VMEM] * 6, [returned], [((slots, rhs, size), F32)]
    )
    leaf = call(
        leaf_kernel,
        [SMEM] + [VMEM] * 3,
        [whole, whole, message, small, small, small],
        [((leaves, rhs, size), BF16)],
    )
    final = call(final_kernel, [SMEM] + [VMEM] * 8, [whole, whole], [whole])

    with jax.named_scope("send"):
        (outgoing,) = send(targets, right_sides)
    incoming = swap(outgoing)
    with jax.named_scope("base"):
        base_image, curve, norm = base(right_sides, diag_shift, self_blocks)
    with jax.named_scope("owner"):
        (sums,) = owner(
            far_rank, block_pos, incoming, near_blocks, far_left, far_right, curve, norm
        )
    back = swap(sums)
    with jax.named_scope("leaf"):
        residual, image, outgoing, curve, norm, step = leaf(
            targets, back, base_image, right_sides
        )
    incoming = swap(outgoing)
    with jax.named_scope("base"):
        base_image, next_curve, next_norm = base(residual, diag_shift, self_blocks)
    with jax.named_scope("owner"):
        (sums,) = owner(
            far_rank, block_pos, incoming, near_blocks, far_left, far_right, next_curve, next_norm
        )
    back = swap(sums)
    with jax.named_scope("final"):
        answer, residual = final(
            targets, back, base_image, right_sides, residual, image, curve, norm, step
        )
    return (answer, residual)


def solution(mesh):
    split = P(AXES, None, None)
    placed = (
        split,
        P(AXES, None),
        split,
        split,
        split,
        split,
        P(AXES),
        split,
        P(None, AXES),
    )
    return jax.shard_map(
        shards, mesh=mesh, in_specs=placed, out_specs=(split, split), check_vma=False
    )
```

time: 488 us -> 153 us (0.31)
  blocking collectives: 213 us -> 51.6 us
  other arithmetic: 123 us -> 0 us
  waiting for transfers between devices: 72.1 us -> 31.2 us
  Pallas kernels: 0 us -> 34 us
  matrix products: 29.9 us -> 0 us
  local copies, waits for them, and re-layouts: 24.7 us -> 18 us
  starting transfers between devices: 22 us -> 16.8 us
    psum x3 -> x0, blocking collectives: 189 us -> none  [the longest x1 62.9 us: shards(): res_gram = lax.psum(inner_gram(residual, residual), ('clus', 'grp'))]
    scatter-add x6 -> x0, other arithmetic: 92.7 us -> none  [the longest x2 34.6 us: shards(): jax.ops.segment_sum(jnp.concatenate([cols_near, cols_far], axis=0), cols_...]
    all_to_all x3 -> x2, waiting for transfers between devices: 72.1 us -> 31.2 us  [swap(): return lax.all_to_all(values, AXES, split_axis=0, concat_axis=0, tiled=True)]
    pallas_call x0 -> x7, Pallas kernels: none -> 34 us  [the longest x1 11.1 us: shards(): owner(far_rank, block_pos, incoming, near_blocks, far_left, far_right, ne...]
    dot_general x25 -> x0, matrix products: 27.3 us -> none  [the longest x5 4.87 us: combine_cols(): jnp.einsum('lri,rs->lsi', field, coefs, precision=lax.Precision.HIGHEST)]
    all_to_all x1 -> x2, blocking collectives: 24.9 us -> 51.6 us  [swap(): return lax.all_to_all(values, AXES, split_axis=0, concat_axis=0, tiled=True)]
    gather x6 -> x0, local copies, waits for them, and re-layouts: 15.4 us -> none  [the longest x2 5.98 us: shards(): x_row = received[rows_at]]
    unnamed x54 -> x62, local copies, waits for them, and re-layouts: 2.78 us -> 18 us
  transfers between devices with their start and end apart: 3 -> 2, of which waited for: 3 -> 2; matrix products, arithmetic and copies ran while one was open for 2% -> 0% of each run, Pallas kernels for 0% -> 1%
where the time goes in v1:
time: 153 us; the launch traced here: 152 us
  blocking collectives  51.6 us (34%)
  Pallas kernels  34 us (22%)
  waiting for transfers between devices  31.2 us (20%)
  local copies, waits for them, and re-layouts  18 us (12%)
  starting transfers between devices  16.8 us (11%)
    all_to_all x2, blocking collectives, swap(): return lax.all_to_all(values, AXES, split_axis=0, concat_axis=0, tiled=True)  51.6 us
    all_to_all x2, waiting for transfers between devices, swap(): return lax.all_to_all(values, AXES, split_axis=0, concat_axis=0, tiled=True)  31.2 us
    unnamed x62, local copies, waits for them, and re-layouts  18 us
    all_to_all x2, starting transfers between devices, swap(): return lax.all_to_all(values, AXES, split_axis=0, concat_axis=0, tiled=True)  16.8 us
    pallas_call x1, Pallas kernels, shards(): owner(far_rank, block_pos, incoming, near_blocks, far_left, far_right, ne...  11.1 us
    pallas_call x1, Pallas kernels, shards(): owner(far_rank, block_pos, incoming, near_blocks, far_left, far_right, cu...  11.1 us
    pallas_call x1, Pallas kernels, shards(): final(targets, back, base_image, right_sides, residual, image, curve, nor...  5.68 us
    pallas_call x1, Pallas kernels, shards(): leaf(targets, back, base_image, right_sides)  3.28 us
  transfers between devices with their start and end apart: 2, of which 2 were waited for; matrix products, arithmetic and copies ran while one was open for 0% of the time, Pallas kernels for 1%

profile of v1, /device:TPU:1, one launch (start us, length us, event | category | flops | bytes accessed | tf_op | source)
XLA Modules:
  0.0 152.5 jit_solution(9082622300541262598)
XLA Ops:
  0.6 0.0 copy-start.8
  0.6 0.9 copy-done.8
  1.5 0.7 copy-done.24
  2.2 0.8 send.1
  3.0 0.0 copy-start.7
  3.0 1.0 copy-done.7
  3.9 12.0 %all-to-all-start = ((bf16[128,16,256]{2,1,0:T(8,128)(2,1)}), bf16[128,16,256]{2,1,0:T(8,128)(2,1)}, u32[]{:S(2)}, u32[]{:S(2)}) async-start(bf16[128,16,256]{2,1,0:T(8,128)(2,1)} %copy-done.7), calls=%async_computation | async-start | bytes 2097152 | tf_op jit(solution)/shard_map/all_to_all | solution.py:269
  15.9 0.0 copy-done.9
  15.9 0.0 copy-done.15
  15.9 0.0 copy-start.5
  15.9 1.2 copy-done.5
  17.2 1.1 base.2
  18.2 0.7 copy-done.13
  18.9 16.1 %all-to-all-done.x_ref = bf16[128,16,256]{2,1,0:T(8,128)(2,1)} async-done(((bf16[128,16,256]{2,1,0:T(8,128)(2,1)}), bf16[128,16,256]{2,1,0:T(8,128)(2,1)}, u32[]{:S(2)}, u32[]{:S(2)}) %all-to-all-start) | async-done | bytes 1048608 | tf_op jit(solution)/shard_map/all_to_all | solution.py:269
  35.0 0.0 copy-done.27
  35.0 0.0 copy-done.29
  35.0 0.0 copy-start.1
  35.0 1.4 copy-done.1
  36.4 1.4 copy-done.3
  37.8 11.1 %owner.2 = bf16[128,40,128]{2,1,0:T(8,128)(2,1)S(1)} custom-call(s32[96]{0:T(128)S(1)} %copy-done.29, s32[2,120]{1,0:T(2,128)S(1)} %copy-done.27, bf16[128,16,256]{2,1,0:T(8,128)(2,1)} %all-to-all-done.x_ref, bf16[24,256,256]{2,1,0:T(8,128)(2,1)S(1)} %copy-done, bf16[96,32,256]{2,1,0:T(8,128)(2,1)S(1)} %copy-done.1, bf16[96,32,256]{2,1,0:T(8,128)(2,1)S(1)} %copy-done.3, ...), custom_call_target="tpu_custom_call" | custom-call | tf_op jit(solution)/shard_map/owner/pallas_call | solution.py:312
  48.9 0.0 copy-start.14
  48.9 0.0 copy-start.25
  48.9 25.8 %all_to_all.20.sums_ref = bf16[128,40,128]{2,1,0:T(8,128)(2,1)S(1)} all-to-all(bf16[128,40,128]{2,1,0:T(8,128)(2,1)S(1)} %owner.2), channel_id=1, replica_groups=mesh['clus'=32,'grp'=4] {'clus','grp'}, dimensions={0} | all-to-all | bytes 2621440 | tf_op jit(solution)/shard_map/all_to_all | solution.py:269
  74.7 3.3 %leaf.1 = (f32[8,16,256]{2,1,0:T(8,128)S(1)}, f32[8,16,256]{2,1,0:T(8,128)S(1)}, bf16[128,16,256]{2,1,0:T(8,128)(2,1)S(1)}, f32[16,128]{1,0:T(8,128)S(1)}, f32[16,128]{1,0:T(8,128)S(1)}, /*index=5*/f32[16,128]{1,0:T(8,128)S(1)}) custom-call(s32[128]{0:T(128)S(1)} %bitcast.2, bf16[128,40,128]{2,1,0:T(8,128)(2,1)S(1)} %all_to_all.20.sums_ref, ...), custom_call_target="tpu_custom_call" | custom-call | tf_op jit(solution)/shard_map/leaf/pallas_call | solution.py:317
  78.0 0.0 copy-start.10
  78.0 1.0 copy-done.10
  79.0 0.6 copy-done.16
  79.6 0.6 copy-done.18
  80.2 4.9 %all-to-all-start.2 = ((bf16[128,16,256]{2,1,0:T(8,128)(2,1)}), bf16[128,16,256]{2,1,0:T(8,128)(2,1)}, u32[]{:S(2)}, u32[]{:S(2)}) async-start(bf16[128,16,256]{2,1,0:T(8,128)(2,1)} %copy-done.10), calls=%async_computation.2 | async-start | bytes 2097152 | tf_op jit(solution)/shard_map/all_to_all | solution.py:269
  85.1 0.0 copy-start.6
  85.1 1.2 copy-done.6
  86.3 1.1 base.3
  87.4 0.7 copy-done.11
  88.0 0.6 copy-done.20
  88.6 0.6 copy-done.22
  89.2 15.1 %all-to-all-done.2.x_ref = bf16[128,16,256]{2,1,0:T(8,128)(2,1)} async-done(((bf16[128,16,256]{2,1,0:T(8,128)(2,1)}), bf16[128,16,256]{2,1,0:T(8,128)(2,1)}, u32[]{:S(2)}, u32[]{:S(2)}) %all-to-all-start.2) | async-done | bytes 1048608 | tf_op jit(solution)/shard_map/all_to_all | solution.py:269
  104.3 1.4 copy-done.2
  105.7 1.4 copy-done.4
  107.1 0.7 copy-done.21
  107.8 0.7 copy-done.23
  108.5 0.7 copy-done.28
  109.2 0.7 copy-done.30
  109.8 11.1 %owner.3 = bf16[128,40,128]{2,1,0:T(8,128)(2,1)S(1)} custom-call(s32[96]{0:T(128)S(1)} %copy-done.30, s32[2,120]{1,0:T(2,128)S(1)} %copy-done.28, bf16[128,16,256]{2,1,0:T(8,128)(2,1)} %all-to-all-done.2.x_ref, bf16[24,256,256]{2,1,0:T(8,128)(2,1)S(1)} %copy-done, bf16[96,32,256]{2,1,0:T(8,128)(2,1)S(1)} %copy-done.2, bf16[96,32,256]{2,1,0:T(8,128)(2,1)S(1)} %copy-done.4, ...), custom_call_target="tpu_custom_call" | custom-call | tf_op jit(solution)/shard_map/owner/pallas_call | solution.py:324
  120.9 0.0 copy-start.12
  120.9 0.0 copy-start.26
  121.0 25.8 %all_to_all.21.sums_ref = bf16[128,40,128]{2,1,0:T(8,128)(2,1)S(1)} all-to-all(bf16[128,40,128]{2,1,0:T(8,128)(2,1)S(1)} %owner.3), channel_id=1, replica_groups=mesh['clus'=32,'grp'=4] {'clus','grp'}, dimensions={0} | all-to-all | bytes 2621440 | tf_op jit(solution)/shard_map/all_to_all | solution.py:269
  146.8 0.0 copy-done.12
  146.8 5.7 %final.1 = (f32[8,16,256]{2,1,0:T(8,128)}, f32[8,16,256]{2,1,0:T(8,128)}) custom-call(s32[128]{0:T(128)S(1)} %bitcast.3, bf16[128,40,128]{2,1,0:T(8,128)(2,1)S(1)} %all_to_all.21.sums_ref, f32[8,16,256]{2,1,0:T(8,128)S(1)} %copy-done.12, f32[8,16,256]{2,1,0:T(8,128)S(1)} %copy-done.9, f32[8,16,256]{2,1,0:T(8,128)S(1)} %get-tuple-element.18.field_ref.residual_ref, ...), custom_call_target="tpu_custom_call" | custom-call | tf_op jit(solution)/shard_map/final/pallas_call | solution.py:329
  (27 shorter events, 0.0 us)
Async XLA Ops:
  0.6 0.9 copy-start.8
  1.5 0.7 copy-start.24
  2.2 13.7 %copy-start.9 = (f32[8,16,256]{2,1,0:T(8,128)S(1)}, f32[8,16,256]{2,1,0:T(8,128)}, u32[]{:S(2)}) copy-start(f32[8,16,256]{2,1,0:T(8,128)} %field_ref.7) | copy-start | bytes 393220
  2.2 13.7 %copy-start.15 = (f32[8,256]{1,0:T(8,128)S(1)}, f32[8,256]{1,0:T(8,128)}, u32[]{:S(2)}) copy-start(f32[8,256]{1,0:T(8,128)} %shift_ref.3) | copy-start | bytes 24580
  2.2 32.8 %copy-start.27 = (s32[2,120]{1,0:T(2,128)S(1)}, s32[2,120]{1,0:T(2,128)}, u32[]{:S(2)}) copy-start(s32[2,120]{1,0:T(2,128)} %at_ref.3) | copy-start | bytes 2884
  2.2 32.8 %copy-start.29 = (s32[96]{0:T(128)S(1)}, s32[96]{0:T(128)}, u32[]{:S(2)}) copy-start(s32[96]{0:T(128)} %rank_ref.3) | copy-start | bytes 1156
  3.0 1.0 copy-start.7
  3.9 31.0 %copy-start = (bf16[24,256,256]{2,1,0:T(8,128)(2,1)S(1)}, bf16[24,256,256]{2,1,0:T(8,128)(2,1)}, u32[]{:S(2)}) copy-start(bf16[24,256,256]{2,1,0:T(8,128)(2,1)} %near_ref.3) | copy-start | bytes 9437188
  3.9 31.0 %all-to-all-start = ((bf16[128,16,256]{2,1,0:T(8,128)(2,1)}), bf16[128,16,256]{2,1,0:T(8,128)(2,1)}, u32[]{:S(2)}, u32[]{:S(2)}) async-start(bf16[128,16,256]{2,1,0:T(8,128)(2,1)} %copy-done.7), calls=%async_computation | async-start | bytes 2097152 | tf_op jit(solution)/shard_map/all_to_all | solution.py:269
  15.9 1.2 copy-start.5
  18.2 0.7 copy-start.13
  35.0 1.4 copy-start.1
  36.4 1.4 copy-start.3
  48.9 25.8 %copy-start.14 = (f32[8,16,256]{2,1,0:T(8,128)S(1)}, f32[8,16,256]{2,1,0:T(8,128)}, u32[]{:S(2)}) copy-start(f32[8,16,256]{2,1,0:T(8,128)} %copy-done.13) | copy-start | bytes 393220
  48.9 25.8 %copy-start.25 = (s32[1,128,1]{1,2,0:T(1,128)S(1)}, s32[1,128,1]{1,2,0:T(1,128)}, u32[]{:S(2)}) copy-start(s32[1,128,1]{1,2,0:T(1,128)} %param.16) | copy-start | bytes 1540
  78.0 1.0 copy-start.10
  79.0 0.6 copy-start.16
  79.6 0.6 copy-start.18
  80.2 24.1 %all-to-all-start.2 = ((bf16[128,16,256]{2,1,0:T(8,128)(2,1)}), bf16[128,16,256]{2,1,0:T(8,128)(2,1)}, u32[]{:S(2)}, u32[]{:S(2)}) async-start(bf16[128,16,256]{2,1,0:T(8,128)(2,1)} %copy-done.10), calls=%async_computation.2 | async-start | bytes 2097152 | tf_op jit(solution)/shard_map/all_to_all | solution.py:269
  85.1 1.2 copy-start.6
  87.4 0.7 copy-start.11
  88.0 0.6 copy-start.20
  88.6 0.6 copy-start.22
  104.3 1.4 copy-start.2
  105.7 1.4 copy-start.4
  107.1 0.7 copy-start.21
  107.8 0.7 copy-start.23
  108.5 0.7 copy-start.28
  109.2 0.7 copy-start.30
  120.9 25.9 %copy-start.12 = (f32[8,16,256]{2,1,0:T(8,128)S(1)}, f32[8,16,256]{2,1,0:T(8,128)}, u32[]{:S(2)}) copy-start(f32[8,16,256]{2,1,0:T(8,128)} %copy-done.11) | copy-start | bytes 393220
  120.9 25.8 %copy-start.17 = (f32[16,128]{1,0:T(8,128)S(1)}, f32[16,128]{1,0:T(8,128)}, u32[]{:S(2)}) copy-start(f32[16,128]{1,0:T(8,128)} %copy-done.16) | copy-start | bytes 24580
  120.9 25.8 %copy-start.19 = (f32[16,128]{1,0:T(8,128)S(1)}, f32[16,128]{1,0:T(8,128)}, u32[]{:S(2)}) copy-start(f32[16,128]{1,0:T(8,128)} %copy-done.18) | copy-start | bytes 24580
  120.9 25.8 %copy-start.26 = (s32[1,128,1]{1,2,0:T(1,128)S(1)}, s32[1,128,1]{1,2,0:T(1,128)}, u32[]{:S(2)}) copy-start(s32[1,128,1]{1,2,0:T(1,128)} %param.16) | copy-start | bytes 1540

commit v2 on v1

v2 whole, which is shorter than its diff:
```python
import jax
import jax.numpy as jnp
from jax import lax
from jax.experimental import pallas as pl
from jax.experimental.pallas import tpu as pltpu
from jax.sharding import PartitionSpec as P

AXES = ("clus", "grp")
HIGHEST = lax.Precision.HIGHEST
NT = (((1,), (1,)), ((), ()))
F32 = jnp.float32
BF16 = jnp.bfloat16

VMEM = pl.BlockSpec(memory_space=pltpu.VMEM)
HBM = pl.BlockSpec(memory_space=pltpu.HBM)
KEPT = pl.BlockSpec(memory_space=pltpu.VMEM)


def iota(shape, dim):
    return lax.broadcasted_iota(jnp.int32, shape, dim)


def spread(values):
    values = values + pltpu.roll(values, 64, 1)
    values = values + pltpu.roll(values, 32, 1)
    return values + pltpu.roll(values, 16, 1)


def block_mask():
    return iota((128, 128), 0) // 16 == iota((128, 128), 1) // 16


def fold(products):
    kept = jnp.where(block_mask(), products, 0.0)
    total = kept[0:16]
    for part in range(1, 8):
        total = total + kept[16 * part : 16 * part + 16]
    return spread(total)


def kron_rows(coefs):
    tiled = jnp.concatenate([coefs] * 8, axis=0)
    return jnp.where(block_mask(), tiled, 0.0).T


def combine(field, kron):
    return jnp.dot(kron, field, precision=HIGHEST, preferred_element_type=F32)


def gram(left, right):
    return fold(lax.dot_general(left, right, NT, precision=HIGHEST, preferred_element_type=F32))


def columns(matrix):
    return [jnp.broadcast_to(matrix[:, at : at + 1], (16, 128)) for at in range(16)]


def factor(matrix):
    row_at = iota((16, 128), 0)
    left = columns(matrix)
    steps = []
    for step in range(16):
        column = left[step]
        pivot = column[step : step + 1]
        scale = jnp.where(pivot > 0, 1.0 / pivot, jnp.nan)
        steps.append((column, scale))
        for later in range(step + 1, 16):
            scaled = left[later][step : step + 1] * scale
            left[later] = jnp.where(row_at == step, scaled, left[later] - column * scaled)
    return steps


def apply_factor(steps, target):
    row_at = iota((16, 128), 0)
    for step, (column, scale) in enumerate(steps):
        scaled = target[step : step + 1] * scale
        target = jnp.where(row_at == step, scaled, target - column * scaled)
    return target


def solve(matrix, target):
    return apply_factor(factor(matrix), target)


def product(left, right):
    total = left[0] * right[0:1]
    for at in range(1, 16):
        total = total + left[at] * right[at : at + 1]
    return total


def pack(first, second):
    group = iota((8, 128), 1) // 16
    tile = jnp.zeros((8, 128), F32)
    at = 0
    for matrix in (first, second):
        high = matrix.astype(BF16).astype(F32)
        low = matrix - high
        for piece in (high, low):
            for half in (piece[0:8], piece[8:16]):
                tile = jnp.where(group == at, half, tile)
                at += 1
    return tile.astype(BF16)


def unpack(tile):
    group = iota((8, 128), 1) // 16
    joined = tile + pltpu.roll(tile, 128 - 32, 1)
    halves = [spread(jnp.where(group == at, joined, 0.0)) for at in (0, 1, 4, 5)]
    return jnp.concatenate(halves[0:2], axis=0), jnp.concatenate(halves[2:4], axis=0)


def fill(leaf_ref, half_ref, stage_ref, message_ref, sems):
    part = stage_ref.shape[0] // 4
    copies = []
    for quarter in range(4):

        def some(at, carry, first=quarter * part):
            for inner in range(8):
                owner = first + at * 8 + inner
                stage_ref[owner] = half_ref[leaf_ref[owner]]
            return carry

        lax.fori_loop(0, part // 8, some, 0)
        here = pl.ds(quarter * part, part)
        copy = pltpu.make_async_copy(stage_ref.at[here], message_ref.at[here], sems.at[quarter])
        copy.start()
        copies.append(copy)
    return copies


def send_kernel(leaf_hbm, field_hbm, message_ref, leaf_ref, field_ref, half_ref, stage_ref, sems):
    leaf_copy = pltpu.make_async_copy(leaf_hbm, leaf_ref, sems.at[4])
    field_copy = pltpu.make_async_copy(field_hbm, field_ref, sems.at[5])
    leaf_copy.start()
    field_copy.start()
    field_copy.wait()
    half_ref[...] = field_ref[...].astype(BF16)
    leaf_copy.wait()
    for copy in fill(leaf_ref, half_ref, stage_ref, message_ref, sems):
        copy.wait()


def local_product(field_ref, shift_ref, self_ref, base_ref, small_ref):
    for leaf in range(field_ref.shape[0]):
        field = field_ref[leaf]
        half = field.astype(BF16)
        block = self_ref[leaf]
        total = shift_ref[leaf : leaf + 1, :] * field
        total = total + lax.dot_general(half, block, NT, preferred_element_type=F32)
        base_ref[leaf] = total + jnp.dot(half, block, preferred_element_type=F32)
    fields = field_ref[...].reshape(128, 256)
    small_ref[0] = gram(fields, base_ref[...].reshape(128, 256))
    small_ref[1] = gram(fields, fields)


def base_kernel(
    field_ref, shift_ref, self_ref, near_hbm, left_hbm, right_hbm,
    base_ref, small_ref, near_ref, left_ref, right_ref, sems,
):
    copies = [
        pltpu.make_async_copy(near_hbm, near_ref, sems.at[0]),
        pltpu.make_async_copy(left_hbm, left_ref, sems.at[1]),
        pltpu.make_async_copy(right_hbm, right_ref, sems.at[2]),
    ]
    for copy in copies:
        copy.start()
    local_product(field_ref, shift_ref, self_ref, base_ref, small_ref)
    for copy in copies:
        copy.wait()


def next_base_kernel(
    field_ref, shift_ref, self_ref, old_ref, first_ref, base_ref, small_ref, part_ref, steps_ref
):
    local_product(field_ref, shift_ref, self_ref, base_ref, small_ref)
    part = combine(first_ref[...].reshape(128, 256), kron_rows(old_ref[2]))
    part_ref[...] = part.reshape(part_ref.shape)
    for step, (column, scale) in enumerate(factor(old_ref[1])):
        steps_ref[step] = column
        steps_ref[16, step : step + 1] = scale


def owner_kernel(
    rank_hbm, at_hbm, x_hbm, near_ref, left_ref, right_ref, small_ref,
    out_ref, rank_ref, at_ref, x_ref, acc_ref, sems,
):
    copies = [
        pltpu.make_async_copy(at_hbm, at_ref, sems.at[0]),
        pltpu.make_async_copy(x_hbm, x_ref, sems.at[1]),
        pltpu.make_async_copy(rank_hbm, rank_ref, sems.at[2]),
    ]
    for copy in copies:
        copy.start()
    slots = x_ref.shape[0]
    near = near_ref.shape[0]
    far = left_ref.shape[0]

    def clear(at, carry):
        acc_ref[pl.ds(at * 8, 8)] = jnp.zeros((8, 16, 256), F32)
        return carry

    lax.fori_loop(0, slots // 8, clear, 0)
    for copy in copies:
        copy.wait()

    def near_some(at, carry):
        sums = []
        for part in range(8):
            which = at * 8 + part
            row, col = at_ref[0, which], at_ref[1, which]
            block = near_ref[which]
            sums.append(
                (row, lax.dot_general(x_ref[col], block, NT, preferred_element_type=F32))
            )
            sums.append((col, jnp.dot(x_ref[row], block, preferred_element_type=F32)))
        for slot, value in sums:
            acc_ref[slot] += value
        return carry

    lax.fori_loop(0, near // 8, near_some, 0)

    lane = iota((16, 256), 1)

    def far_project(first):
        left = left_ref[pl.ds(first, 8)].reshape(256, 256)
        right = right_ref[pl.ds(first, 8)].reshape(256, 256)
        rows = [at_ref[0, near + first + part] for part in range(8)]
        cols = [at_ref[1, near + first + part] for part in range(8)]
        x_row = jnp.concatenate([x_ref[slot] for slot in rows], axis=0)
        x_col = jnp.concatenate([x_ref[slot] for slot in cols], axis=0)
        kept = jnp.concatenate(
            [
                (lane >= 32 * part) & (lane < 32 * part + rank_ref[first + part])
                for part in range(8)
            ],
            axis=0,
        )
        right_proj = lax.dot_general(x_col, right, NT, preferred_element_type=F32)
        left_proj = lax.dot_general(x_row, left, NT, preferred_element_type=F32)
        right_proj = jnp.where(kept, right_proj, 0.0).astype(BF16)
        left_proj = jnp.where(kept, left_proj, 0.0).astype(BF16)
        return rows, cols, left, right, right_proj, left_proj

    def far_some(at, carry):
        sums = []
        for rows, cols, left, right, right_proj, left_proj in [
            far_project(at * 32 + 8 * group) for group in range(4)
        ]:
            to_row = jnp.dot(right_proj, left, preferred_element_type=F32)
            to_col = jnp.dot(left_proj, right, preferred_element_type=F32)
            for part in range(8):
                sums.append((rows[part], to_row[16 * part : 16 * part + 16]))
                sums.append((cols[part], to_col[16 * part : 16 * part + 16]))
        for slot, value in sums:
            acc_ref[slot] += value
        return carry

    lax.fori_loop(0, far // 32, far_some, 0)

    products = jnp.zeros((128, 128), F32)
    for at in range(slots // 8):
        here = slice(at * 8, at * 8 + 8)
        sums = acc_ref[here].astype(BF16)
        out_ref[here, 0:16, :] = sums[:, :, 0:128]
        out_ref[here, 16:32, :] = sums[:, :, 128:256]
        products = products + lax.dot_general(
            x_ref[here].reshape(128, 256),
            sums.reshape(128, 256),
            NT,
            preferred_element_type=F32,
        )
    tile = pack(fold(products) + small_ref[0], small_ref[1])

    def attach(at, carry):
        out_ref[pl.ds(at * 8, 8), 32:40, :] = jnp.broadcast_to(tile[None], (8, 8, 128))
        return carry

    lax.fori_loop(0, slots // 8, attach, 0)


def add_returned(leaf_ref, sums_ref, acc_ref):
    def some(at, tiles):
        for part in range(8):
            owner = at * 8 + part
            leaf = leaf_ref[owner]
            acc_ref[leaf, :, 0:128] += sums_ref[owner, 0:16, :].astype(F32)
            acc_ref[leaf, :, 128:256] += sums_ref[owner, 16:32, :].astype(F32)
            tiles = tiles + sums_ref[owner, 32:40, :].astype(F32)
        return tiles

    return lax.fori_loop(0, sums_ref.shape[0] // 8, some, jnp.zeros((8, 128), F32))


def leaf_kernel(
    leaf_hbm, sums_ref, base_ref, field_ref,
    residual_ref, image_ref, small_ref, message_ref,
    leaf_ref, half_ref, stage_ref, sems,
):
    leaf_copy = pltpu.make_async_copy(leaf_hbm, leaf_ref, sems.at[4])
    leaf_copy.start()
    image_ref[...] = base_ref[...]
    leaf_copy.wait()
    curve, norm = unpack(add_returned(leaf_ref, sums_ref, image_ref))
    step = solve(curve, norm)
    image = image_ref[...].reshape(128, 256)
    residual = field_ref[...].reshape(128, 256) - combine(image, kron_rows(step))
    half_ref[...] = residual.reshape(residual_ref.shape).astype(BF16)
    copies = fill(leaf_ref, half_ref, stage_ref, message_ref, sems)
    residual_ref[...] = residual.reshape(residual_ref.shape)
    small_ref[0] = curve
    small_ref[1] = norm
    small_ref[2] = step
    for copy in copies:
        copy.wait()


def final_kernel(
    leaf_hbm, sums_ref, base_ref, field_ref, residual_ref, image_ref, small_ref, part_ref, steps_ref,
    solution_ref, out_ref, leaf_ref, acc_ref, sem,
):
    leaf_copy = pltpu.make_async_copy(leaf_hbm, leaf_ref, sem)
    leaf_copy.start()
    acc_ref[...] = base_ref[...]
    leaf_copy.wait()
    curve, next_norm = unpack(add_returned(leaf_ref, sums_ref, acc_ref))
    steps = [(steps_ref[step], steps_ref[16, step : step + 1]) for step in range(16)]
    coef = apply_factor(steps, next_norm)
    moved = product(columns(small_ref[0]), coef)
    moved = product(columns(coef.T[0:16]), moved)
    step = solve(curve - moved, next_norm)
    kron_coef = kron_rows(coef)
    residual = residual_ref[...].reshape(128, 256)
    direction = residual + combine(field_ref[...].reshape(128, 256), kron_coef)
    image = acc_ref[...].reshape(128, 256) + combine(
        image_ref[...].reshape(128, 256), kron_coef
    )
    kron_step = kron_rows(step)
    answer = part_ref[...].reshape(128, 256) + combine(direction, kron_step)
    solution_ref[...] = answer.reshape(solution_ref.shape)
    out_ref[...] = (residual - combine(image, kron_step)).reshape(out_ref.shape)


def call(kernel, ins, outs, scratch, cost=None):
    spaces = [HBM if getattr(out, "memory_space", None) == pltpu.HBM else VMEM for out in outs]
    run = pl.pallas_call(
        kernel,
        out_shape=list(outs),
        in_specs=list(ins),
        out_specs=spaces,
        scratch_shapes=list(scratch),
        compiler_params=pltpu.CompilerParams(vmem_limit_bytes=24 * 1024 * 1024),
        cost_estimate=cost,
    )

    def placed(*values):
        return run(
            *(
                pltpu.with_memory_space_constraint(value, spec.memory_space)
                if spec is HBM or spec is KEPT
                else value
                for value, spec in zip(values, ins)
            )
        )

    return placed


def swap(values):
    return lax.all_to_all(values, AXES, split_axis=0, concat_axis=0, tiled=True)


def shards(
    right_sides,
    diag_shift,
    self_blocks,
    near_blocks,
    far_left,
    far_right,
    far_rank,
    send_leaf,
    block_pos,
):
    leaves, rhs, size = right_sides.shape
    slots = send_leaf.shape[1]
    targets = send_leaf.reshape(slots)
    whole = (leaves, rhs, size)
    message = (slots, rhs, size)
    local_cost = pl.CostEstimate(
        flops=4 * leaves * rhs * size * size, bytes_accessed=2 * leaves * size * size, transcendentals=0
    )
    send = call(
        send_kernel,
        [HBM, HBM],
        [pltpu.HBM(message, BF16)],
        [
            pltpu.SMEM((slots,), jnp.int32),
            pltpu.VMEM(whole, F32),
            pltpu.VMEM(whole, BF16),
            pltpu.VMEM(message, BF16),
            pltpu.SemaphoreType.DMA((6,)),
        ],
    )
    base = call(
        base_kernel,
        [VMEM, VMEM, VMEM, HBM, HBM, HBM],
        [
            pltpu.VMEM(whole, F32),
            pltpu.VMEM((2, rhs, 128), F32),
            pltpu.VMEM(near_blocks.shape, BF16),
            pltpu.VMEM(far_left.shape, BF16),
            pltpu.VMEM(far_right.shape, BF16),
        ],
        [pltpu.SemaphoreType.DMA((3,))],
        local_cost,
    )
    next_base = call(
        next_base_kernel,
        [KEPT, VMEM, VMEM, KEPT, VMEM],
        [
            pltpu.VMEM(whole, F32),
            pltpu.VMEM((2, rhs, 128), F32),
            pltpu.VMEM(whole, F32),
            pltpu.VMEM((17, rhs, 128), F32),
        ],
        [],
        local_cost,
    )
    owner = call(
        owner_kernel,
        [HBM, HBM, HBM, KEPT, KEPT, KEPT, KEPT],
        [pltpu.VMEM((slots, 40, 128), BF16)],
        [
            pltpu.SMEM(far_rank.shape, jnp.int32),
            pltpu.SMEM(block_pos.shape, jnp.int32),
            pltpu.VMEM(message, BF16),
            pltpu.VMEM(message, F32),
            pltpu.SemaphoreType.DMA((3,)),
        ],
    )
    leaf = call(
        leaf_kernel,
        [HBM, VMEM, KEPT, VMEM],
        [
            pltpu.VMEM(whole, F32),
            pltpu.VMEM(whole, F32),
            pltpu.VMEM((3, rhs, 128), F32),
            pltpu.HBM(message, BF16),
        ],
        [
            pltpu.SMEM((slots,), jnp.int32),
            pltpu.VMEM(whole, BF16),
            pltpu.VMEM(message, BF16),
            pltpu.SemaphoreType.DMA((5,)),
        ],
    )
    final = call(
        final_kernel,
        [HBM, VMEM, KEPT, VMEM, KEPT, KEPT, KEPT, KEPT, KEPT],
        [jax.ShapeDtypeStruct(whole, F32), jax.ShapeDtypeStruct(whole, F32)],
        [pltpu.SMEM((slots,), jnp.int32), pltpu.VMEM(whole, F32), pltpu.SemaphoreType.DMA],
    )

    with jax.named_scope("send"):
        (outgoing,) = send(targets, right_sides)
    incoming = swap(outgoing)
    with jax.named_scope("base"):
        base_image, small, near, left, right = base(
            right_sides, diag_shift, self_blocks, near_blocks, far_left, far_right
        )
    with jax.named_scope("owner"):
        (sums,) = owner(far_rank, block_pos, incoming, near, left, right, small)
    back = swap(sums)
    with jax.named_scope("leaf"):
        residual, image, old, outgoing = leaf(targets, back, base_image, right_sides)
    incoming = swap(outgoing)
    with jax.named_scope("base"):
        base_image, small, part, steps = next_base(
            residual, diag_shift, self_blocks, old, right_sides
        )
    with jax.named_scope("owner"):
        (sums,) = owner(far_rank, block_pos, incoming, near, left, right, small)
    back = swap(sums)
    with jax.named_scope("final"):
        answer, residual = final(
            targets, back, base_image, right_sides, residual, image, old, part, steps
        )
    return (answer, residual)


def solution(mesh):
    split = P(AXES, None, None)
    placed = (
        split,
        P(AXES, None),
        split,
        split,
        split,
        split,
        P(AXES),
        split,
        P(None, AXES),
    )
    return jax.shard_map(
        shards, mesh=mesh, in_specs=placed, out_specs=(split, split), check_vma=False
    )
```

time: 153 us -> 137 us (0.90)
  Pallas kernels: 34 us -> 24.9 us
  waiting for transfers between devices: 31.2 us -> 26.7 us
  local copies, waits for them, and re-layouts: 18 us -> 15 us
    pallas_call x7, Pallas kernels: 34 us -> 24.9 us  [placed(): run(*(pltpu.with_memory_space_constraint(value, spec.memory_space) if spe...]
    all_to_all x2, waiting for transfers between devices: 31.2 us -> 26.7 us  [swap(): return lax.all_to_all(values, AXES, split_axis=0, concat_axis=0, tiled=True)]
    unnamed x62 -> x42, local copies, waits for them, and re-layouts: 18 us -> 15 us
  transfers between devices with their start and end apart: 2 -> 2, of which waited for: 2 -> 2; matrix products, arithmetic and copies ran while one was open for 0% -> 0% of each run, Pallas kernels for 1% -> 3%
where the time goes in v2:
time: 137 us; the launch traced here: 136 us
  blocking collectives  51.6 us (38%)
  waiting for transfers between devices  26.7 us (19%)
  Pallas kernels  24.9 us (18%)
  starting transfers between devices  16.8 us (12%)
  local copies, waits for them, and re-layouts  15 us (11%)
    all_to_all x2, blocking collectives, swap(): return lax.all_to_all(values, AXES, split_axis=0, concat_axis=0, tiled=True)  51.6 us
    all_to_all x2, waiting for transfers between devices, swap(): return lax.all_to_all(values, AXES, split_axis=0, concat_axis=0, tiled=True)  26.7 us
    pallas_call x7, Pallas kernels, placed(): run(*(pltpu.with_memory_space_constraint(value, spec.memory_space) if spe...  24.9 us
    all_to_all x2, starting transfers between devices, swap(): return lax.all_to_all(values, AXES, split_axis=0, concat_axis=0, tiled=True)  16.8 us
    unnamed x42, local copies, waits for them, and re-layouts  15 us
  transfers between devices with their start and end apart: 2, of which 2 were waited for; matrix products, arithmetic and copies ran while one was open for 0% of the time, Pallas kernels for 3%

profile of v2, /device:TPU:1, one launch (start us, length us, event | category | flops | bytes accessed | tf_op | source)
XLA Modules:
  0.0 135.9 jit_solution(11498009975041122764)
XLA Ops:
  0.6 0.0 copy-start.8
  0.6 0.0 copy-start.18
  0.6 2.1 %send.1 = bf16[128,16,256]{2,1,0:T(8,128)(2,1)} custom-call(s32[128]{0:T(128)} %bitcast.1, f32[8,16,256]{2,1,0:T(8,128)} %field_ref.5), custom_call_target="tpu_custom_call" | custom-call | tf_op jit(solution)/shard_map/send/pallas_call | solution.py:357
  2.7 12.0 %all-to-all-start = ((bf16[128,16,256]{2,1,0:T(8,128)(2,1)}), bf16[128,16,256]{2,1,0:T(8,128)(2,1)}, u32[]{:S(2)}, u32[]{:S(2)}) async-start(bf16[128,16,256]{2,1,0:T(8,128)(2,1)} %send.1), calls=%async_computation | async-start | bytes 2097152 | tf_op jit(solution)/shard_map/all_to_all | solution.py:370
  14.7 0.0 copy-done.8
  14.7 0.0 copy-done.18
  14.7 0.0 copy-start.6
  14.7 1.2 copy-done.6
  16.0 3.0 %base.2 = (f32[8,16,256]{2,1,0:T(8,128)S(1)}, f32[2,16,128]{2,1,0:T(8,128)S(1)}, bf16[24,256,256]{2,1,0:T(8,128)(2,1)S(1)}, bf16[96,32,256]{2,1,0:T(8,128)(2,1)S(1)}, bf16[96,32,256]{2,1,0:T(8,128)(2,1)S(1)}) custom-call(f32[8,16,256]{2,1,0:T(8,128)S(1)} %copy-done.8, f32[8,256]{1,0:T(8,128)S(1)} %copy-done.18, bf16[8,256,256]{2,1,0:T(8,128)(2,1)S(1)} %copy-done.6, ...), custom_call_target="tpu_custom_call" | custom-call | flops 33554432 | bytes 1048576 | tf_op jit(solution)/shard_map/base/pallas_call | solution.py:357
  18.9 0.0 copy-start
  18.9 1.2 copy-done
  20.1 0.0 copy-start.3
  20.1 1.1 copy-done.3
  21.3 12.5 %all-to-all-done.x_hbm = bf16[128,16,256]{2,1,0:T(8,128)(2,1)} async-done(((bf16[128,16,256]{2,1,0:T(8,128)(2,1)}), bf16[128,16,256]{2,1,0:T(8,128)(2,1)}, u32[]{:S(2)}, u32[]{:S(2)}) %all-to-all-start) | async-done | bytes 1048608 | tf_op jit(solution)/shard_map/all_to_all | solution.py:370
  33.8 0.0 copy-start.1
  33.8 1.4 %copy-done.1 = bf16[96,32,256]{2,1,0:T(8,128)(2,1)S(1)} copy-done((bf16[96,32,256]{2,1,0:T(8,128)(2,1)S(1)}, bf16[96,32,256]{2,1,0:T(8,128)(2,1)}, u32[]{:S(2)}) %copy-start.1) | copy-done | bytes 1572888
  35.2 0.0 copy-start.4
  35.2 1.4 %copy-done.4 = bf16[96,32,256]{2,1,0:T(8,128)(2,1)S(1)} copy-done((bf16[96,32,256]{2,1,0:T(8,128)(2,1)S(1)}, bf16[96,32,256]{2,1,0:T(8,128)(2,1)}, u32[]{:S(2)}) %copy-start.4) | copy-done | bytes 1572888
  36.6 6.2 %owner.2 = bf16[128,40,128]{2,1,0:T(8,128)(2,1)S(1)} custom-call(s32[96]{0:T(128)} %rank_hbm.3, s32[2,120]{1,0:T(2,128)} %at_hbm.3, bf16[128,16,256]{2,1,0:T(8,128)(2,1)} %all-to-all-done.x_hbm, bf16[24,256,256]{2,1,0:T(8,128)(2,1)S(1)} %get-tuple-element.15.near_ref, bf16[96,32,256]{2,1,0:T(8,128)(2,1)S(1)} %copy-done.1, ...), custom_call_target="tpu_custom_call" | custom-call | tf_op jit(solution)/shard_map/owner/pallas_call | solution.py:357
  42.8 25.8 %all_to_all.20.sums_ref = bf16[128,40,128]{2,1,0:T(8,128)(2,1)S(1)} all-to-all(bf16[128,40,128]{2,1,0:T(8,128)(2,1)S(1)} %owner.2), channel_id=1, replica_groups=mesh['clus'=32,'grp'=4] {'clus','grp'}, dimensions={0} | all-to-all | bytes 2621440 | tf_op jit(solution)/shard_map/all_to_all | solution.py:370
  68.6 3.2 %leaf.1 = (f32[8,16,256]{2,1,0:T(8,128)S(1)}, f32[8,16,256]{2,1,0:T(8,128)S(1)}, f32[3,16,128]{2,1,0:T(8,128)S(1)}, bf16[128,16,256]{2,1,0:T(8,128)(2,1)}) custom-call(s32[128]{0:T(128)} %bitcast.2, bf16[128,40,128]{2,1,0:T(8,128)(2,1)S(1)} %all_to_all.20.sums_ref, f32[8,16,256]{2,1,0:T(8,128)S(1)} %get-tuple-element.19.base_ref, f32[8,16,256]{2,1,0:T(8,128)S(1)} %copy-done.8), custom_call_target="tpu_custom_call" | custom-call | tf_op jit(solution)/shard_map/leaf/pallas_call | solution.py:357
  71.7 0.0 copy-start.9
  71.7 0.6 copy-done.9
  72.4 0.6 copy-done.15
  73.0 4.9 %all-to-all-start.2 = ((bf16[128,16,256]{2,1,0:T(8,128)(2,1)}), bf16[128,16,256]{2,1,0:T(8,128)(2,1)}, u32[]{:S(2)}, u32[]{:S(2)}) async-start(bf16[128,16,256]{2,1,0:T(8,128)(2,1)} %get-tuple-element.20), calls=%async_computation.2 | async-start | bytes 2097152 | tf_op jit(solution)/shard_map/all_to_all | solution.py:370
  77.9 0.0 copy-start.7
  77.9 1.2 copy-done.7
  79.1 0.7 copy-done.16
  79.8 1.2 base.3
  81.0 0.0 copy-start.11
  81.0 0.6 copy-done.11
  81.7 0.6 copy-done.13
  82.3 0.6 copy-done.19
  82.9 14.2 %all-to-all-done.2.x_hbm = bf16[128,16,256]{2,1,0:T(8,128)(2,1)} async-done(((bf16[128,16,256]{2,1,0:T(8,128)(2,1)}), bf16[128,16,256]{2,1,0:T(8,128)(2,1)}, u32[]{:S(2)}, u32[]{:S(2)}) %all-to-all-start.2) | async-done | bytes 1048608 | tf_op jit(solution)/shard_map/all_to_all | solution.py:370
  97.1 1.4 %copy-done.2 = bf16[96,32,256]{2,1,0:T(8,128)(2,1)S(1)} copy-done((bf16[96,32,256]{2,1,0:T(8,128)(2,1)S(1)}, bf16[96,32,256]{2,1,0:T(8,128)(2,1)}, u32[]{:S(2)}) %copy-start.2) | copy-done | bytes 1572888
  98.5 1.4 %copy-done.5 = bf16[96,32,256]{2,1,0:T(8,128)(2,1)S(1)} copy-done((bf16[96,32,256]{2,1,0:T(8,128)(2,1)S(1)}, bf16[96,32,256]{2,1,0:T(8,128)(2,1)}, u32[]{:S(2)}) %copy-start.5) | copy-done | bytes 1572888
  99.9 0.7 copy-done.20
  100.6 6.1 %owner.3 = bf16[128,40,128]{2,1,0:T(8,128)(2,1)S(1)} custom-call(s32[96]{0:T(128)} %rank_hbm.3, s32[2,120]{1,0:T(2,128)} %at_hbm.3, bf16[128,16,256]{2,1,0:T(8,128)(2,1)} %all-to-all-done.2.x_hbm, bf16[24,256,256]{2,1,0:T(8,128)(2,1)S(1)} %get-tuple-element.15.near_ref, bf16[96,32,256]{2,1,0:T(8,128)(2,1)S(1)} %copy-done.2, ...), custom_call_target="tpu_custom_call" | custom-call | tf_op jit(solution)/shard_map/owner/pallas_call | solution.py:357
  106.8 0.0 copy-start.10
  106.8 0.0 copy-start.12
  106.8 0.0 copy-start.14
  106.8 0.0 copy-start.17
  106.8 25.8 %all_to_all.21.sums_ref = bf16[128,40,128]{2,1,0:T(8,128)(2,1)S(1)} all-to-all(bf16[128,40,128]{2,1,0:T(8,128)(2,1)S(1)} %owner.3), channel_id=1, replica_groups=mesh['clus'=32,'grp'=4] {'clus','grp'}, dimensions={0} | all-to-all | bytes 2621440 | tf_op jit(solution)/shard_map/all_to_all | solution.py:370
  132.6 0.0 copy-done.10
  132.6 0.0 copy-done.12
  132.6 0.0 copy-done.14
  132.6 0.0 copy-done.17
  132.6 3.3 %final.1 = (f32[8,16,256]{2,1,0:T(8,128)}, f32[8,16,256]{2,1,0:T(8,128)}) custom-call(s32[128]{0:T(128)} %bitcast.3, bf16[128,40,128]{2,1,0:T(8,128)(2,1)S(1)} %all_to_all.21.sums_ref, f32[8,16,256]{2,1,0:T(8,128)S(1)} %copy-done.12, f32[8,16,256]{2,1,0:T(8,128)S(1)} %copy-done.8, f32[8,16,256]{2,1,0:T(8,128)S(1)} %get-tuple-element.21.field_ref.residual_ref, ...), custom_call_target="tpu_custom_call" | custom-call | tf_op jit(solution)/shard_map/final/pallas_call | solution.py:357
  (7 shorter events, 0.0 us)
Async XLA Ops:
  0.6 14.1 %copy-start.8 = (f32[8,16,256]{2,1,0:T(8,128)S(1)}, f32[8,16,256]{2,1,0:T(8,128)}, u32[]{:S(2)}) copy-start(f32[8,16,256]{2,1,0:T(8,128)} %field_ref.5) | copy-start | bytes 393220
  0.6 14.1 %copy-start.18 = (f32[8,256]{1,0:T(8,128)S(1)}, f32[8,256]{1,0:T(8,128)}, u32[]{:S(2)}) copy-start(f32[8,256]{1,0:T(8,128)} %shift_ref.3) | copy-start | bytes 24580
  2.7 31.0 %all-to-all-start = ((bf16[128,16,256]{2,1,0:T(8,128)(2,1)}), bf16[128,16,256]{2,1,0:T(8,128)(2,1)}, u32[]{:S(2)}, u32[]{:S(2)}) async-start(bf16[128,16,256]{2,1,0:T(8,128)(2,1)} %send.1), calls=%async_computation | async-start | bytes 2097152 | tf_op jit(solution)/shard_map/all_to_all | solution.py:370
  14.7 1.2 copy-start.6
  18.9 1.2 copy-start
  20.1 1.2 copy-start.3
  33.8 1.4 %copy-start.1 = (bf16[96,32,256]{2,1,0:T(8,128)(2,1)S(1)}, bf16[96,32,256]{2,1,0:T(8,128)(2,1)}, u32[]{:S(2)}) copy-start(bf16[96,32,256]{2,1,0:T(8,128)(2,1)} %copy-done) | copy-start | bytes 4718596
  35.2 1.4 %copy-start.4 = (bf16[96,32,256]{2,1,0:T(8,128)(2,1)S(1)}, bf16[96,32,256]{2,1,0:T(8,128)(2,1)}, u32[]{:S(2)}) copy-start(bf16[96,32,256]{2,1,0:T(8,128)(2,1)} %copy-done.3) | copy-start | bytes 4718596
  71.7 0.7 copy-start.9
  72.4 0.6 copy-start.15
  73.0 24.1 %all-to-all-start.2 = ((bf16[128,16,256]{2,1,0:T(8,128)(2,1)}), bf16[128,16,256]{2,1,0:T(8,128)(2,1)}, u32[]{:S(2)}, u32[]{:S(2)}) async-start(bf16[128,16,256]{2,1,0:T(8,128)(2,1)} %get-tuple-element.20), calls=%async_computation.2 | async-start | bytes 2097152 | tf_op jit(solution)/shard_map/all_to_all | solution.py:370
  77.9 1.2 copy-start.7
  79.1 0.7 copy-start.16
  81.0 0.7 copy-start.11
  81.7 0.6 copy-start.13
  82.3 0.6 copy-start.19
  97.1 1.4 %copy-start.2 = (bf16[96,32,256]{2,1,0:T(8,128)(2,1)S(1)}, bf16[96,32,256]{2,1,0:T(8,128)(2,1)}, u32[]{:S(2)}) copy-start(bf16[96,32,256]{2,1,0:T(8,128)(2,1)} %copy-done) | copy-start | bytes 4718596
  98.5 1.4 %copy-start.5 = (bf16[96,32,256]{2,1,0:T(8,128)(2,1)S(1)}, bf16[96,32,256]{2,1,0:T(8,128)(2,1)}, u32[]{:S(2)}) copy-start(bf16[96,32,256]{2,1,0:T(8,128)(2,1)} %copy-done.3) | copy-start | bytes 4718596
  99.9 0.7 copy-start.20
  106.8 25.9 %copy-start.10 = (f32[8,16,256]{2,1,0:T(8,128)S(1)}, f32[8,16,256]{2,1,0:T(8,128)}, u32[]{:S(2)}) copy-start(f32[8,16,256]{2,1,0:T(8,128)} %copy-done.9) | copy-start | bytes 393220
  106.8 25.8 %copy-start.12 = (f32[8,16,256]{2,1,0:T(8,128)S(1)}, f32[8,16,256]{2,1,0:T(8,128)}, u32[]{:S(2)}) copy-start(f32[8,16,256]{2,1,0:T(8,128)} %copy-done.11) | copy-start | bytes 393220
  106.8 25.8 %copy-start.14 = (f32[8,16,256]{2,1,0:T(8,128)S(1)}, f32[8,16,256]{2,1,0:T(8,128)}, u32[]{:S(2)}) copy-start(f32[8,16,256]{2,1,0:T(8,128)} %copy-done.13) | copy-start | bytes 393220
  106.8 25.8 %copy-start.17 = (f32[3,16,128]{2,1,0:T(8,128)S(1)}, f32[3,16,128]{2,1,0:T(8,128)}, u32[]{:S(2)}) copy-start(f32[3,16,128]{2,1,0:T(8,128)} %copy-done.15) | copy-start | bytes 73732

commit v3 on v2

--- a/solution.py
+++ b/solution.py
@@ -6,6 +6,7 @@
 from jax.sharding import PartitionSpec as P
 
 AXES = ("clus", "grp")
+KEPT_NEAR = 8
 HIGHEST = lax.Precision.HIGHEST
 NT = (((1,), (1,)), ((), ()))
 F32 = jnp.float32
@@ -155,24 +156,26 @@
 
 
 def base_kernel(
-    field_ref, shift_ref, self_ref, near_hbm, left_hbm, right_hbm,
-    base_ref, small_ref, near_ref, left_ref, right_ref, sems,
+    field_ref, shift_ref, self_hbm, near_hbm, base_ref, small_ref, near_ref, self_ref, sems
 ):
-    copies = [
-        pltpu.make_async_copy(near_hbm, near_ref, sems.at[0]),
-        pltpu.make_async_copy(left_hbm, left_ref, sems.at[1]),
-        pltpu.make_async_copy(right_hbm, right_ref, sems.at[2]),
-    ]
-    for copy in copies:
-        copy.start()
+    self_copy = pltpu.make_async_copy(self_hbm, self_ref, sems.at[0])
+    near_copy = pltpu.make_async_copy(
+        near_hbm.at[pl.ds(0, near_ref.shape[0])], near_ref, sems.at[1]
+    )
+    self_copy.start()
+    near_copy.start()
+    self_copy.wait()
     local_product(field_ref, shift_ref, self_ref, base_ref, small_ref)
-    for copy in copies:
-        copy.wait()
+    near_copy.wait()
 
 
 def next_base_kernel(
-    field_ref, shift_ref, self_ref, old_ref, first_ref, base_ref, small_ref, part_ref, steps_ref
+    field_ref, shift_ref, self_hbm, old_ref, first_ref,
+    base_ref, small_ref, part_ref, steps_ref, self_ref, sem,
 ):
+    self_copy = pltpu.make_async_copy(self_hbm, self_ref, sem)
+    self_copy.start()
+    self_copy.wait()
     local_product(field_ref, shift_ref, self_ref, base_ref, small_ref)
     part = combine(first_ref[...].reshape(128, 256), kron_rows(old_ref[2]))
     part_ref[...] = part.reshape(part_ref.shape)
@@ -182,43 +185,53 @@
 
 
 def owner_kernel(
-    rank_hbm, at_hbm, x_hbm, near_ref, left_ref, right_ref, small_ref,
-    out_ref, rank_ref, at_ref, x_ref, acc_ref, sems,
+    rank_hbm, at_hbm, x_ref, kept_ref, near_hbm, left_hbm, right_hbm, small_ref,
+    out_ref, rank_ref, at_ref, near_ref, left_ref, right_ref, acc_ref, sems,
 ):
+    kept = kept_ref.shape[0]
+    streamed = near_ref.shape[0]
+    near = kept + streamed
+    slots = x_ref.shape[0]
+    far = left_ref.shape[0]
     copies = [
         pltpu.make_async_copy(at_hbm, at_ref, sems.at[0]),
-        pltpu.make_async_copy(x_hbm, x_ref, sems.at[1]),
+        pltpu.make_async_copy(near_hbm.at[pl.ds(kept, streamed)], near_ref, sems.at[1]),
         pltpu.make_async_copy(rank_hbm, rank_ref, sems.at[2]),
+        pltpu.make_async_copy(left_hbm, left_ref, sems.at[3]),
+        pltpu.make_async_copy(right_hbm, right_ref, sems.at[4]),
     ]
     for copy in copies:
         copy.start()
-    slots = x_ref.shape[0]
-    near = near_ref.shape[0]
-    far = left_ref.shape[0]
 
     def clear(at, carry):
         acc_ref[pl.ds(at * 8, 8)] = jnp.zeros((8, 16, 256), F32)
         return carry
 
     lax.fori_loop(0, slots // 8, clear, 0)
-    for copy in copies:
+    copies[0].wait()
+
+    def near_part(block_ref, shift):
+        def some(at, carry):
+            sums = []
+            for part in range(8):
+                which = at * 8 + part
+                row, col = at_ref[0, shift + which], at_ref[1, shift + which]
+                block = block_ref[which]
+                sums.append(
+                    (row, lax.dot_general(x_ref[col], block, NT, preferred_element_type=F32))
+                )
+                sums.append((col, jnp.dot(x_ref[row], block, preferred_element_type=F32)))
+            for slot, value in sums:
+                acc_ref[slot] += value
+            return carry
+
+        lax.fori_loop(0, block_ref.shape[0] // 8, some, 0)
+
+    near_part(kept_ref, 0)
+    copies[1].wait()
+    near_part(near_ref, kept)
+    for copy in copies[2:]:
         copy.wait()
-
-    def near_some(at, carry):
-        sums = []
-        for part in range(8):
-            which = at * 8 + part
-            row, col = at_ref[0, which], at_ref[1, which]
-            block = near_ref[which]
-            sums.append(
-                (row, lax.dot_general(x_ref[col], block, NT, preferred_element_type=F32))
-            )
-            sums.append((col, jnp.dot(x_ref[row], block, preferred_element_type=F32)))
-        for slot, value in sums:
-            acc_ref[slot] += value
-        return carry
-
-    lax.fori_loop(0, near // 8, near_some, 0)
 
     lane = iota((16, 256), 1)
 
@@ -403,39 +416,39 @@
     )
     base = call(
         base_kernel,
-        [VMEM, VMEM, VMEM, HBM, HBM, HBM],
+        [VMEM, VMEM, HBM, HBM],
         [
             pltpu.VMEM(whole, F32),
             pltpu.VMEM((2, rhs, 128), F32),
-            pltpu.VMEM(near_blocks.shape, BF16),
-            pltpu.VMEM(far_left.shape, BF16),
-            pltpu.VMEM(far_right.shape, BF16),
+            pltpu.VMEM((KEPT_NEAR, size, size), BF16),
         ],
-        [pltpu.SemaphoreType.DMA((3,))],
+        [pltpu.VMEM(self_blocks.shape, BF16), pltpu.SemaphoreType.DMA((2,))],
         local_cost,
     )
     next_base = call(
         next_base_kernel,
-        [KEPT, VMEM, VMEM, KEPT, VMEM],
+        [KEPT, VMEM, HBM, KEPT, VMEM],
         [
             pltpu.VMEM(whole, F32),
             pltpu.VMEM((2, rhs, 128), F32),
             pltpu.VMEM(whole, F32),
             pltpu.VMEM((17, rhs, 128), F32),
         ],
-        [],
+        [pltpu.VMEM(self_blocks.shape, BF16), pltpu.SemaphoreType.DMA],
         local_cost,
     )
     owner = call(
         owner_kernel,
-        [HBM, HBM, HBM, KEPT, KEPT, KEPT, KEPT],
+        [HBM, HBM, VMEM, KEPT, HBM, HBM, HBM, KEPT],
         [pltpu.VMEM((slots, 40, 128), BF16)],
         [
             pltpu.SMEM(far_rank.shape, jnp.int32),
             pltpu.SMEM(block_pos.shape, jnp.int32),
-            pltpu.VMEM(message, BF16),
+            pltpu.VMEM((near_blocks.shape[0] - KEPT_NEAR, size, size), BF16),
+            pltpu.VMEM(far_left.shape, BF16),
+            pltpu.VMEM(far_right.shape, BF16),
             pltpu.VMEM(message, F32),
-            pltpu.SemaphoreType.DMA((3,)),
+            pltpu.SemaphoreType.DMA((5,)),
         ],
     )
     leaf = call(
@@ -465,11 +478,11 @@
         (outgoing,) = send(targets, right_sides)
     incoming = swap(outgoing)
     with jax.named_scope("base"):
-        base_image, small, near, left, right = base(
-            right_sides, diag_shift, self_blocks, near_blocks, far_left, far_right
+        base_image, small, kept = base(
+            right_sides, diag_shift, self_blocks, near_blocks
         )
     with jax.named_scope("owner"):
-        (sums,) = owner(far_rank, block_pos, incoming, near, left, right, small)
+        (sums,) = owner(far_rank, block_pos, incoming, kept, near_blocks, far_left, far_right, small)
     back = swap(sums)
     with jax.named_scope("leaf"):
         residual, image, old, outgoing = leaf(targets, back, base_image, right_sides)
@@ -479,7 +492,7 @@
             residual, diag_shift, self_blocks, old, right_sides
         )
     with jax.named_scope("owner"):
-        (sums,) = owner(far_rank, block_pos, incoming, near, left, right, small)
+        (sums,) = owner(far_rank, block_pos, incoming, kept, near_blocks, far_left, far_right, small)
     back = swap(sums)
     with jax.named_scope("final"):
         answer, residual = final(

time: 137 us -> 127 us (0.927)
  local copies, waits for them, and re-layouts: 15 us -> 0.01 us
  waiting for transfers between devices: 26.7 us -> 34.2 us
  starting transfers between devices: 16.8 us -> 15.3 us
    unnamed x42 -> x4, local copies, waits for them, and re-layouts: 15 us -> 0.01 us
    all_to_all x2, waiting for transfers between devices: 26.7 us -> 34.2 us  [swap(): return lax.all_to_all(values, AXES, split_axis=0, concat_axis=0, tiled=True)]
    all_to_all x2, starting transfers between devices: 16.8 us -> 15.3 us  [swap(): return lax.all_to_all(values, AXES, split_axis=0, concat_axis=0, tiled=True)]
  transfers between devices with their start and end apart: 2 -> 2, of which waited for: 2 -> 2; matrix products, arithmetic and copies ran while one was open for 0% -> 0% of each run, Pallas kernels for 3% -> 4%
where the time goes in v3:
time: 127 us
  blocking collectives  51.6 us (41%)
  waiting for transfers between devices  34.2 us (27%)
  Pallas kernels  25.1 us (20%)
  starting transfers between devices  15.3 us (12%)
    all_to_all x2, blocking collectives, swap(): return lax.all_to_all(values, AXES, split_axis=0, concat_axis=0, tiled=True)  51.6 us
    all_to_all x2, waiting for transfers between devices, swap(): return lax.all_to_all(values, AXES, split_axis=0, concat_axis=0, tiled=True)  34.2 us
    pallas_call x7, Pallas kernels, placed(): run(*(pltpu.with_memory_space_constraint(value, spec.memory_space) if spe...  25.1 us
    all_to_all x2, starting transfers between devices, swap(): return lax.all_to_all(values, AXES, split_axis=0, concat_axis=0, tiled=True)  15.3 us
  transfers between devices with their start and end apart: 2, of which 2 were waited for; matrix products, arithmetic and copies ran while one was open for 0% of the time, Pallas kernels for 4%

profile of v3, /device:TPU:1, one launch (start us, length us, event | category | flops | bytes accessed | tf_op | source)
XLA Modules:
  0.0 127.0 jit_solution(8157862156133451415)
XLA Ops:
  0.6 2.0 %send.1 = bf16[128,16,256]{2,1,0:T(8,128)(2,1)} custom-call(s32[128]{0:T(128)} %bitcast.1, f32[8,16,256]{2,1,0:T(8,128)} %field_ref.5), custom_call_target="tpu_custom_call" | custom-call | tf_op jit(solution)/shard_map/send/pallas_call | solution.py:370
  2.6 0.0 copy-start
  2.6 0.0 copy-start.1
  2.7 11.5 %all-to-all-start = ((bf16[128,16,256]{2,1,0:T(8,128)(2,1)}), bf16[128,16,256]{2,1,0:T(8,128)(2,1)S(1)}, u32[]{:S(2)}, u32[]{:S(2)}) async-start(bf16[128,16,256]{2,1,0:T(8,128)(2,1)} %send.1), calls=%async_computation | async-start | bytes 2097152 | tf_op jit(solution)/shard_map/all_to_all | solution.py:383
  14.2 0.0 copy-done
  14.2 0.0 copy-done.1
  14.2 2.3 %base.2 = (f32[8,16,256]{2,1,0:T(8,128)S(1)}, f32[2,16,128]{2,1,0:T(8,128)S(1)}, bf16[8,256,256]{2,1,0:T(8,128)(2,1)S(1)}) custom-call(f32[8,16,256]{2,1,0:T(8,128)S(1)} %copy-done, f32[8,256]{1,0:T(8,128)S(1)} %copy-done.1, bf16[8,256,256]{2,1,0:T(8,128)(2,1)} %self_hbm.3, bf16[24,256,256]{2,1,0:T(8,128)(2,1)} %near_hbm.5), custom_call_target="tpu_custom_call" | custom-call | flops 33554432 | bytes 1048576 | tf_op jit(solution)/shard_map/base/pallas_call | solution.py:370
  16.5 17.1 %all-to-all-done.x_ref = bf16[128,16,256]{2,1,0:T(8,128)(2,1)S(1)} async-done(((bf16[128,16,256]{2,1,0:T(8,128)(2,1)}), bf16[128,16,256]{2,1,0:T(8,128)(2,1)S(1)}, u32[]{:S(2)}, u32[]{:S(2)}) %all-to-all-start) | async-done | bytes 1048608 | tf_op jit(solution)/shard_map/all_to_all | solution.py:383
  33.6 6.0 %owner.2 = bf16[128,40,128]{2,1,0:T(8,128)(2,1)S(1)} custom-call(s32[96]{0:T(128)} %rank_hbm.3, s32[2,120]{1,0:T(2,128)} %at_hbm.3, bf16[128,16,256]{2,1,0:T(8,128)(2,1)S(1)} %all-to-all-done.x_ref, bf16[8,256,256]{2,1,0:T(8,128)(2,1)S(1)} %get-tuple-element.13.kept_ref, bf16[24,256,256]{2,1,0:T(8,128)(2,1)} %near_hbm.5, bf16[96,32,256]{2,1,0:T(8,128)(2,1)} %left_hbm.3, ...), custom_call_target="tpu_custom_call" | custom-call | tf_op jit(solution)/shard_map/owner/pallas_call | solution.py:370
  39.6 25.8 %all_to_all.20.sums_ref = bf16[128,40,128]{2,1,0:T(8,128)(2,1)S(1)} all-to-all(bf16[128,40,128]{2,1,0:T(8,128)(2,1)S(1)} %owner.2), channel_id=1, replica_groups=mesh['clus'=32,'grp'=4] {'clus','grp'}, dimensions={0} | all-to-all | bytes 2621440 | tf_op jit(solution)/shard_map/all_to_all | solution.py:383
  65.4 3.1 %leaf.1 = (f32[8,16,256]{2,1,0:T(8,128)S(1)}, f32[8,16,256]{2,1,0:T(8,128)S(1)}, f32[3,16,128]{2,1,0:T(8,128)S(1)}, bf16[128,16,256]{2,1,0:T(8,128)(2,1)}) custom-call(s32[128]{0:T(128)} %bitcast.2, bf16[128,40,128]{2,1,0:T(8,128)(2,1)S(1)} %all_to_all.20.sums_ref, f32[8,16,256]{2,1,0:T(8,128)S(1)} %get-tuple-element.15.base_ref, f32[8,16,256]{2,1,0:T(8,128)S(1)} %copy-done), custom_call_target="tpu_custom_call" | custom-call | tf_op jit(solution)/shard_map/leaf/pallas_call | solution.py:370
  68.5 3.8 %all-to-all-start.2 = ((bf16[128,16,256]{2,1,0:T(8,128)(2,1)}), bf16[128,16,256]{2,1,0:T(8,128)(2,1)S(1)}, u32[]{:S(2)}, u32[]{:S(2)}) async-start(bf16[128,16,256]{2,1,0:T(8,128)(2,1)} %get-tuple-element.16), calls=%async_computation.2 | async-start | bytes 2097152 | tf_op jit(solution)/shard_map/all_to_all | solution.py:383
  72.3 2.4 %base.3 = (f32[8,16,256]{2,1,0:T(8,128)S(1)}, f32[2,16,128]{2,1,0:T(8,128)S(1)}, f32[8,16,256]{2,1,0:T(8,128)S(1)}, f32[17,16,128]{2,1,0:T(8,128)S(1)}) custom-call(f32[8,16,256]{2,1,0:T(8,128)S(1)} %get-tuple-element.17.field_ref.residual_ref, f32[8,256]{1,0:T(8,128)S(1)} %copy-done.1, bf16[8,256,256]{2,1,0:T(8,128)(2,1)} %self_hbm.3, ...), custom_call_target="tpu_custom_call" | custom-call | flops 33554432 | bytes 1048576 | tf_op jit(solution)/shard_map/base/pallas_call | solution.py:370
  74.8 17.1 %all-to-all-done.2.x_ref = bf16[128,16,256]{2,1,0:T(8,128)(2,1)S(1)} async-done(((bf16[128,16,256]{2,1,0:T(8,128)(2,1)}), bf16[128,16,256]{2,1,0:T(8,128)(2,1)S(1)}, u32[]{:S(2)}, u32[]{:S(2)}) %all-to-all-start.2) | async-done | bytes 1048608 | tf_op jit(solution)/shard_map/all_to_all | solution.py:383
  91.9 6.0 %owner.3 = bf16[128,40,128]{2,1,0:T(8,128)(2,1)S(1)} custom-call(s32[96]{0:T(128)} %rank_hbm.3, s32[2,120]{1,0:T(2,128)} %at_hbm.3, bf16[128,16,256]{2,1,0:T(8,128)(2,1)S(1)} %all-to-all-done.2.x_ref, bf16[8,256,256]{2,1,0:T(8,128)(2,1)S(1)} %get-tuple-element.13.kept_ref, bf16[24,256,256]{2,1,0:T(8,128)(2,1)} %near_hbm.5, bf16[96,32,256]{2,1,0:T(8,128)(2,1)} %left_hbm.3, ...), custom_call_target="tpu_custom_call" | custom-call | tf_op jit(solution)/shard_map/owner/pallas_call | solution.py:370
  97.9 25.8 %all_to_all.21.sums_ref = bf16[128,40,128]{2,1,0:T(8,128)(2,1)S(1)} all-to-all(bf16[128,40,128]{2,1,0:T(8,128)(2,1)S(1)} %owner.3), channel_id=1, replica_groups=mesh['clus'=32,'grp'=4] {'clus','grp'}, dimensions={0} | all-to-all | bytes 2621440 | tf_op jit(solution)/shard_map/all_to_all | solution.py:383
  123.7 3.3 %final.1 = (f32[8,16,256]{2,1,0:T(8,128)}, f32[8,16,256]{2,1,0:T(8,128)}) custom-call(s32[128]{0:T(128)} %bitcast.3, bf16[128,40,128]{2,1,0:T(8,128)(2,1)S(1)} %all_to_all.21.sums_ref, f32[8,16,256]{2,1,0:T(8,128)S(1)} %get-tuple-element.20.base_ref, f32[8,16,256]{2,1,0:T(8,128)S(1)} %copy-done, f32[8,16,256]{2,1,0:T(8,128)S(1)} %get-tuple-element.17.field_ref.residual_ref, ...), custom_call_target="tpu_custom_call" | custom-call | tf_op jit(solution)/shard_map/final/pallas_call | solution.py:370
Async XLA Ops:
  2.6 11.5 %copy-start = (f32[8,16,256]{2,1,0:T(8,128)S(1)}, f32[8,16,256]{2,1,0:T(8,128)}, u32[]{:S(2)}) copy-start(f32[8,16,256]{2,1,0:T(8,128)} %field_ref.5) | copy-start | bytes 393220
  2.6 11.5 %copy-start.1 = (f32[8,256]{1,0:T(8,128)S(1)}, f32[8,256]{1,0:T(8,128)}, u32[]{:S(2)}) copy-start(f32[8,256]{1,0:T(8,128)} %shift_ref.3) | copy-start | bytes 24580
  2.7 30.9 %all-to-all-start = ((bf16[128,16,256]{2,1,0:T(8,128)(2,1)}), bf16[128,16,256]{2,1,0:T(8,128)(2,1)S(1)}, u32[]{:S(2)}, u32[]{:S(2)}) async-start(bf16[128,16,256]{2,1,0:T(8,128)(2,1)} %send.1), calls=%async_computation | async-start | bytes 2097152 | tf_op jit(solution)/shard_map/all_to_all | solution.py:383
  68.5 23.4 %all-to-all-start.2 = ((bf16[128,16,256]{2,1,0:T(8,128)(2,1)}), bf16[128,16,256]{2,1,0:T(8,128)(2,1)S(1)}, u32[]{:S(2)}, u32[]{:S(2)}) async-start(bf16[128,16,256]{2,1,0:T(8,128)(2,1)} %get-tuple-element.16), calls=%async_computation.2 | async-start | bytes 2097152 | tf_op jit(solution)/shard_map/all_to_all | solution.py:383

commit v4 on v3

--- a/solution.py
+++ b/solution.py
@@ -15,6 +15,7 @@
 VMEM = pl.BlockSpec(memory_space=pltpu.VMEM)
 HBM = pl.BlockSpec(memory_space=pltpu.HBM)
 KEPT = pl.BlockSpec(memory_space=pltpu.VMEM)
+TABLE = pl.BlockSpec(memory_space=pltpu.SMEM)
 
 
 def iota(shape, dim):
@@ -56,9 +57,9 @@
     return [jnp.broadcast_to(matrix[:, at : at + 1], (16, 128)) for at in range(16)]
 
 
-def factor(matrix):
+def factor(parts):
     row_at = iota((16, 128), 0)
-    left = columns(matrix)
+    left = list(parts)
     steps = []
     for step in range(16):
         column = left[step]
@@ -79,8 +80,8 @@
     return target
 
 
-def solve(matrix, target):
-    return apply_factor(factor(matrix), target)
+def solve(parts, target):
+    return apply_factor(factor(parts), target)
 
 
 def product(left, right):
@@ -107,8 +108,26 @@
 def unpack(tile):
     group = iota((8, 128), 1) // 16
     joined = tile + pltpu.roll(tile, 128 - 32, 1)
-    halves = [spread(jnp.where(group == at, joined, 0.0)) for at in (0, 1, 4, 5)]
-    return jnp.concatenate(halves[0:2], axis=0), jnp.concatenate(halves[2:4], axis=0)
+    first = [
+        jnp.concatenate(
+            [
+                jnp.broadcast_to(joined[:, at : at + 1], (8, 128)),
+                jnp.broadcast_to(joined[:, 16 + at : 17 + at], (8, 128)),
+            ],
+            axis=0,
+        )
+        for at in range(16)
+    ]
+    halves = [spread(jnp.where(group == at, joined, 0.0)) for at in (4, 5)]
+    return first, jnp.concatenate(halves, axis=0)
+
+
+def from_columns(parts):
+    group = iota((16, 128), 1) % 16
+    matrix = parts[0]
+    for at in range(1, 16):
+        matrix = jnp.where(group == at, parts[at], matrix)
+    return matrix
 
 
 def fill(leaf_ref, half_ref, stage_ref, message_ref, sems):
@@ -156,8 +175,16 @@
 
 
 def base_kernel(
-    field_ref, shift_ref, self_hbm, near_hbm, base_ref, small_ref, near_ref, self_ref, sems
+    field_ref, shift_ref, self_hbm, near_hbm, leaf_hbm, rank_hbm, at_hbm,
+    base_ref, small_ref, near_ref, leaf_ref, rank_ref, at_ref, self_ref, sems,
 ):
+    tables = [
+        pltpu.make_async_copy(leaf_hbm, leaf_ref, sems.at[2]),
+        pltpu.make_async_copy(rank_hbm, rank_ref, sems.at[3]),
+        pltpu.make_async_copy(at_hbm, at_ref, sems.at[4]),
+    ]
+    for table in tables:
+        table.start()
     self_copy = pltpu.make_async_copy(self_hbm, self_ref, sems.at[0])
     near_copy = pltpu.make_async_copy(
         near_hbm.at[pl.ds(0, near_ref.shape[0])], near_ref, sems.at[1]
@@ -167,6 +194,8 @@
     self_copy.wait()
     local_product(field_ref, shift_ref, self_ref, base_ref, small_ref)
     near_copy.wait()
+    for table in tables:
+        table.wait()
 
 
 def next_base_kernel(
@@ -179,14 +208,14 @@
     local_product(field_ref, shift_ref, self_ref, base_ref, small_ref)
     part = combine(first_ref[...].reshape(128, 256), kron_rows(old_ref[2]))
     part_ref[...] = part.reshape(part_ref.shape)
-    for step, (column, scale) in enumerate(factor(old_ref[1])):
+    for step, (column, scale) in enumerate(factor(columns(old_ref[1]))):
         steps_ref[step] = column
         steps_ref[16, step : step + 1] = scale
 
 
 def owner_kernel(
-    rank_hbm, at_hbm, x_ref, kept_ref, near_hbm, left_hbm, right_hbm, small_ref,
-    out_ref, rank_ref, at_ref, near_ref, left_ref, right_ref, acc_ref, sems,
+    rank_ref, at_ref, x_ref, kept_ref, near_hbm, left_hbm, right_hbm, small_ref,
+    out_ref, near_ref, left_ref, right_ref, acc_ref, sems,
 ):
     kept = kept_ref.shape[0]
     streamed = near_ref.shape[0]
@@ -194,11 +223,9 @@
     slots = x_ref.shape[0]
     far = left_ref.shape[0]
     copies = [
-        pltpu.make_async_copy(at_hbm, at_ref, sems.at[0]),
-        pltpu.make_async_copy(near_hbm.at[pl.ds(kept, streamed)], near_ref, sems.at[1]),
-        pltpu.make_async_copy(rank_hbm, rank_ref, sems.at[2]),
-        pltpu.make_async_copy(left_hbm, left_ref, sems.at[3]),
-        pltpu.make_async_copy(right_hbm, right_ref, sems.at[4]),
+        pltpu.make_async_copy(near_hbm.at[pl.ds(kept, streamed)], near_ref, sems.at[0]),
+        pltpu.make_async_copy(left_hbm, left_ref, sems.at[1]),
+        pltpu.make_async_copy(right_hbm, right_ref, sems.at[2]),
     ]
     for copy in copies:
         copy.start()
@@ -208,29 +235,23 @@
         return carry
 
     lax.fori_loop(0, slots // 8, clear, 0)
+
+    def near_part(block_ref, shift):
+        sums = []
+        for which in range(block_ref.shape[0]):
+            row, col = at_ref[0, shift + which], at_ref[1, shift + which]
+            block = block_ref[which]
+            sums.append(
+                (row, lax.dot_general(x_ref[col], block, NT, preferred_element_type=F32))
+            )
+            sums.append((col, jnp.dot(x_ref[row], block, preferred_element_type=F32)))
+        for slot, value in sums:
+            acc_ref[slot] += value
+
+    near_part(kept_ref, 0)
     copies[0].wait()
-
-    def near_part(block_ref, shift):
-        def some(at, carry):
-            sums = []
-            for part in range(8):
-                which = at * 8 + part
-                row, col = at_ref[0, shift + which], at_ref[1, shift + which]
-                block = block_ref[which]
-                sums.append(
-                    (row, lax.dot_general(x_ref[col], block, NT, preferred_element_type=F32))
-                )
-                sums.append((col, jnp.dot(x_ref[row], block, preferred_element_type=F32)))
-            for slot, value in sums:
-                acc_ref[slot] += value
-            return carry
-
-        lax.fori_loop(0, block_ref.shape[0] // 8, some, 0)
-
-    near_part(kept_ref, 0)
-    copies[1].wait()
     near_part(near_ref, kept)
-    for copy in copies[2:]:
+    for copy in copies[1:]:
         copy.wait()
 
     lane = iota((16, 256), 1)
@@ -258,7 +279,7 @@
     def far_some(at, carry):
         sums = []
         for rows, cols, left, right, right_proj, left_proj in [
-            far_project(at * 32 + 8 * group) for group in range(4)
+            far_project(at * 48 + 8 * group) for group in range(6)
         ]:
             to_row = jnp.dot(right_proj, left, preferred_element_type=F32)
             to_col = jnp.dot(left_proj, right, preferred_element_type=F32)
@@ -269,7 +290,7 @@
             acc_ref[slot] += value
         return carry
 
-    lax.fori_loop(0, far // 32, far_some, 0)
+    lax.fori_loop(0, far // 48, far_some, 0)
 
     products = jnp.zeros((128, 128), F32)
     for at in range(slots // 8):
@@ -306,14 +327,11 @@
 
 
 def leaf_kernel(
-    leaf_hbm, sums_ref, base_ref, field_ref,
+    leaf_ref, sums_ref, base_ref, field_ref,
     residual_ref, image_ref, small_ref, message_ref,
-    leaf_ref, half_ref, stage_ref, sems,
+    half_ref, stage_ref, sems,
 ):
-    leaf_copy = pltpu.make_async_copy(leaf_hbm, leaf_ref, sems.at[4])
-    leaf_copy.start()
     image_ref[...] = base_ref[...]
-    leaf_copy.wait()
     curve, norm = unpack(add_returned(leaf_ref, sums_ref, image_ref))
     step = solve(curve, norm)
     image = image_ref[...].reshape(128, 256)
@@ -321,7 +339,7 @@
     half_ref[...] = residual.reshape(residual_ref.shape).astype(BF16)
     copies = fill(leaf_ref, half_ref, stage_ref, message_ref, sems)
     residual_ref[...] = residual.reshape(residual_ref.shape)
-    small_ref[0] = curve
+    small_ref[0] = from_columns(curve)
     small_ref[1] = norm
     small_ref[2] = step
     for copy in copies:
@@ -329,19 +347,17 @@
 
 
 def final_kernel(
-    leaf_hbm, sums_ref, base_ref, field_ref, residual_ref, image_ref, small_ref, part_ref, steps_ref,
-    solution_ref, out_ref, leaf_ref, acc_ref, sem,
+    leaf_ref, sums_ref, base_ref, field_ref, residual_ref, image_ref, small_ref, part_ref, steps_ref,
+    solution_ref, out_ref, acc_ref,
 ):
-    leaf_copy = pltpu.make_async_copy(leaf_hbm, leaf_ref, sem)
-    leaf_copy.start()
     acc_ref[...] = base_ref[...]
-    leaf_copy.wait()
     curve, next_norm = unpack(add_returned(leaf_ref, sums_ref, acc_ref))
     steps = [(steps_ref[step], steps_ref[16, step : step + 1]) for step in range(16)]
     coef = apply_factor(steps, next_norm)
     moved = product(columns(small_ref[0]), coef)
     moved = product(columns(coef.T[0:16]), moved)
-    step = solve(curve - moved, next_norm)
+    moved = columns(moved)
+    step = solve([curve[at] - moved[at] for at in range(16)], next_norm)
     kron_coef = kron_rows(coef)
     residual = residual_ref[...].reshape(128, 256)
     direction = residual + combine(field_ref[...].reshape(128, 256), kron_coef)
@@ -355,7 +371,8 @@
 
 
 def call(kernel, ins, outs, scratch, cost=None):
-    spaces = [HBM if getattr(out, "memory_space", None) == pltpu.HBM else VMEM for out in outs]
+    kinds = {pltpu.HBM: HBM, pltpu.SMEM: TABLE}
+    spaces = [kinds.get(getattr(out, "memory_space", None), VMEM) for out in outs]
     run = pl.pallas_call(
         kernel,
         out_shape=list(outs),
@@ -370,7 +387,7 @@
         return run(
             *(
                 pltpu.with_memory_space_constraint(value, spec.memory_space)
-                if spec is HBM or spec is KEPT
+                if spec is not VMEM
                 else value
                 for value, spec in zip(values, ins)
             )
@@ -416,13 +433,16 @@
     )
     base = call(
         base_kernel,
-        [VMEM, VMEM, HBM, HBM],
+        [VMEM, VMEM, HBM, HBM, HBM, HBM, HBM],
         [
             pltpu.VMEM(whole, F32),
             pltpu.VMEM((2, rhs, 128), F32),
             pltpu.VMEM((KEPT_NEAR, size, size), BF16),
+            pltpu.SMEM((slots,), jnp.int32),
+            pltpu.SMEM(far_rank.shape, jnp.int32),
+            pltpu.SMEM(block_pos.shape, jnp.int32),
         ],
-        [pltpu.VMEM(self_blocks.shape, BF16), pltpu.SemaphoreType.DMA((2,))],
+        [pltpu.VMEM(self_blocks.shape, BF16), pltpu.SemaphoreType.DMA((5,))],
         local_cost,
     )
     next_base = call(
@@ -439,21 +459,19 @@
     )
     owner = call(
         owner_kernel,
-        [HBM, HBM, VMEM, KEPT, HBM, HBM, HBM, KEPT],
+        [TABLE, TABLE, VMEM, KEPT, HBM, HBM, HBM, KEPT],
         [pltpu.VMEM((slots, 40, 128), BF16)],
         [
-            pltpu.SMEM(far_rank.shape, jnp.int32),
-            pltpu.SMEM(block_pos.shape, jnp.int32),
             pltpu.VMEM((near_blocks.shape[0] - KEPT_NEAR, size, size), BF16),
             pltpu.VMEM(far_left.shape, BF16),
             pltpu.VMEM(far_right.shape, BF16),
             pltpu.VMEM(message, F32),
-            pltpu.SemaphoreType.DMA((5,)),
+            pltpu.SemaphoreType.DMA((3,)),
         ],
     )
     leaf = call(
         leaf_kernel,
-        [HBM, VMEM, KEPT, VMEM],
+        [TABLE, VMEM, KEPT, VMEM],
         [
             pltpu.VMEM(whole, F32),
             pltpu.VMEM(whole, F32),
@@ -461,42 +479,45 @@
             pltpu.HBM(message, BF16),
         ],
         [
-            pltpu.SMEM((slots,), jnp.int32),
             pltpu.VMEM(whole, BF16),
             pltpu.VMEM(message, BF16),
-            pltpu.SemaphoreType.DMA((5,)),
+            pltpu.SemaphoreType.DMA((4,)),
         ],
     )
     final = call(
         final_kernel,
-        [HBM, VMEM, KEPT, VMEM, KEPT, KEPT, KEPT, KEPT, KEPT],
+        [TABLE, VMEM, KEPT, VMEM, KEPT, KEPT, KEPT, KEPT, KEPT],
         [jax.ShapeDtypeStruct(whole, F32), jax.ShapeDtypeStruct(whole, F32)],
-        [pltpu.SMEM((slots,), jnp.int32), pltpu.VMEM(whole, F32), pltpu.SemaphoreType.DMA],
+        [pltpu.VMEM(whole, F32)],
     )
 
     with jax.named_scope("send"):
         (outgoing,) = send(targets, right_sides)
     incoming = swap(outgoing)
     with jax.named_scope("base"):
-        base_image, small, kept = base(
-            right_sides, diag_shift, self_blocks, near_blocks
+        base_image, small, kept, leaf_table, rank_table, at_table = base(
+            right_sides, diag_shift, self_blocks, near_blocks, targets, far_rank, block_pos
         )
     with jax.named_scope("owner"):
-        (sums,) = owner(far_rank, block_pos, incoming, kept, near_blocks, far_left, far_right, small)
+        (sums,) = owner(
+            rank_table, at_table, incoming, kept, near_blocks, far_left, far_right, small
+        )
     back = swap(sums)
     with jax.named_scope("leaf"):
-        residual, image, old, outgoing = leaf(targets, back, base_image, right_sides)
+        residual, image, old, outgoing = leaf(leaf_table, back, base_image, right_sides)
     incoming = swap(outgoing)
     with jax.named_scope("base"):
         base_image, small, part, steps = next_base(
             residual, diag_shift, self_blocks, old, right_sides
         )
     with jax.named_scope("owner"):
-        (sums,) = owner(far_rank, block_pos, incoming, kept, near_blocks, far_left, far_right, small)
+        (sums,) = owner(
+            rank_table, at_table, incoming, kept, near_blocks, far_left, far_right, small
+        )
     back = swap(sums)
     with jax.named_scope("final"):
         answer, residual = final(
-            targets, back, base_image, right_sides, residual, image, old, part, steps
+            leaf_table, back, base_image, right_sides, residual, image, old, part, steps
         )
     return (answer, residual)
 

time: 127 us -> 125 us (0.984)
  Pallas kernels: 25.1 us -> 22.7 us
    pallas_call x7, Pallas kernels: 25.1 us -> 22.7 us  [placed(): run(*(pltpu.with_memory_space_constraint(value, spec.memory_space) if spe...]
where the time goes in v4:
time: 125 us
  blocking collectives  51.6 us (41%)
  waiting for transfers between devices  34.2 us (27%)
  Pallas kernels  22.7 us (18%)
  starting transfers between devices  15.3 us (12%)
    all_to_all x2, blocking collectives, swap(): return lax.all_to_all(values, AXES, split_axis=0, concat_axis=0, tiled=True)  51.6 us
    all_to_all x2, waiting for transfers between devices, swap(): return lax.all_to_all(values, AXES, split_axis=0, concat_axis=0, tiled=True)  34.2 us
    pallas_call x7, Pallas kernels, placed(): run(*(pltpu.with_memory_space_constraint(value, spec.memory_space) if spe...  22.7 us
    all_to_all x2, starting transfers between devices, swap(): return lax.all_to_all(values, AXES, split_axis=0, concat_axis=0, tiled=True)  15.3 us
  transfers between devices with their start and end apart: 2, of which 2 were waited for; matrix products, arithmetic and copies ran while one was open for 0% of the time, Pallas kernels for 4%

profile of v4, /device:TPU:1, one launch (start us, length us, event | category | flops | bytes accessed | tf_op | source)
XLA Modules:
  0.0 124.6 jit_solution(17428801244114665781)
XLA Ops:
  0.6 2.0 %send.1 = bf16[128,16,256]{2,1,0:T(8,128)(2,1)} custom-call(s32[128]{0:T(128)} %bitcast.1, f32[8,16,256]{2,1,0:T(8,128)} %field_ref.5), custom_call_target="tpu_custom_call" | custom-call | tf_op jit(solution)/shard_map/send/pallas_call | solution.py:387
  2.6 0.0 copy-start
  2.6 0.0 copy-start.1
  2.7 11.5 %all-to-all-start = ((bf16[128,16,256]{2,1,0:T(8,128)(2,1)}), bf16[128,16,256]{2,1,0:T(8,128)(2,1)S(1)}, u32[]{:S(2)}, u32[]{:S(2)}) async-start(bf16[128,16,256]{2,1,0:T(8,128)(2,1)} %send.1), calls=%async_computation | async-start | bytes 2097152 | tf_op jit(solution)/shard_map/all_to_all | solution.py:400
  14.2 0.0 copy-done
  14.2 0.0 copy-done.1
  14.2 2.4 %base.2 = (f32[8,16,256]{2,1,0:T(8,128)S(1)}, f32[2,16,128]{2,1,0:T(8,128)S(1)}, bf16[8,256,256]{2,1,0:T(8,128)(2,1)S(1)}, s32[128]{0:T(128)S(4)}, s32[96]{0:T(128)S(4)}, /*index=5*/s32[2,120]{1,0:T(2,128)S(4)}) custom-call(f32[8,16,256]{2,1,0:T(8,128)S(1)} %copy-done, f32[8,256]{1,0:T(8,128)S(1)} %copy-done.1, bf16[8,256,256]{2,1,0:T(8,128)(2,1)} %self_hbm.3, ...), custom_call_target="tpu_custom_call" | custom-call | flops 33554432 | bytes 1048576 | tf_op jit(solution)/shard_map/base/pallas_call | solution.py:387
  16.6 17.0 %all-to-all-done.x_ref = bf16[128,16,256]{2,1,0:T(8,128)(2,1)S(1)} async-done(((bf16[128,16,256]{2,1,0:T(8,128)(2,1)}), bf16[128,16,256]{2,1,0:T(8,128)(2,1)S(1)}, u32[]{:S(2)}, u32[]{:S(2)}) %all-to-all-start) | async-done | bytes 1048608 | tf_op jit(solution)/shard_map/all_to_all | solution.py:400
  33.6 5.5 %owner.2 = bf16[128,40,128]{2,1,0:T(8,128)(2,1)S(1)} custom-call(s32[96]{0:T(128)S(4)} %get-tuple-element.17.rank_ref, s32[2,120]{1,0:T(2,128)S(4)} %get-tuple-element.18.at_ref, bf16[128,16,256]{2,1,0:T(8,128)(2,1)S(1)} %all-to-all-done.x_ref, bf16[8,256,256]{2,1,0:T(8,128)(2,1)S(1)} %get-tuple-element.19.kept_ref, bf16[24,256,256]{2,1,0:T(8,128)(2,1)} %near_hbm.5, ...), custom_call_target="tpu_custom_call" | custom-call | tf_op jit(solution)/shard_map/owner/pallas_call | solution.py:387
  39.1 25.8 %all_to_all.20.sums_ref = bf16[128,40,128]{2,1,0:T(8,128)(2,1)S(1)} all-to-all(bf16[128,40,128]{2,1,0:T(8,128)(2,1)S(1)} %owner.2), channel_id=1, replica_groups=mesh['clus'=32,'grp'=4] {'clus','grp'}, dimensions={0} | all-to-all | bytes 2621440 | tf_op jit(solution)/shard_map/all_to_all | solution.py:400
  64.9 2.3 %leaf.1 = (f32[8,16,256]{2,1,0:T(8,128)S(1)}, f32[8,16,256]{2,1,0:T(8,128)S(1)}, f32[3,16,128]{2,1,0:T(8,128)S(1)}, bf16[128,16,256]{2,1,0:T(8,128)(2,1)}) custom-call(s32[128]{0:T(128)S(4)} %get-tuple-element.16.leaf_ref, bf16[128,40,128]{2,1,0:T(8,128)(2,1)S(1)} %all_to_all.20.sums_ref, f32[8,16,256]{2,1,0:T(8,128)S(1)} %get-tuple-element.21.base_ref, ...), custom_call_target="tpu_custom_call" | custom-call | tf_op jit(solution)/shard_map/leaf/pallas_call | solution.py:387
  67.3 3.8 %all-to-all-start.2 = ((bf16[128,16,256]{2,1,0:T(8,128)(2,1)}), bf16[128,16,256]{2,1,0:T(8,128)(2,1)S(1)}, u32[]{:S(2)}, u32[]{:S(2)}) async-start(bf16[128,16,256]{2,1,0:T(8,128)(2,1)} %get-tuple-element.22), calls=%async_computation.2 | async-start | bytes 2097152 | tf_op jit(solution)/shard_map/all_to_all | solution.py:400
  71.1 2.4 %base.3 = (f32[8,16,256]{2,1,0:T(8,128)S(1)}, f32[2,16,128]{2,1,0:T(8,128)S(1)}, f32[8,16,256]{2,1,0:T(8,128)S(1)}, f32[17,16,128]{2,1,0:T(8,128)S(1)}) custom-call(f32[8,16,256]{2,1,0:T(8,128)S(1)} %get-tuple-element.23.field_ref.residual_ref, f32[8,256]{1,0:T(8,128)S(1)} %copy-done.1, bf16[8,256,256]{2,1,0:T(8,128)(2,1)} %self_hbm.3, ...), custom_call_target="tpu_custom_call" | custom-call | flops 33554432 | bytes 1048576 | tf_op jit(solution)/shard_map/base/pallas_call | solution.py:387
  73.5 17.1 %all-to-all-done.2.x_ref = bf16[128,16,256]{2,1,0:T(8,128)(2,1)S(1)} async-done(((bf16[128,16,256]{2,1,0:T(8,128)(2,1)}), bf16[128,16,256]{2,1,0:T(8,128)(2,1)S(1)}, u32[]{:S(2)}, u32[]{:S(2)}) %all-to-all-start.2) | async-done | bytes 1048608 | tf_op jit(solution)/shard_map/all_to_all | solution.py:400
  90.7 5.5 %owner.3 = bf16[128,40,128]{2,1,0:T(8,128)(2,1)S(1)} custom-call(s32[96]{0:T(128)S(4)} %get-tuple-element.17.rank_ref, s32[2,120]{1,0:T(2,128)S(4)} %get-tuple-element.18.at_ref, bf16[128,16,256]{2,1,0:T(8,128)(2,1)S(1)} %all-to-all-done.2.x_ref, bf16[8,256,256]{2,1,0:T(8,128)(2,1)S(1)} %get-tuple-element.19.kept_ref, bf16[24,256,256]{2,1,0:T(8,128)(2,1)} %near_hbm.5, ...), custom_call_target="tpu_custom_call" | custom-call | tf_op jit(solution)/shard_map/owner/pallas_call | solution.py:387
  96.2 25.8 %all_to_all.21.sums_ref = bf16[128,40,128]{2,1,0:T(8,128)(2,1)S(1)} all-to-all(bf16[128,40,128]{2,1,0:T(8,128)(2,1)S(1)} %owner.3), channel_id=1, replica_groups=mesh['clus'=32,'grp'=4] {'clus','grp'}, dimensions={0} | all-to-all | bytes 2621440 | tf_op jit(solution)/shard_map/all_to_all | solution.py:400
  122.0 2.5 %final.1 = (f32[8,16,256]{2,1,0:T(8,128)}, f32[8,16,256]{2,1,0:T(8,128)}) custom-call(s32[128]{0:T(128)S(4)} %get-tuple-element.16.leaf_ref, bf16[128,40,128]{2,1,0:T(8,128)(2,1)S(1)} %all_to_all.21.sums_ref, f32[8,16,256]{2,1,0:T(8,128)S(1)} %get-tuple-element.26.base_ref, f32[8,16,256]{2,1,0:T(8,128)S(1)} %copy-done, ...), custom_call_target="tpu_custom_call" | custom-call | tf_op jit(solution)/shard_map/final/pallas_call | solution.py:387
Async XLA Ops:
  2.6 11.5 %copy-start = (f32[8,16,256]{2,1,0:T(8,128)S(1)}, f32[8,16,256]{2,1,0:T(8,128)}, u32[]{:S(2)}) copy-start(f32[8,16,256]{2,1,0:T(8,128)} %field_ref.5) | copy-start | bytes 393220
  2.6 11.5 %copy-start.1 = (f32[8,256]{1,0:T(8,128)S(1)}, f32[8,256]{1,0:T(8,128)}, u32[]{:S(2)}) copy-start(f32[8,256]{1,0:T(8,128)} %shift_ref.3) | copy-start | bytes 24580
  2.7 30.9 %all-to-all-start = ((bf16[128,16,256]{2,1,0:T(8,128)(2,1)}), bf16[128,16,256]{2,1,0:T(8,128)(2,1)S(1)}, u32[]{:S(2)}, u32[]{:S(2)}) async-start(bf16[128,16,256]{2,1,0:T(8,128)(2,1)} %send.1), calls=%async_computation | async-start | bytes 2097152 | tf_op jit(solution)/shard_map/all_to_all | solution.py:400
  67.3 23.4 %all-to-all-start.2 = ((bf16[128,16,256]{2,1,0:T(8,128)(2,1)}), bf16[128,16,256]{2,1,0:T(8,128)(2,1)S(1)}, u32[]{:S(2)}, u32[]{:S(2)}) async-start(bf16[128,16,256]{2,1,0:T(8,128)(2,1)} %get-tuple-element.22), calls=%async_computation.2 | async-start | bytes 2097152 | tf_op jit(solution)/shard_map/all_to_all | solution.py:400

commit v5 on v4

--- a/solution.py
+++ b/solution.py
@@ -7,6 +7,7 @@
 
 AXES = ("clus", "grp")
 KEPT_NEAR = 8
+QUARTERS = 4
 HIGHEST = lax.Precision.HIGHEST
 NT = (((1,), (1,)), ((), ()))
 F32 = jnp.float32
@@ -222,13 +223,25 @@
     near = kept + streamed
     slots = x_ref.shape[0]
     far = left_ref.shape[0]
-    copies = [
-        pltpu.make_async_copy(near_hbm.at[pl.ds(kept, streamed)], near_ref, sems.at[0]),
-        pltpu.make_async_copy(left_hbm, left_ref, sems.at[1]),
-        pltpu.make_async_copy(right_hbm, right_ref, sems.at[2]),
-    ]
-    for copy in copies:
-        copy.start()
+    near_step = streamed // QUARTERS
+    far_step = far // QUARTERS
+    copies = []
+    for quarter in range(QUARTERS):
+        near_from = quarter * near_step
+        far_here = pl.ds(quarter * far_step, far_step)
+        copies.append(
+            [
+                pltpu.make_async_copy(
+                    near_hbm.at[pl.ds(kept + near_from, near_step)],
+                    near_ref.at[pl.ds(near_from, near_step)],
+                    sems.at[quarter, 0],
+                ),
+                pltpu.make_async_copy(left_hbm.at[far_here], left_ref.at[far_here], sems.at[quarter, 1]),
+                pltpu.make_async_copy(right_hbm.at[far_here], right_ref.at[far_here], sems.at[quarter, 2]),
+            ]
+        )
+        for copy in copies[quarter]:
+            copy.start()
 
     def clear(at, carry):
         acc_ref[pl.ds(at * 8, 8)] = jnp.zeros((8, 16, 256), F32)
@@ -236,23 +249,16 @@
 
     lax.fori_loop(0, slots // 8, clear, 0)
 
-    def near_part(block_ref, shift):
+    def near_sums(block_ref, first, count, shift):
         sums = []
-        for which in range(block_ref.shape[0]):
+        for which in range(first, first + count):
             row, col = at_ref[0, shift + which], at_ref[1, shift + which]
             block = block_ref[which]
             sums.append(
                 (row, lax.dot_general(x_ref[col], block, NT, preferred_element_type=F32))
             )
             sums.append((col, jnp.dot(x_ref[row], block, preferred_element_type=F32)))
-        for slot, value in sums:
-            acc_ref[slot] += value
-
-    near_part(kept_ref, 0)
-    copies[0].wait()
-    near_part(near_ref, kept)
-    for copy in copies[1:]:
-        copy.wait()
+        return sums
 
     lane = iota((16, 256), 1)
 
@@ -276,21 +282,28 @@
         left_proj = jnp.where(kept, left_proj, 0.0).astype(BF16)
         return rows, cols, left, right, right_proj, left_proj
 
-    def far_some(at, carry):
+    def far_sums(first, count):
         sums = []
         for rows, cols, left, right, right_proj, left_proj in [
-            far_project(at * 48 + 8 * group) for group in range(6)
+            far_project(first + at) for at in range(0, count, 8)
         ]:
             to_row = jnp.dot(right_proj, left, preferred_element_type=F32)
             to_col = jnp.dot(left_proj, right, preferred_element_type=F32)
             for part in range(8):
                 sums.append((rows[part], to_row[16 * part : 16 * part + 16]))
                 sums.append((cols[part], to_col[16 * part : 16 * part + 16]))
+        return sums
+
+    def add(sums):
         for slot, value in sums:
             acc_ref[slot] += value
-        return carry
-
-    lax.fori_loop(0, far // 48, far_some, 0)
+
+    add(near_sums(kept_ref, 0, kept, 0))
+    for quarter in range(QUARTERS):
+        for copy in copies[quarter]:
+            copy.wait()
+        sums = far_sums(quarter * far_step, far_step)
+        add(sums + near_sums(near_ref, quarter * near_step, near_step, kept))
 
     products = jnp.zeros((128, 128), F32)
     for at in range(slots // 8):
@@ -313,28 +326,34 @@
     lax.fori_loop(0, slots // 8, attach, 0)
 
 
-def add_returned(leaf_ref, sums_ref, acc_ref):
+def add_returned(leaf_ref, sums_ref, accs):
     def some(at, tiles):
-        for part in range(8):
-            owner = at * 8 + part
+        for part in range(16):
+            owner = at * 16 + part
             leaf = leaf_ref[owner]
+            acc_ref = accs[part % len(accs)]
             acc_ref[leaf, :, 0:128] += sums_ref[owner, 0:16, :].astype(F32)
             acc_ref[leaf, :, 128:256] += sums_ref[owner, 16:32, :].astype(F32)
             tiles = tiles + sums_ref[owner, 32:40, :].astype(F32)
         return tiles
 
-    return lax.fori_loop(0, sums_ref.shape[0] // 8, some, jnp.zeros((8, 128), F32))
+    for acc_ref in accs[1:]:
+        acc_ref[...] = jnp.zeros(acc_ref.shape, F32)
+    tiles = lax.fori_loop(0, sums_ref.shape[0] // 16, some, jnp.zeros((8, 128), F32))
+    return tiles, (accs[0][...] + accs[1][...]) + (accs[2][...] + accs[3][...])
 
 
 def leaf_kernel(
     leaf_ref, sums_ref, base_ref, field_ref,
     residual_ref, image_ref, small_ref, message_ref,
-    half_ref, stage_ref, sems,
+    half_ref, stage_ref, acc_a, acc_b, acc_c, sems,
 ):
     image_ref[...] = base_ref[...]
-    curve, norm = unpack(add_returned(leaf_ref, sums_ref, image_ref))
+    tiles, image = add_returned(leaf_ref, sums_ref, (image_ref, acc_a, acc_b, acc_c))
+    curve, norm = unpack(tiles)
     step = solve(curve, norm)
-    image = image_ref[...].reshape(128, 256)
+    image_ref[...] = image
+    image = image.reshape(128, 256)
     residual = field_ref[...].reshape(128, 256) - combine(image, kron_rows(step))
     half_ref[...] = residual.reshape(residual_ref.shape).astype(BF16)
     copies = fill(leaf_ref, half_ref, stage_ref, message_ref, sems)
@@ -348,10 +367,11 @@
 
 def final_kernel(
     leaf_ref, sums_ref, base_ref, field_ref, residual_ref, image_ref, small_ref, part_ref, steps_ref,
-    solution_ref, out_ref, acc_ref,
+    solution_ref, out_ref, acc_ref, acc_a, acc_b, acc_c,
 ):
     acc_ref[...] = base_ref[...]
-    curve, next_norm = unpack(add_returned(leaf_ref, sums_ref, acc_ref))
+    tiles, returned = add_returned(leaf_ref, sums_ref, (acc_ref, acc_a, acc_b, acc_c))
+    curve, next_norm = unpack(tiles)
     steps = [(steps_ref[step], steps_ref[16, step : step + 1]) for step in range(16)]
     coef = apply_factor(steps, next_norm)
     moved = product(columns(small_ref[0]), coef)
@@ -361,7 +381,7 @@
     kron_coef = kron_rows(coef)
     residual = residual_ref[...].reshape(128, 256)
     direction = residual + combine(field_ref[...].reshape(128, 256), kron_coef)
-    image = acc_ref[...].reshape(128, 256) + combine(
+    image = returned.reshape(128, 256) + combine(
         image_ref[...].reshape(128, 256), kron_coef
     )
     kron_step = kron_rows(step)
@@ -466,7 +486,7 @@
             pltpu.VMEM(far_left.shape, BF16),
             pltpu.VMEM(far_right.shape, BF16),
             pltpu.VMEM(message, F32),
-            pltpu.SemaphoreType.DMA((3,)),
+            pltpu.SemaphoreType.DMA((QUARTERS, 3)),
         ],
     )
     leaf = call(
@@ -481,6 +501,9 @@
         [
             pltpu.VMEM(whole, BF16),
             pltpu.VMEM(message, BF16),
+            pltpu.VMEM(whole, F32),
+            pltpu.VMEM(whole, F32),
+            pltpu.VMEM(whole, F32),
             pltpu.SemaphoreType.DMA((4,)),
         ],
     )
@@ -488,7 +511,7 @@
         final_kernel,
         [TABLE, VMEM, KEPT, VMEM, KEPT, KEPT, KEPT, KEPT, KEPT],
         [jax.ShapeDtypeStruct(whole, F32), jax.ShapeDtypeStruct(whole, F32)],
-        [pltpu.VMEM(whole, F32)],
+        [pltpu.VMEM(whole, F32)] * 4,
     )
 
     with jax.named_scope("send"):

time: 125 us -> 124 us (level)
  no operation moved by 1% of the time
where the time goes in v5:
time: 124 us
  blocking collectives  51.6 us (42%)
  waiting for transfers between devices  34.2 us (28%)
  Pallas kernels  21.7 us (18%)
  starting transfers between devices  15.3 us (12%)
    all_to_all x2, blocking collectives, swap(): return lax.all_to_all(values, AXES, split_axis=0, concat_axis=0, tiled=True)  51.6 us
    all_to_all x2, waiting for transfers between devices, swap(): return lax.all_to_all(values, AXES, split_axis=0, concat_axis=0, tiled=True)  34.2 us
    pallas_call x7, Pallas kernels, placed(): run(*(pltpu.with_memory_space_constraint(value, spec.memory_space) if spe...  21.7 us
    all_to_all x2, starting transfers between devices, swap(): return lax.all_to_all(values, AXES, split_axis=0, concat_axis=0, tiled=True)  15.3 us
  transfers between devices with their start and end apart: 2, of which 2 were waited for; matrix products, arithmetic and copies ran while one was open for 0% of the time, Pallas kernels for 4%

profile of v5, /device:TPU:1, one launch (start us, length us, event | category | flops | bytes accessed | tf_op | source)
XLA Modules:
  0.0 123.6 jit_solution(2454074091053361357)
XLA Ops:
  0.6 2.0 %send.1 = bf16[128,16,256]{2,1,0:T(8,128)(2,1)} custom-call(s32[128]{0:T(128)} %bitcast.1, f32[8,16,256]{2,1,0:T(8,128)} %field_ref.5), custom_call_target="tpu_custom_call" | custom-call | tf_op jit(solution)/shard_map/send/pallas_call | solution.py:407
  2.6 0.0 copy-start
  2.6 0.0 copy-start.1
  2.7 11.5 %all-to-all-start = ((bf16[128,16,256]{2,1,0:T(8,128)(2,1)}), bf16[128,16,256]{2,1,0:T(8,128)(2,1)S(1)}, u32[]{:S(2)}, u32[]{:S(2)}) async-start(bf16[128,16,256]{2,1,0:T(8,128)(2,1)} %send.1), calls=%async_computation | async-start | bytes 2097152 | tf_op jit(solution)/shard_map/all_to_all | solution.py:420
  14.2 0.0 copy-done
  14.2 0.0 copy-done.1
  14.2 2.4 %base.2 = (f32[8,16,256]{2,1,0:T(8,128)S(1)}, f32[2,16,128]{2,1,0:T(8,128)S(1)}, bf16[8,256,256]{2,1,0:T(8,128)(2,1)S(1)}, s32[128]{0:T(128)S(4)}, s32[96]{0:T(128)S(4)}, /*index=5*/s32[2,120]{1,0:T(2,128)S(4)}) custom-call(f32[8,16,256]{2,1,0:T(8,128)S(1)} %copy-done, f32[8,256]{1,0:T(8,128)S(1)} %copy-done.1, bf16[8,256,256]{2,1,0:T(8,128)(2,1)} %self_hbm.3, ...), custom_call_target="tpu_custom_call" | custom-call | flops 33554432 | bytes 1048576 | tf_op jit(solution)/shard_map/base/pallas_call | solution.py:407
  16.6 17.0 %all-to-all-done.x_ref = bf16[128,16,256]{2,1,0:T(8,128)(2,1)S(1)} async-done(((bf16[128,16,256]{2,1,0:T(8,128)(2,1)}), bf16[128,16,256]{2,1,0:T(8,128)(2,1)S(1)}, u32[]{:S(2)}, u32[]{:S(2)}) %all-to-all-start) | async-done | bytes 1048608 | tf_op jit(solution)/shard_map/all_to_all | solution.py:420
  33.6 5.3 %owner.2 = bf16[128,40,128]{2,1,0:T(8,128)(2,1)S(1)} custom-call(s32[96]{0:T(128)S(4)} %get-tuple-element.17.rank_ref, s32[2,120]{1,0:T(2,128)S(4)} %get-tuple-element.18.at_ref, bf16[128,16,256]{2,1,0:T(8,128)(2,1)S(1)} %all-to-all-done.x_ref, bf16[8,256,256]{2,1,0:T(8,128)(2,1)S(1)} %get-tuple-element.19.kept_ref, bf16[24,256,256]{2,1,0:T(8,128)(2,1)} %near_hbm.5, ...), custom_call_target="tpu_custom_call" | custom-call | tf_op jit(solution)/shard_map/owner/pallas_call | solution.py:407
  38.9 25.8 %all_to_all.20.sums_ref = bf16[128,40,128]{2,1,0:T(8,128)(2,1)S(1)} all-to-all(bf16[128,40,128]{2,1,0:T(8,128)(2,1)S(1)} %owner.2), channel_id=1, replica_groups=mesh['clus'=32,'grp'=4] {'clus','grp'}, dimensions={0} | all-to-all | bytes 2621440 | tf_op jit(solution)/shard_map/all_to_all | solution.py:420
  64.7 2.0 %leaf.1 = (f32[8,16,256]{2,1,0:T(8,128)S(1)}, f32[8,16,256]{2,1,0:T(8,128)S(1)}, f32[3,16,128]{2,1,0:T(8,128)S(1)}, bf16[128,16,256]{2,1,0:T(8,128)(2,1)}) custom-call(s32[128]{0:T(128)S(4)} %get-tuple-element.16.leaf_ref, bf16[128,40,128]{2,1,0:T(8,128)(2,1)S(1)} %all_to_all.20.sums_ref, f32[8,16,256]{2,1,0:T(8,128)S(1)} %get-tuple-element.21.base_ref, ...), custom_call_target="tpu_custom_call" | custom-call | tf_op jit(solution)/shard_map/leaf/pallas_call | solution.py:407
  66.7 3.8 %all-to-all-start.2 = ((bf16[128,16,256]{2,1,0:T(8,128)(2,1)}), bf16[128,16,256]{2,1,0:T(8,128)(2,1)S(1)}, u32[]{:S(2)}, u32[]{:S(2)}) async-start(bf16[128,16,256]{2,1,0:T(8,128)(2,1)} %get-tuple-element.22), calls=%async_computation.2 | async-start | bytes 2097152 | tf_op jit(solution)/shard_map/all_to_all | solution.py:420
  70.6 2.4 %base.3 = (f32[8,16,256]{2,1,0:T(8,128)S(1)}, f32[2,16,128]{2,1,0:T(8,128)S(1)}, f32[8,16,256]{2,1,0:T(8,128)S(1)}, f32[17,16,128]{2,1,0:T(8,128)S(1)}) custom-call(f32[8,16,256]{2,1,0:T(8,128)S(1)} %get-tuple-element.23.field_ref.residual_ref, f32[8,256]{1,0:T(8,128)S(1)} %copy-done.1, bf16[8,256,256]{2,1,0:T(8,128)(2,1)} %self_hbm.3, ...), custom_call_target="tpu_custom_call" | custom-call | flops 33554432 | bytes 1048576 | tf_op jit(solution)/shard_map/base/pallas_call | solution.py:407
  73.0 17.1 %all-to-all-done.2.x_ref = bf16[128,16,256]{2,1,0:T(8,128)(2,1)S(1)} async-done(((bf16[128,16,256]{2,1,0:T(8,128)(2,1)}), bf16[128,16,256]{2,1,0:T(8,128)(2,1)S(1)}, u32[]{:S(2)}, u32[]{:S(2)}) %all-to-all-start.2) | async-done | bytes 1048608 | tf_op jit(solution)/shard_map/all_to_all | solution.py:420
  90.1 5.3 %owner.3 = bf16[128,40,128]{2,1,0:T(8,128)(2,1)S(1)} custom-call(s32[96]{0:T(128)S(4)} %get-tuple-element.17.rank_ref, s32[2,120]{1,0:T(2,128)S(4)} %get-tuple-element.18.at_ref, bf16[128,16,256]{2,1,0:T(8,128)(2,1)S(1)} %all-to-all-done.2.x_ref, bf16[8,256,256]{2,1,0:T(8,128)(2,1)S(1)} %get-tuple-element.19.kept_ref, bf16[24,256,256]{2,1,0:T(8,128)(2,1)} %near_hbm.5, ...), custom_call_target="tpu_custom_call" | custom-call | tf_op jit(solution)/shard_map/owner/pallas_call | solution.py:407
  95.5 25.8 %all_to_all.21.sums_ref = bf16[128,40,128]{2,1,0:T(8,128)(2,1)S(1)} all-to-all(bf16[128,40,128]{2,1,0:T(8,128)(2,1)S(1)} %owner.3), channel_id=1, replica_groups=mesh['clus'=32,'grp'=4] {'clus','grp'}, dimensions={0} | all-to-all | bytes 2621440 | tf_op jit(solution)/shard_map/all_to_all | solution.py:420
  121.3 2.3 %final.1 = (f32[8,16,256]{2,1,0:T(8,128)}, f32[8,16,256]{2,1,0:T(8,128)}) custom-call(s32[128]{0:T(128)S(4)} %get-tuple-element.16.leaf_ref, bf16[128,40,128]{2,1,0:T(8,128)(2,1)S(1)} %all_to_all.21.sums_ref, f32[8,16,256]{2,1,0:T(8,128)S(1)} %get-tuple-element.26.base_ref, f32[8,16,256]{2,1,0:T(8,128)S(1)} %copy-done, ...), custom_call_target="tpu_custom_call" | custom-call | tf_op jit(solution)/shard_map/final/pallas_call | solution.py:407
Async XLA Ops:
  2.6 11.5 %copy-start = (f32[8,16,256]{2,1,0:T(8,128)S(1)}, f32[8,16,256]{2,1,0:T(8,128)}, u32[]{:S(2)}) copy-start(f32[8,16,256]{2,1,0:T(8,128)} %field_ref.5) | copy-start | bytes 393220
  2.6 11.5 %copy-start.1 = (f32[8,256]{1,0:T(8,128)S(1)}, f32[8,256]{1,0:T(8,128)}, u32[]{:S(2)}) copy-start(f32[8,256]{1,0:T(8,128)} %shift_ref.3) | copy-start | bytes 24580
  2.7 30.9 %all-to-all-start = ((bf16[128,16,256]{2,1,0:T(8,128)(2,1)}), bf16[128,16,256]{2,1,0:T(8,128)(2,1)S(1)}, u32[]{:S(2)}, u32[]{:S(2)}) async-start(bf16[128,16,256]{2,1,0:T(8,128)(2,1)} %send.1), calls=%async_computation | async-start | bytes 2097152 | tf_op jit(solution)/shard_map/all_to_all | solution.py:420
  66.7 23.4 %all-to-all-start.2 = ((bf16[128,16,256]{2,1,0:T(8,128)(2,1)}), bf16[128,16,256]{2,1,0:T(8,128)(2,1)S(1)}, u32[]{:S(2)}, u32[]{:S(2)}) async-start(bf16[128,16,256]{2,1,0:T(8,128)(2,1)} %get-tuple-element.22), calls=%async_computation.2 | async-start | bytes 2097152 | tf_op jit(solution)/shard_map/all_to_all | solution.py:420

commit v6 on v5

v6 whole, which is shorter than its diff:
```python
import jax
import jax.numpy as jnp
from jax import lax
from jax.experimental import pallas as pl
from jax.experimental.pallas import tpu as pltpu
from jax.sharding import PartitionSpec as P

AXES = ("clus", "grp")
KEPT_NEAR = 16
QUARTERS = 4
HIGHEST = lax.Precision.HIGHEST
NT = (((1,), (1,)), ((), ()))
F32 = jnp.float32
BF16 = jnp.bfloat16

VMEM = pl.BlockSpec(memory_space=pltpu.VMEM)
HBM = pl.BlockSpec(memory_space=pltpu.HBM)
KEPT = pl.BlockSpec(memory_space=pltpu.VMEM)
TABLE = pl.BlockSpec(memory_space=pltpu.SMEM)


def iota(shape, dim):
    return lax.broadcasted_iota(jnp.int32, shape, dim)


def spread(values):
    values = values + pltpu.roll(values, 64, 1)
    values = values + pltpu.roll(values, 32, 1)
    return values + pltpu.roll(values, 16, 1)


def block_mask():
    return iota((128, 128), 0) // 16 == iota((128, 128), 1) // 16


def fold(products):
    kept = jnp.where(block_mask(), products, 0.0)
    total = kept[0:16]
    for part in range(1, 8):
        total = total + kept[16 * part : 16 * part + 16]
    return spread(total)


def kron_rows(coefs):
    tiled = jnp.concatenate([coefs] * 8, axis=0)
    return jnp.where(block_mask(), tiled, 0.0).T


def combine(field, kron):
    return jnp.dot(kron, field, precision=HIGHEST, preferred_element_type=F32)


def gram(left, right):
    return fold(lax.dot_general(left, right, NT, precision=HIGHEST, preferred_element_type=F32))


def columns(matrix):
    return [jnp.broadcast_to(matrix[:, at : at + 1], (16, 128)) for at in range(16)]


def factor(parts):
    row_at = iota((16, 128), 0)
    left = list(parts)
    steps = []
    for step in range(16):
        column = left[step]
        pivot = column[step : step + 1]
        scale = jnp.where(pivot > 0, 1.0 / pivot, jnp.nan)
        steps.append((column, scale))
        for later in range(step + 1, 16):
            scaled = left[later][step : step + 1] * scale
            left[later] = jnp.where(row_at == step, scaled, left[later] - column * scaled)
    return steps


def apply_factor(steps, target):
    row_at = iota((16, 128), 0)
    for step, (column, scale) in enumerate(steps):
        scaled = target[step : step + 1] * scale
        target = jnp.where(row_at == step, scaled, target - column * scaled)
    return target


def solve(parts, target):
    return apply_factor(factor(parts), target)


def product(left, right):
    total = left[0] * right[0:1]
    for at in range(1, 16):
        total = total + left[at] * right[at : at + 1]
    return total


def pack(first, second):
    group = iota((8, 128), 1) // 16
    tile = jnp.zeros((8, 128), F32)
    at = 0
    for matrix in (first, second):
        high = matrix.astype(BF16).astype(F32)
        low = matrix - high
        for piece in (high, low):
            for half in (piece[0:8], piece[8:16]):
                tile = jnp.where(group == at, half, tile)
                at += 1
    return tile.astype(BF16)


def unpack(tile):
    group = iota((8, 128), 1) // 16
    joined = tile + pltpu.roll(tile, 128 - 32, 1)
    first = [
        jnp.concatenate(
            [
                jnp.broadcast_to(joined[:, at : at + 1], (8, 128)),
                jnp.broadcast_to(joined[:, 16 + at : 17 + at], (8, 128)),
            ],
            axis=0,
        )
        for at in range(16)
    ]
    halves = [spread(jnp.where(group == at, joined, 0.0)) for at in (4, 5)]
    return first, jnp.concatenate(halves, axis=0)


def from_columns(parts):
    group = iota((16, 128), 1) % 16
    matrix = parts[0]
    for at in range(1, 16):
        matrix = jnp.where(group == at, parts[at], matrix)
    return matrix


def fill(leaf_ref, half_ref, message_ref):
    def some(at, carry):
        for inner in range(16):
            owner = at * 16 + inner
            message_ref[owner] = half_ref[leaf_ref[owner]]
        return carry

    lax.fori_loop(0, message_ref.shape[0] // 16, some, 0)


def send_kernel(
    leaf_hbm, rank_hbm, at_hbm, field_hbm, near_hbm,
    message_ref, leaf_ref, rank_ref, at_ref, kept_ref, field_ref, half_ref, sems,
):
    copies = [
        pltpu.make_async_copy(field_hbm, field_ref, sems.at[0]),
        pltpu.make_async_copy(leaf_hbm, leaf_ref, sems.at[1]),
        pltpu.make_async_copy(rank_hbm, rank_ref, sems.at[2]),
        pltpu.make_async_copy(at_hbm, at_ref, sems.at[3]),
        pltpu.make_async_copy(near_hbm.at[pl.ds(0, kept_ref.shape[0])], kept_ref, sems.at[4]),
    ]
    for copy in copies:
        copy.start()
    copies[0].wait()
    half_ref[...] = field_ref[...].astype(BF16)
    copies[1].wait()
    fill(leaf_ref, half_ref, message_ref)
    for copy in copies[2:]:
        copy.wait()


def local_product(field_ref, shift_ref, self_ref, base_ref):
    for leaf in range(field_ref.shape[0]):
        field = field_ref[leaf]
        half = field.astype(BF16)
        block = self_ref[leaf]
        total = shift_ref[leaf : leaf + 1, :] * field
        total = total + lax.dot_general(half, block, NT, preferred_element_type=F32)
        base_ref[leaf] = total + jnp.dot(half, block, preferred_element_type=F32)


def first_owner_kernel(
    rank_ref, at_ref, x_ref, kept_ref, near_hbm, left_hbm, right_hbm, self_hbm, field_ref, shift_ref,
    out_ref, base_ref, near_ref, left_ref, right_ref, self_ref, acc_ref, sems,
):
    kept = kept_ref.shape[0]
    near_step = near_ref.shape[0] // QUARTERS
    far_step = left_ref.shape[0] // QUARTERS
    copies = []
    for quarter in range(QUARTERS):
        near_from = quarter * near_step
        far_here = pl.ds(quarter * far_step, far_step)
        copies.append(
            [
                pltpu.make_async_copy(
                    near_hbm.at[pl.ds(kept + near_from, near_step)],
                    near_ref.at[pl.ds(near_from, near_step)],
                    sems.at[quarter, 0],
                ),
                pltpu.make_async_copy(left_hbm.at[far_here], left_ref.at[far_here], sems.at[quarter, 1]),
                pltpu.make_async_copy(right_hbm.at[far_here], right_ref.at[far_here], sems.at[quarter, 2]),
            ]
        )
        for copy in copies[quarter]:
            copy.start()
    self_copy = pltpu.make_async_copy(self_hbm, self_ref, sems.at[0, 3])
    self_copy.start()
    products = Products(rank_ref, at_ref, x_ref, left_ref, right_ref, kept + near_ref.shape[0], acc_ref)
    products.clear()
    products.add(products.near(kept_ref, 0, kept, 0))
    for quarter in range(QUARTERS):
        for copy in copies[quarter]:
            copy.wait()
        sums = products.far(quarter * far_step, far_step)
        products.add(sums + products.near(near_ref, quarter * near_step, near_step, kept))
    self_copy.wait()
    local_product(field_ref, shift_ref, self_ref, base_ref)
    finish(x_ref, acc_ref, field_ref, base_ref, out_ref)


def next_owner_kernel(
    rank_ref, at_ref, x_ref, near_ref, left_ref, right_ref, self_ref, field_ref, shift_ref, old_ref,
    out_ref, base_ref, steps_ref, acc_ref,
):
    near = near_ref.shape[0]
    near_step = near // QUARTERS
    far_step = left_ref.shape[0] // QUARTERS
    products = Products(rank_ref, at_ref, x_ref, left_ref, right_ref, near, acc_ref)
    products.clear()

    def some(quarter, carry):
        sums = products.far(quarter * far_step, far_step)
        products.add(sums + products.near(near_ref, quarter * near_step, near_step, 0))
        return carry

    lax.fori_loop(0, QUARTERS, some, 0)
    local_product(field_ref, shift_ref, self_ref, base_ref)
    for step, (column, scale) in enumerate(factor(columns(old_ref[1]))):
        steps_ref[step] = column
        steps_ref[16, step : step + 1] = scale
    finish(x_ref, acc_ref, field_ref, base_ref, out_ref)


class Products:
    def __init__(self, rank_ref, at_ref, x_ref, left_ref, right_ref, near_count, acc_ref):
        self.rank_ref = rank_ref
        self.at_ref = at_ref
        self.x_ref = x_ref
        self.left_ref = left_ref
        self.right_ref = right_ref
        self.near_count = near_count
        self.acc_ref = acc_ref

    def clear(self):
        def some(at, carry):
            self.acc_ref[pl.ds(at * 8, 8)] = jnp.zeros((8, 16, 256), F32)
            return carry

        lax.fori_loop(0, self.acc_ref.shape[0] // 8, some, 0)

    def add(self, sums):
        for slot, value in sums:
            self.acc_ref[slot] += value

    def near(self, block_ref, first, count, shift):
        sums = []
        for part in range(count):
            which = first + part
            row, col = self.at_ref[0, shift + which], self.at_ref[1, shift + which]
            block = block_ref[which]
            sums.append(
                (row, lax.dot_general(self.x_ref[col], block, NT, preferred_element_type=F32))
            )
            sums.append((col, jnp.dot(self.x_ref[row], block, preferred_element_type=F32)))
        return sums

    def project(self, first):
        lane = iota((16, 256), 1)
        left = self.left_ref[pl.ds(first, 8)].reshape(256, 256)
        right = self.right_ref[pl.ds(first, 8)].reshape(256, 256)
        rows = [self.at_ref[0, self.near_count + first + part] for part in range(8)]
        cols = [self.at_ref[1, self.near_count + first + part] for part in range(8)]
        x_row = jnp.concatenate([self.x_ref[slot] for slot in rows], axis=0)
        x_col = jnp.concatenate([self.x_ref[slot] for slot in cols], axis=0)
        kept = jnp.concatenate(
            [
                (lane >= 32 * part) & (lane < 32 * part + self.rank_ref[first + part])
                for part in range(8)
            ],
            axis=0,
        )
        right_proj = lax.dot_general(x_col, right, NT, preferred_element_type=F32)
        left_proj = lax.dot_general(x_row, left, NT, preferred_element_type=F32)
        right_proj = jnp.where(kept, right_proj, 0.0).astype(BF16)
        left_proj = jnp.where(kept, left_proj, 0.0).astype(BF16)
        return rows, cols, left, right, right_proj, left_proj

    def far(self, first, count):
        sums = []
        for rows, cols, left, right, right_proj, left_proj in [
            self.project(first + at) for at in range(0, count, 8)
        ]:
            to_row = jnp.dot(right_proj, left, preferred_element_type=F32)
            to_col = jnp.dot(left_proj, right, preferred_element_type=F32)
            for part in range(8):
                sums.append((rows[part], to_row[16 * part : 16 * part + 16]))
                sums.append((cols[part], to_col[16 * part : 16 * part + 16]))
        return sums


def finish(x_ref, acc_ref, field_ref, base_ref, out_ref):
    slots = x_ref.shape[0]
    fields = field_ref[...].reshape(128, 256)
    curve = gram(fields, base_ref[...].reshape(128, 256))
    norm = gram(fields, fields)
    products = jnp.zeros((128, 128), F32)
    for at in range(slots // 16):
        here = slice(at * 16, at * 16 + 16)
        sums = acc_ref[here].astype(BF16)
        out_ref[here, 0:16, :] = sums[:, :, 0:128]
        out_ref[here, 16:32, :] = sums[:, :, 128:256]
        pair = lax.dot_general(
            x_ref[here].reshape(256, 256),
            sums.reshape(256, 256),
            NT,
            preferred_element_type=F32,
        )
        products = products + (pair[0:128, 0:128] + pair[128:256, 128:256])
    tile = pack(fold(products) + curve, norm)

    def attach(at, carry):
        out_ref[pl.ds(at * 8, 8), 32:40, :] = jnp.broadcast_to(tile[None], (8, 8, 128))
        return carry

    lax.fori_loop(0, slots // 8, attach, 0)


def add_returned(leaf_ref, sums_ref, accs):
    def some(at, tiles):
        for part in range(16):
            owner = at * 16 + part
            leaf = leaf_ref[owner]
            acc_ref = accs[part % len(accs)]
            acc_ref[leaf, :, 0:128] += sums_ref[owner, 0:16, :].astype(F32)
            acc_ref[leaf, :, 128:256] += sums_ref[owner, 16:32, :].astype(F32)
            tiles = tiles + sums_ref[owner, 32:40, :].astype(F32)
        return tiles

    for acc_ref in accs[1:]:
        acc_ref[...] = jnp.zeros(acc_ref.shape, F32)
    tiles = lax.fori_loop(0, sums_ref.shape[0] // 16, some, jnp.zeros((8, 128), F32))
    return tiles, (accs[0][...] + accs[1][...]) + (accs[2][...] + accs[3][...])


def leaf_kernel(
    leaf_ref, sums_ref, base_ref, field_ref,
    residual_ref, image_ref, small_ref, message_ref,
    half_ref, acc_a, acc_b, acc_c,
):
    image_ref[...] = base_ref[...]
    tiles, image = add_returned(leaf_ref, sums_ref, (image_ref, acc_a, acc_b, acc_c))
    curve, norm = unpack(tiles)
    step = solve(curve, norm)
    image_ref[...] = image
    image = image.reshape(128, 256)
    residual = field_ref[...].reshape(128, 256) - combine(image, kron_rows(step))
    half_ref[...] = residual.reshape(residual_ref.shape).astype(BF16)
    fill(leaf_ref, half_ref, message_ref)
    residual_ref[...] = residual.reshape(residual_ref.shape)
    small_ref[0] = from_columns(curve)
    small_ref[1] = norm
    small_ref[2] = step


def final_kernel(
    leaf_ref, sums_ref, base_ref, field_ref, residual_ref, image_ref, small_ref, steps_ref,
    solution_ref, out_ref, acc_ref, acc_a, acc_b, acc_c,
):
    acc_ref[...] = base_ref[...]
    tiles, returned = add_returned(leaf_ref, sums_ref, (acc_ref, acc_a, acc_b, acc_c))
    curve, next_norm = unpack(tiles)
    steps = [(steps_ref[step], steps_ref[16, step : step + 1]) for step in range(16)]
    coef = apply_factor(steps, next_norm)
    moved = product(columns(small_ref[0]), coef)
    moved = product(columns(coef.T[0:16]), moved)
    moved = columns(moved)
    step = solve([curve[at] - moved[at] for at in range(16)], next_norm)
    kron_coef = kron_rows(coef)
    part = combine(field_ref[...].reshape(128, 256), kron_rows(small_ref[2]))
    residual = residual_ref[...].reshape(128, 256)
    direction = residual + combine(field_ref[...].reshape(128, 256), kron_coef)
    image = returned.reshape(128, 256) + combine(
        image_ref[...].reshape(128, 256), kron_coef
    )
    kron_step = kron_rows(step)
    answer = part + combine(direction, kron_step)
    solution_ref[...] = answer.reshape(solution_ref.shape)
    out_ref[...] = (residual - combine(image, kron_step)).reshape(out_ref.shape)


def call(kernel, ins, outs, scratch, cost=None):
    kinds = {pltpu.HBM: HBM, pltpu.SMEM: TABLE}
    spaces = [kinds.get(getattr(out, "memory_space", None), VMEM) for out in outs]
    run = pl.pallas_call(
        kernel,
        out_shape=list(outs),
        in_specs=list(ins),
        out_specs=spaces,
        scratch_shapes=list(scratch),
        compiler_params=pltpu.CompilerParams(vmem_limit_bytes=24 * 1024 * 1024),
        cost_estimate=cost,
    )

    def placed(*values):
        return run(
            *(
                pltpu.with_memory_space_constraint(value, spec.memory_space)
                if spec is not VMEM
                else value
                for value, spec in zip(values, ins)
            )
        )

    return placed


def swap(values):
    return lax.all_to_all(values, AXES, split_axis=0, concat_axis=0, tiled=True)


def shards(
    right_sides,
    diag_shift,
    self_blocks,
    near_blocks,
    far_left,
    far_right,
    far_rank,
    send_leaf,
    block_pos,
):
    leaves, rhs, size = right_sides.shape
    slots = send_leaf.shape[1]
    targets = send_leaf.reshape(slots)
    whole = (leaves, rhs, size)
    message = (slots, rhs, size)
    tables = [
        pltpu.SMEM((slots,), jnp.int32),
        pltpu.SMEM(far_rank.shape, jnp.int32),
        pltpu.SMEM(block_pos.shape, jnp.int32),
    ]
    send = call(
        send_kernel,
        [HBM, HBM, HBM, HBM, HBM],
        [jax.ShapeDtypeStruct(message, BF16)]
        + tables
        + [pltpu.VMEM((KEPT_NEAR, size, size), BF16)],
        [pltpu.VMEM(whole, F32), pltpu.VMEM(whole, BF16), pltpu.SemaphoreType.DMA((5,))],
    )
    owner_outs = [pltpu.VMEM((slots, 40, 128), BF16), pltpu.VMEM(whole, F32)]
    owner = call(
        first_owner_kernel,
        [TABLE, TABLE, VMEM, KEPT, HBM, HBM, HBM, HBM, VMEM, VMEM],
        owner_outs,
        [
            pltpu.VMEM((near_blocks.shape[0] - KEPT_NEAR, size, size), BF16),
            pltpu.VMEM(far_left.shape, BF16),
            pltpu.VMEM(far_right.shape, BF16),
            pltpu.VMEM(self_blocks.shape, BF16),
            pltpu.VMEM(message, F32),
            pltpu.SemaphoreType.DMA((QUARTERS, 4)),
        ],
    )
    next_owner = call(
        next_owner_kernel,
        [TABLE, TABLE] + [VMEM] * 7 + [KEPT],
        owner_outs + [pltpu.VMEM((17, rhs, 128), F32)],
        [pltpu.VMEM(message, F32)],
    )
    leaf = call(
        leaf_kernel,
        [TABLE, VMEM, KEPT, VMEM],
        [
            pltpu.VMEM(whole, F32),
            pltpu.VMEM(whole, F32),
            pltpu.VMEM((3, rhs, 128), F32),
            jax.ShapeDtypeStruct(message, BF16),
        ],
        [pltpu.VMEM(whole, BF16)] + [pltpu.VMEM(whole, F32)] * 3,
    )
    final = call(
        final_kernel,
        [TABLE, VMEM, KEPT, VMEM, KEPT, KEPT, KEPT, KEPT],
        [jax.ShapeDtypeStruct(whole, F32), jax.ShapeDtypeStruct(whole, F32)],
        [pltpu.VMEM(whole, F32)] * 4,
    )
    stored = (near_blocks, far_left, far_right, self_blocks)

    with jax.named_scope("send"):
        outgoing, leaf_table, rank_table, at_table, kept = send(
            targets, far_rank, block_pos, right_sides, near_blocks
        )
    incoming = swap(outgoing)
    with jax.named_scope("owner"):
        sums, base_image = owner(
            rank_table, at_table, incoming, kept, *stored, right_sides, diag_shift
        )
    back = swap(sums)
    with jax.named_scope("leaf"):
        residual, image, old, outgoing = leaf(leaf_table, back, base_image, right_sides)
    incoming = swap(outgoing)
    with jax.named_scope("owner"):
        sums, base_image, steps = next_owner(
            rank_table, at_table, incoming, *stored, residual, diag_shift, old
        )
    back = swap(sums)
    with jax.named_scope("final"):
        answer, residual = final(
            leaf_table, back, base_image, right_sides, residual, image, old, steps
        )
    return (answer, residual)


def solution(mesh):
    split = P(AXES, None, None)
    placed = (
        split,
        P(AXES, None),
        split,
        split,
        split,
        split,
        P(AXES),
        split,
        P(None, AXES),
    )
    return jax.shard_map(
        shards, mesh=mesh, in_specs=placed, out_specs=(split, split), check_vma=False
    )
```

time: 124 us -> 122 us (0.984)
  blocking collectives: 51.6 us -> 105 us
  waiting for transfers between devices: 34.2 us -> 0 us
  starting transfers between devices: 15.3 us -> 0 us
  Pallas kernels: 21.7 us -> 15.8 us
    all_to_all x2 -> x4, blocking collectives: 51.6 us -> 105 us  [swap(): return lax.all_to_all(values, AXES, split_axis=0, concat_axis=0, tiled=True)]
    all_to_all x2 -> x0, waiting for transfers between devices: 34.2 us -> none  [swap(): return lax.all_to_all(values, AXES, split_axis=0, concat_axis=0, tiled=True)]
    all_to_all x2 -> x0, starting transfers between devices: 15.3 us -> none  [swap(): return lax.all_to_all(values, AXES, split_axis=0, concat_axis=0, tiled=True)]
    pallas_call x7 -> x5, Pallas kernels: 21.7 us -> 15.8 us  [placed(): run(*(pltpu.with_memory_space_constraint(value, spec.memory_space) if spe...]
  transfers between devices with their start and end apart: 2 -> 0, of which waited for: 2 -> 0; matrix products, arithmetic and copies ran while one was open for 0% -> 0% of each run, Pallas kernels for 4% -> 0%
where the time goes in v6:
time: 122 us
  blocking collectives  105 us (86%)
  Pallas kernels  15.8 us (13%)
    all_to_all x4, blocking collectives, swap(): return lax.all_to_all(values, AXES, split_axis=0, concat_axis=0, tiled=True)  105 us
    pallas_call x5, Pallas kernels, placed(): run(*(pltpu.with_memory_space_constraint(value, spec.memory_space) if spe...  15.8 us

profile of v6, /device:TPU:1, one launch (start us, length us, event | category | flops | bytes accessed | tf_op | source)
XLA Modules:
  0.0 122.0 jit_solution(15930025839807168769)
XLA Ops:
  0.6 1.7 %send.1 = (bf16[128,16,256]{2,1,0:T(8,128)(2,1)S(1)}, s32[128]{0:T(128)S(4)}, s32[96]{0:T(128)S(4)}, s32[2,120]{1,0:T(2,128)S(4)}, bf16[16,256,256]{2,1,0:T(8,128)(2,1)S(1)}) custom-call(s32[128]{0:T(128)} %bitcast.1, s32[96]{0:T(128)} %rank_hbm.1, s32[2,120]{1,0:T(2,128)} %at_hbm.1, f32[8,16,256]{2,1,0:T(8,128)} %field_ref.5, bf16[24,256,256]{2,1,0:T(8,128)(2,1)} %near_ref.1), custom_call_target="tpu_custom_call" | custom-call | tf_op jit(solution)/shard_map/send/pallas_call | solution.py:408
  2.4 0.0 copy-start.4
  2.4 0.0 copy-start.5
  2.4 30.7 %all_to_all.20.x_ref = bf16[128,16,256]{2,1,0:T(8,128)(2,1)S(1)} all-to-all(bf16[128,16,256]{2,1,0:T(8,128)(2,1)S(1)} %get-tuple-element.19), channel_id=1, replica_groups=mesh['clus'=32,'grp'=4] {'clus','grp'}, dimensions={0} | all-to-all | bytes 2097152 | tf_op jit(solution)/shard_map/all_to_all | solution.py:421
  33.1 0.0 copy-done.4
  33.1 0.0 copy-done.5
  33.1 0.0 copy-start.3
  33.1 5.6 %owner.2 = (bf16[128,40,128]{2,1,0:T(8,128)(2,1)S(1)}, f32[8,16,256]{2,1,0:T(8,128)S(1)}) custom-call(s32[96]{0:T(128)S(4)} %get-tuple-element.17.rank_ref, s32[2,120]{1,0:T(2,128)S(4)} %get-tuple-element.18.at_ref, bf16[128,16,256]{2,1,0:T(8,128)(2,1)S(1)} %all_to_all.20.x_ref, bf16[16,256,256]{2,1,0:T(8,128)(2,1)S(1)} %get-tuple-element.20.kept_ref, ...), custom_call_target="tpu_custom_call" | custom-call | tf_op jit(solution)/shard_map/owner/pallas_call | solution.py:408
  38.7 0.0 copy-start.1
  38.8 0.0 copy-start.2
  38.8 25.8 %all_to_all.21.sums_ref = bf16[128,40,128]{2,1,0:T(8,128)(2,1)S(1)} all-to-all(bf16[128,40,128]{2,1,0:T(8,128)(2,1)S(1)} %get-tuple-element.21), channel_id=1, replica_groups=mesh['clus'=32,'grp'=4] {'clus','grp'}, dimensions={0} | all-to-all | bytes 2621440 | tf_op jit(solution)/shard_map/all_to_all | solution.py:421
  64.6 0.0 copy-start
  64.6 1.1 leaf.1
  65.7 23.1 %all_to_all.22.x_ref = bf16[128,16,256]{2,1,0:T(8,128)(2,1)S(1)} all-to-all(bf16[128,16,256]{2,1,0:T(8,128)(2,1)S(1)} %get-tuple-element.23), channel_id=1, replica_groups=mesh['clus'=32,'grp'=4] {'clus','grp'}, dimensions={0} | all-to-all | bytes 2097152 | tf_op jit(solution)/shard_map/all_to_all | solution.py:421
  88.8 0.0 copy-done.3
  88.8 0.0 copy-done.1
  88.8 0.0 copy-done.2
  88.8 0.0 copy-done
  88.8 5.0 %owner.3 = (bf16[128,40,128]{2,1,0:T(8,128)(2,1)S(1)}, f32[8,16,256]{2,1,0:T(8,128)S(1)}, f32[17,16,128]{2,1,0:T(8,128)S(1)}) custom-call(s32[96]{0:T(128)S(4)} %get-tuple-element.17.rank_ref, s32[2,120]{1,0:T(2,128)S(4)} %get-tuple-element.18.at_ref, bf16[128,16,256]{2,1,0:T(8,128)(2,1)S(1)} %all_to_all.22.x_ref, bf16[24,256,256]{2,1,0:T(8,128)(2,1)S(1)} %copy-done, ...), custom_call_target="tpu_custom_call" | custom-call | tf_op jit(solution)/shard_map/owner/pallas_call | solution.py:408
  93.8 25.8 %all_to_all.23.sums_ref = bf16[128,40,128]{2,1,0:T(8,128)(2,1)S(1)} all-to-all(bf16[128,40,128]{2,1,0:T(8,128)(2,1)S(1)} %get-tuple-element.26), channel_id=1, replica_groups=mesh['clus'=32,'grp'=4] {'clus','grp'}, dimensions={0} | all-to-all | bytes 2621440 | tf_op jit(solution)/shard_map/all_to_all | solution.py:421
  119.6 2.4 %final.1 = (f32[8,16,256]{2,1,0:T(8,128)}, f32[8,16,256]{2,1,0:T(8,128)}) custom-call(s32[128]{0:T(128)S(4)} %get-tuple-element.16.leaf_ref, bf16[128,40,128]{2,1,0:T(8,128)(2,1)S(1)} %all_to_all.23.sums_ref, f32[8,16,256]{2,1,0:T(8,128)S(1)} %get-tuple-element.27.base_ref, f32[8,16,256]{2,1,0:T(8,128)S(1)} %copy-done.4, ...), custom_call_target="tpu_custom_call" | custom-call | tf_op jit(solution)/shard_map/final/pallas_call | solution.py:408
Async XLA Ops:
  2.4 30.8 %copy-start.4 = (f32[8,16,256]{2,1,0:T(8,128)S(1)}, f32[8,16,256]{2,1,0:T(8,128)}, u32[]{:S(2)}) copy-start(f32[8,16,256]{2,1,0:T(8,128)} %field_ref.5) | copy-start | bytes 393220
  2.4 30.7 %copy-start.5 = (f32[8,256]{1,0:T(8,128)S(1)}, f32[8,256]{1,0:T(8,128)}, u32[]{:S(2)}) copy-start(f32[8,256]{1,0:T(8,128)} %shift_ref.3) | copy-start | bytes 24580
  33.1 55.7 %copy-start.3 = (bf16[8,256,256]{2,1,0:T(8,128)(2,1)S(1)}, bf16[8,256,256]{2,1,0:T(8,128)(2,1)}, u32[]{:S(2)}) copy-start(bf16[8,256,256]{2,1,0:T(8,128)(2,1)} %self_ref.1) | copy-start | bytes 3145732
  38.7 50.0 %copy-start.1 = (bf16[96,32,256]{2,1,0:T(8,128)(2,1)S(1)}, bf16[96,32,256]{2,1,0:T(8,128)(2,1)}, u32[]{:S(2)}) copy-start(bf16[96,32,256]{2,1,0:T(8,128)(2,1)} %left_ref.1) | copy-start | bytes 4718596
  38.8 50.0 %copy-start.2 = (bf16[96,32,256]{2,1,0:T(8,128)(2,1)S(1)}, bf16[96,32,256]{2,1,0:T(8,128)(2,1)}, u32[]{:S(2)}) copy-start(bf16[96,32,256]{2,1,0:T(8,128)(2,1)} %right_ref.1) | copy-start | bytes 4718596
  64.6 24.2 %copy-start = (bf16[24,256,256]{2,1,0:T(8,128)(2,1)S(1)}, bf16[24,256,256]{2,1,0:T(8,128)(2,1)}, u32[]{:S(2)}) copy-start(bf16[24,256,256]{2,1,0:T(8,128)(2,1)} %near_ref.1) | copy-start | bytes 9437188

commit v7 on v6

--- a/solution.py
+++ b/solution.py
@@ -6,7 +6,7 @@
 from jax.sharding import PartitionSpec as P
 
 AXES = ("clus", "grp")
-KEPT_NEAR = 16
+KEPT_NEAR = 4
 QUARTERS = 4
 HIGHEST = lax.Precision.HIGHEST
 NT = (((1,), (1,)), ((), ()))
@@ -173,40 +173,25 @@
 
 
 def first_owner_kernel(
-    rank_ref, at_ref, x_ref, kept_ref, near_hbm, left_hbm, right_hbm, self_hbm, field_ref, shift_ref,
-    out_ref, base_ref, near_ref, left_ref, right_ref, self_ref, acc_ref, sems,
+    rank_ref, at_ref, x_ref, kept_ref, near_hbm, left_ref, right_ref, self_hbm, field_ref, shift_ref,
+    out_ref, base_ref, near_ref, self_ref, acc_ref, sems,
 ):
     kept = kept_ref.shape[0]
-    near_step = near_ref.shape[0] // QUARTERS
+    kept_step = kept // QUARTERS
     far_step = left_ref.shape[0] // QUARTERS
-    copies = []
+    rest = near_ref.shape[0]
+    near_copy = pltpu.make_async_copy(near_hbm.at[pl.ds(kept, rest)], near_ref, sems.at[0])
+    self_copy = pltpu.make_async_copy(self_hbm, self_ref, sems.at[1])
+    near_copy.start()
+    self_copy.start()
+    products = Products(rank_ref, at_ref, x_ref, left_ref, right_ref, kept + rest, acc_ref)
+    products.clear()
     for quarter in range(QUARTERS):
-        near_from = quarter * near_step
-        far_here = pl.ds(quarter * far_step, far_step)
-        copies.append(
-            [
-                pltpu.make_async_copy(
-                    near_hbm.at[pl.ds(kept + near_from, near_step)],
-                    near_ref.at[pl.ds(near_from, near_step)],
-                    sems.at[quarter, 0],
-                ),
-                pltpu.make_async_copy(left_hbm.at[far_here], left_ref.at[far_here], sems.at[quarter, 1]),
-                pltpu.make_async_copy(right_hbm.at[far_here], right_ref.at[far_here], sems.at[quarter, 2]),
-            ]
-        )
-        for copy in copies[quarter]:
-            copy.start()
-    self_copy = pltpu.make_async_copy(self_hbm, self_ref, sems.at[0, 3])
-    self_copy.start()
-    products = Products(rank_ref, at_ref, x_ref, left_ref, right_ref, kept + near_ref.shape[0], acc_ref)
-    products.clear()
-    products.add(products.near(kept_ref, 0, kept, 0))
-    for quarter in range(QUARTERS):
-        for copy in copies[quarter]:
-            copy.wait()
         sums = products.far(quarter * far_step, far_step)
-        products.add(sums + products.near(near_ref, quarter * near_step, near_step, kept))
+        products.add(sums + products.near(kept_ref, quarter * kept_step, kept_step, 0))
+    near_copy.wait()
     self_copy.wait()
+    products.add(products.near(near_ref, 0, rest, kept))
     local_product(field_ref, shift_ref, self_ref, base_ref)
     finish(x_ref, acc_ref, field_ref, base_ref, out_ref)
 
@@ -221,12 +206,9 @@
     products = Products(rank_ref, at_ref, x_ref, left_ref, right_ref, near, acc_ref)
     products.clear()
 
-    def some(quarter, carry):
+    for quarter in range(QUARTERS):
         sums = products.far(quarter * far_step, far_step)
         products.add(sums + products.near(near_ref, quarter * near_step, near_step, 0))
-        return carry
-
-    lax.fori_loop(0, QUARTERS, some, 0)
     local_product(field_ref, shift_ref, self_ref, base_ref)
     for step, (column, scale) in enumerate(factor(columns(old_ref[1]))):
         steps_ref[step] = column
@@ -453,15 +435,13 @@
     owner_outs = [pltpu.VMEM((slots, 40, 128), BF16), pltpu.VMEM(whole, F32)]
     owner = call(
         first_owner_kernel,
-        [TABLE, TABLE, VMEM, KEPT, HBM, HBM, HBM, HBM, VMEM, VMEM],
+        [TABLE, TABLE, VMEM, KEPT, HBM, VMEM, VMEM, HBM, VMEM, VMEM],
         owner_outs,
         [
             pltpu.VMEM((near_blocks.shape[0] - KEPT_NEAR, size, size), BF16),
-            pltpu.VMEM(far_left.shape, BF16),
-            pltpu.VMEM(far_right.shape, BF16),
             pltpu.VMEM(self_blocks.shape, BF16),
             pltpu.VMEM(message, F32),
-            pltpu.SemaphoreType.DMA((QUARTERS, 4)),
+            pltpu.SemaphoreType.DMA((2,)),
         ],
     )
     next_owner = call(

time: 122 us -> 121 us (level)
  Pallas kernels: 15.8 us -> 14.2 us
    pallas_call x5, Pallas kernels: 15.8 us -> 14.2 us  [placed(): run(*(pltpu.with_memory_space_constraint(value, spec.memory_space) if spe...]
where the time goes in v7:
time: 121 us; the launch traced here: 120 us
  blocking collectives  105 us (87%)
  Pallas kernels  14.2 us (12%)
    all_to_all x4, blocking collectives, swap(): return lax.all_to_all(values, AXES, split_axis=0, concat_axis=0, tiled=True)  105 us
    pallas_call x5, Pallas kernels, placed(): run(*(pltpu.with_memory_space_constraint(value, spec.memory_space) if spe...  14.2 us

profile of v7, /device:TPU:1, one launch (start us, length us, event | category | flops | bytes accessed | tf_op | source)
XLA Modules:
  0.0 120.3 jit_solution(11953474211371525514)
XLA Ops:
  0.6 0.0 copy-start.2
  0.6 1.3 %send.1 = (bf16[128,16,256]{2,1,0:T(8,128)(2,1)S(1)}, s32[128]{0:T(128)S(4)}, s32[96]{0:T(128)S(4)}, s32[2,120]{1,0:T(2,128)S(4)}, bf16[4,256,256]{2,1,0:T(8,128)(2,1)S(1)}) custom-call(s32[128]{0:T(128)} %bitcast.1, s32[96]{0:T(128)} %rank_hbm.1, s32[2,120]{1,0:T(2,128)} %at_hbm.1, f32[8,16,256]{2,1,0:T(8,128)} %field_ref.5, bf16[24,256,256]{2,1,0:T(8,128)(2,1)} %near_ref.1), custom_call_target="tpu_custom_call" | custom-call | tf_op jit(solution)/shard_map/send/pallas_call | solution.py:390
  1.9 0.0 copy-start.1
  1.9 0.0 copy-start.4
  1.9 0.0 copy-start.5
  2.0 30.7 %all_to_all.20.x_ref = bf16[128,16,256]{2,1,0:T(8,128)(2,1)S(1)} all-to-all(bf16[128,16,256]{2,1,0:T(8,128)(2,1)S(1)} %get-tuple-element.19), channel_id=1, replica_groups=mesh['clus'=32,'grp'=4] {'clus','grp'}, dimensions={0} | all-to-all | bytes 2097152 | tf_op jit(solution)/shard_map/all_to_all | solution.py:403
  32.7 0.0 copy-done.2
  32.7 0.0 copy-done.1
  32.7 0.0 copy-done.4
  32.7 0.0 copy-done.5
  32.7 4.7 %owner.2 = (bf16[128,40,128]{2,1,0:T(8,128)(2,1)S(1)}, f32[8,16,256]{2,1,0:T(8,128)S(1)}) custom-call(s32[96]{0:T(128)S(4)} %get-tuple-element.17.rank_ref, s32[2,120]{1,0:T(2,128)S(4)} %get-tuple-element.18.at_ref, bf16[128,16,256]{2,1,0:T(8,128)(2,1)S(1)} %all_to_all.20.x_ref, bf16[4,256,256]{2,1,0:T(8,128)(2,1)S(1)} %get-tuple-element.20.kept_ref, ...), custom_call_target="tpu_custom_call" | custom-call | tf_op jit(solution)/shard_map/owner/pallas_call | solution.py:390
  37.5 0.0 copy-start.3
  37.5 25.8 %all_to_all.21.sums_ref = bf16[128,40,128]{2,1,0:T(8,128)(2,1)S(1)} all-to-all(bf16[128,40,128]{2,1,0:T(8,128)(2,1)S(1)} %get-tuple-element.21), channel_id=1, replica_groups=mesh['clus'=32,'grp'=4] {'clus','grp'}, dimensions={0} | all-to-all | bytes 2621440 | tf_op jit(solution)/shard_map/all_to_all | solution.py:403
  63.3 0.0 copy-start
  63.3 1.1 leaf.1
  64.4 23.1 %all_to_all.22.x_ref = bf16[128,16,256]{2,1,0:T(8,128)(2,1)S(1)} all-to-all(bf16[128,16,256]{2,1,0:T(8,128)(2,1)S(1)} %get-tuple-element.23), channel_id=1, replica_groups=mesh['clus'=32,'grp'=4] {'clus','grp'}, dimensions={0} | all-to-all | bytes 2097152 | tf_op jit(solution)/shard_map/all_to_all | solution.py:403
  87.5 0.0 copy-done.3
  87.5 0.0 copy-done
  87.5 4.6 %owner.3 = (bf16[128,40,128]{2,1,0:T(8,128)(2,1)S(1)}, f32[8,16,256]{2,1,0:T(8,128)S(1)}, f32[17,16,128]{2,1,0:T(8,128)S(1)}) custom-call(s32[96]{0:T(128)S(4)} %get-tuple-element.17.rank_ref, s32[2,120]{1,0:T(2,128)S(4)} %get-tuple-element.18.at_ref, bf16[128,16,256]{2,1,0:T(8,128)(2,1)S(1)} %all_to_all.22.x_ref, bf16[24,256,256]{2,1,0:T(8,128)(2,1)S(1)} %copy-done, ...), custom_call_target="tpu_custom_call" | custom-call | tf_op jit(solution)/shard_map/owner/pallas_call | solution.py:390
  92.1 25.8 %all_to_all.23.sums_ref = bf16[128,40,128]{2,1,0:T(8,128)(2,1)S(1)} all-to-all(bf16[128,40,128]{2,1,0:T(8,128)(2,1)S(1)} %get-tuple-element.26), channel_id=1, replica_groups=mesh['clus'=32,'grp'=4] {'clus','grp'}, dimensions={0} | all-to-all | bytes 2621440 | tf_op jit(solution)/shard_map/all_to_all | solution.py:403
  117.9 2.4 %final.1 = (f32[8,16,256]{2,1,0:T(8,128)}, f32[8,16,256]{2,1,0:T(8,128)}) custom-call(s32[128]{0:T(128)S(4)} %get-tuple-element.16.leaf_ref, bf16[128,40,128]{2,1,0:T(8,128)(2,1)S(1)} %all_to_all.23.sums_ref, f32[8,16,256]{2,1,0:T(8,128)S(1)} %get-tuple-element.27.base_ref, f32[8,16,256]{2,1,0:T(8,128)S(1)} %copy-done.4, ...), custom_call_target="tpu_custom_call" | custom-call | tf_op jit(solution)/shard_map/final/pallas_call | solution.py:390
Async XLA Ops:
  0.6 32.1 %copy-start.2 = (bf16[96,32,256]{2,1,0:T(8,128)(2,1)S(1)}, bf16[96,32,256]{2,1,0:T(8,128)(2,1)}, u32[]{:S(2)}) copy-start(bf16[96,32,256]{2,1,0:T(8,128)(2,1)} %right_ref.3) | copy-start | bytes 4718596
  1.9 30.8 %copy-start.1 = (bf16[96,32,256]{2,1,0:T(8,128)(2,1)S(1)}, bf16[96,32,256]{2,1,0:T(8,128)(2,1)}, u32[]{:S(2)}) copy-start(bf16[96,32,256]{2,1,0:T(8,128)(2,1)} %left_ref.3) | copy-start | bytes 4718596
  1.9 30.8 %copy-start.4 = (f32[8,16,256]{2,1,0:T(8,128)S(1)}, f32[8,16,256]{2,1,0:T(8,128)}, u32[]{:S(2)}) copy-start(f32[8,16,256]{2,1,0:T(8,128)} %field_ref.5) | copy-start | bytes 393220
  1.9 30.7 %copy-start.5 = (f32[8,256]{1,0:T(8,128)S(1)}, f32[8,256]{1,0:T(8,128)}, u32[]{:S(2)}) copy-start(f32[8,256]{1,0:T(8,128)} %shift_ref.3) | copy-start | bytes 24580
  37.5 50.0 %copy-start.3 = (bf16[8,256,256]{2,1,0:T(8,128)(2,1)S(1)}, bf16[8,256,256]{2,1,0:T(8,128)(2,1)}, u32[]{:S(2)}) copy-start(bf16[8,256,256]{2,1,0:T(8,128)(2,1)} %self_ref.1) | copy-start | bytes 3145732
  63.3 24.2 %copy-start = (bf16[24,256,256]{2,1,0:T(8,128)(2,1)S(1)}, bf16[24,256,256]{2,1,0:T(8,128)(2,1)}, u32[]{:S(2)}) copy-start(bf16[24,256,256]{2,1,0:T(8,128)(2,1)} %near_ref.1) | copy-start | bytes 9437188

commit v8 on v7

--- a/solution.py
+++ b/solution.py
@@ -48,6 +48,21 @@
 
 def combine(field, kron):
     return jnp.dot(kron, field, precision=HIGHEST, preferred_element_type=F32)
+
+
+def pieces(values):
+    high = values.astype(BF16)
+    return high, (values - high.astype(F32)).astype(BF16)
+
+
+def combine_pieces(field, kron):
+    high, low = pieces(field)
+    kron_high, kron_low = pieces(kron)
+    main = jnp.dot(
+        jnp.concatenate([kron_high, kron_low], axis=0), high, preferred_element_type=F32
+    )
+    rest = jnp.dot(kron_high, low, preferred_element_type=F32)
+    return main[0:128] + (main[128:256] + rest)
 
 
 def gram(left, right):
@@ -191,8 +206,8 @@
         products.add(sums + products.near(kept_ref, quarter * kept_step, kept_step, 0))
     near_copy.wait()
     self_copy.wait()
+    local_product(field_ref, shift_ref, self_ref, base_ref)
     products.add(products.near(near_ref, 0, rest, kept))
-    local_product(field_ref, shift_ref, self_ref, base_ref)
     finish(x_ref, acc_ref, field_ref, base_ref, out_ref)
 
 
@@ -208,8 +223,9 @@
 
     for quarter in range(QUARTERS):
         sums = products.far(quarter * far_step, far_step)
+        if quarter == QUARTERS - 1:
+            local_product(field_ref, shift_ref, self_ref, base_ref)
         products.add(sums + products.near(near_ref, quarter * near_step, near_step, 0))
-    local_product(field_ref, shift_ref, self_ref, base_ref)
     for step, (column, scale) in enumerate(factor(columns(old_ref[1]))):
         steps_ref[step] = column
         steps_ref[16, step : step + 1] = scale
@@ -349,7 +365,7 @@
 
 def final_kernel(
     leaf_ref, sums_ref, base_ref, field_ref, residual_ref, image_ref, small_ref, steps_ref,
-    solution_ref, out_ref, acc_ref, acc_a, acc_b, acc_c,
+    solution_hbm, out_hbm, acc_ref, acc_a, acc_b, acc_c, solution_ref, out_ref, sems,
 ):
     acc_ref[...] = base_ref[...]
     tiles, returned = add_returned(leaf_ref, sums_ref, (acc_ref, acc_a, acc_b, acc_c))
@@ -361,16 +377,22 @@
     moved = columns(moved)
     step = solve([curve[at] - moved[at] for at in range(16)], next_norm)
     kron_coef = kron_rows(coef)
-    part = combine(field_ref[...].reshape(128, 256), kron_rows(small_ref[2]))
+    part = combine_pieces(field_ref[...].reshape(128, 256), kron_rows(small_ref[2]))
     residual = residual_ref[...].reshape(128, 256)
-    direction = residual + combine(field_ref[...].reshape(128, 256), kron_coef)
-    image = returned.reshape(128, 256) + combine(
+    direction = residual + combine_pieces(field_ref[...].reshape(128, 256), kron_coef)
+    image = returned.reshape(128, 256) + combine_pieces(
         image_ref[...].reshape(128, 256), kron_coef
     )
     kron_step = kron_rows(step)
-    answer = part + combine(direction, kron_step)
+    answer = part + combine_pieces(direction, kron_step)
     solution_ref[...] = answer.reshape(solution_ref.shape)
-    out_ref[...] = (residual - combine(image, kron_step)).reshape(out_ref.shape)
+    solution_copy = pltpu.make_async_copy(solution_ref, solution_hbm, sems.at[0])
+    solution_copy.start()
+    out_ref[...] = (residual - combine_pieces(image, kron_step)).reshape(out_ref.shape)
+    out_copy = pltpu.make_async_copy(out_ref, out_hbm, sems.at[1])
+    out_copy.start()
+    solution_copy.wait()
+    out_copy.wait()
 
 
 def call(kernel, ins, outs, scratch, cost=None):
@@ -464,8 +486,8 @@
     final = call(
         final_kernel,
         [TABLE, VMEM, KEPT, VMEM, KEPT, KEPT, KEPT, KEPT],
-        [jax.ShapeDtypeStruct(whole, F32), jax.ShapeDtypeStruct(whole, F32)],
-        [pltpu.VMEM(whole, F32)] * 4,
+        [pltpu.HBM(whole, F32), pltpu.HBM(whole, F32)],
+        [pltpu.VMEM(whole, F32)] * 6 + [pltpu.SemaphoreType.DMA((2,))],
     )
     stored = (near_blocks, far_left, far_right, self_blocks)
 

time: 121 us -> 120 us (level)
  no operation moved by 1% of the time
where the time goes in v8:
time: 120 us
  blocking collectives  105 us (88%)
  Pallas kernels  13.8 us (12%)
    all_to_all x4, blocking collectives, swap(): return lax.all_to_all(values, AXES, split_axis=0, concat_axis=0, tiled=True)  105 us
    pallas_call x5, Pallas kernels, placed(): run(*(pltpu.with_memory_space_constraint(value, spec.memory_space) if spe...  13.8 us

profile of v8, /device:TPU:1, one launch (start us, length us, event | category | flops | bytes accessed | tf_op | source)
XLA Modules:
  0.0 120.0 jit_solution(6839757993092395972)
XLA Ops:
  0.6 0.0 copy-start.2
  0.6 1.3 %send.1 = (bf16[128,16,256]{2,1,0:T(8,128)(2,1)S(1)}, s32[128]{0:T(128)S(4)}, s32[96]{0:T(128)S(4)}, s32[2,120]{1,0:T(2,128)S(4)}, bf16[4,256,256]{2,1,0:T(8,128)(2,1)S(1)}) custom-call(s32[128]{0:T(128)} %bitcast.1, s32[96]{0:T(128)} %rank_hbm.1, s32[2,120]{1,0:T(2,128)} %at_hbm.1, f32[8,16,256]{2,1,0:T(8,128)} %field_ref.5, bf16[24,256,256]{2,1,0:T(8,128)(2,1)} %near_ref.1), custom_call_target="tpu_custom_call" | custom-call | tf_op jit(solution)/shard_map/send/pallas_call | solution.py:412
  1.9 0.0 copy-start.1
  1.9 0.0 copy-start.4
  1.9 0.0 copy-start.5
  2.0 30.7 %all_to_all.20.x_ref = bf16[128,16,256]{2,1,0:T(8,128)(2,1)S(1)} all-to-all(bf16[128,16,256]{2,1,0:T(8,128)(2,1)S(1)} %get-tuple-element.19), channel_id=1, replica_groups=mesh['clus'=32,'grp'=4] {'clus','grp'}, dimensions={0} | all-to-all | bytes 2097152 | tf_op jit(solution)/shard_map/all_to_all | solution.py:425
  32.7 0.0 copy-done.2
  32.7 0.0 copy-done.1
  32.7 0.0 copy-done.4
  32.7 0.0 copy-done.5
  32.7 4.7 %owner.2 = (bf16[128,40,128]{2,1,0:T(8,128)(2,1)S(1)}, f32[8,16,256]{2,1,0:T(8,128)S(1)}) custom-call(s32[96]{0:T(128)S(4)} %get-tuple-element.17.rank_ref, s32[2,120]{1,0:T(2,128)S(4)} %get-tuple-element.18.at_ref, bf16[128,16,256]{2,1,0:T(8,128)(2,1)S(1)} %all_to_all.20.x_ref, bf16[4,256,256]{2,1,0:T(8,128)(2,1)S(1)} %get-tuple-element.20.kept_ref, ...), custom_call_target="tpu_custom_call" | custom-call | tf_op jit(solution)/shard_map/owner/pallas_call | solution.py:412
  37.4 0.0 copy-start.3
  37.4 25.8 %all_to_all.21.sums_ref = bf16[128,40,128]{2,1,0:T(8,128)(2,1)S(1)} all-to-all(bf16[128,40,128]{2,1,0:T(8,128)(2,1)S(1)} %get-tuple-element.21), channel_id=1, replica_groups=mesh['clus'=32,'grp'=4] {'clus','grp'}, dimensions={0} | all-to-all | bytes 2621440 | tf_op jit(solution)/shard_map/all_to_all | solution.py:425
  63.2 0.0 copy-start
  63.2 1.1 leaf.1
  64.4 23.1 %all_to_all.22.x_ref = bf16[128,16,256]{2,1,0:T(8,128)(2,1)S(1)} all-to-all(bf16[128,16,256]{2,1,0:T(8,128)(2,1)S(1)} %get-tuple-element.23), channel_id=1, replica_groups=mesh['clus'=32,'grp'=4] {'clus','grp'}, dimensions={0} | all-to-all | bytes 2097152 | tf_op jit(solution)/shard_map/all_to_all | solution.py:425
  87.4 0.0 copy-done.3
  87.4 0.0 copy-done
  87.4 4.5 %owner.3 = (bf16[128,40,128]{2,1,0:T(8,128)(2,1)S(1)}, f32[8,16,256]{2,1,0:T(8,128)S(1)}, f32[17,16,128]{2,1,0:T(8,128)S(1)}) custom-call(s32[96]{0:T(128)S(4)} %get-tuple-element.17.rank_ref, s32[2,120]{1,0:T(2,128)S(4)} %get-tuple-element.18.at_ref, bf16[128,16,256]{2,1,0:T(8,128)(2,1)S(1)} %all_to_all.22.x_ref, bf16[24,256,256]{2,1,0:T(8,128)(2,1)S(1)} %copy-done, ...), custom_call_target="tpu_custom_call" | custom-call | tf_op jit(solution)/shard_map/owner/pallas_call | solution.py:412
  92.0 25.8 %all_to_all.23.sums_ref = bf16[128,40,128]{2,1,0:T(8,128)(2,1)S(1)} all-to-all(bf16[128,40,128]{2,1,0:T(8,128)(2,1)S(1)} %get-tuple-element.26), channel_id=1, replica_groups=mesh['clus'=32,'grp'=4] {'clus','grp'}, dimensions={0} | all-to-all | bytes 2621440 | tf_op jit(solution)/shard_map/all_to_all | solution.py:425
  117.8 2.2 %final.1 = (f32[8,16,256]{2,1,0:T(8,128)}, f32[8,16,256]{2,1,0:T(8,128)}) custom-call(s32[128]{0:T(128)S(4)} %get-tuple-element.16.leaf_ref, bf16[128,40,128]{2,1,0:T(8,128)(2,1)S(1)} %all_to_all.23.sums_ref, f32[8,16,256]{2,1,0:T(8,128)S(1)} %get-tuple-element.27.base_ref, f32[8,16,256]{2,1,0:T(8,128)S(1)} %copy-done.4, ...), custom_call_target="tpu_custom_call" | custom-call | tf_op jit(solution)/shard_map/final/pallas_call | solution.py:412
Async XLA Ops:
  0.6 32.1 %copy-start.2 = (bf16[96,32,256]{2,1,0:T(8,128)(2,1)S(1)}, bf16[96,32,256]{2,1,0:T(8,128)(2,1)}, u32[]{:S(2)}) copy-start(bf16[96,32,256]{2,1,0:T(8,128)(2,1)} %right_ref.3) | copy-start | bytes 4718596
  1.9 30.8 %copy-start.1 = (bf16[96,32,256]{2,1,0:T(8,128)(2,1)S(1)}, bf16[96,32,256]{2,1,0:T(8,128)(2,1)}, u32[]{:S(2)}) copy-start(bf16[96,32,256]{2,1,0:T(8,128)(2,1)} %left_ref.3) | copy-start | bytes 4718596
  1.9 30.8 %copy-start.4 = (f32[8,16,256]{2,1,0:T(8,128)S(1)}, f32[8,16,256]{2,1,0:T(8,128)}, u32[]{:S(2)}) copy-start(f32[8,16,256]{2,1,0:T(8,128)} %field_ref.5) | copy-start | bytes 393220
  1.9 30.7 %copy-start.5 = (f32[8,256]{1,0:T(8,128)S(1)}, f32[8,256]{1,0:T(8,128)}, u32[]{:S(2)}) copy-start(f32[8,256]{1,0:T(8,128)} %shift_ref.3) | copy-start | bytes 24580
  37.4 50.0 %copy-start.3 = (bf16[8,256,256]{2,1,0:T(8,128)(2,1)S(1)}, bf16[8,256,256]{2,1,0:T(8,128)(2,1)}, u32[]{:S(2)}) copy-start(bf16[8,256,256]{2,1,0:T(8,128)(2,1)} %self_ref.1) | copy-start | bytes 3145732
  63.2 24.2 %copy-start = (bf16[24,256,256]{2,1,0:T(8,128)(2,1)S(1)}, bf16[24,256,256]{2,1,0:T(8,128)(2,1)}, u32[]{:S(2)}) copy-start(bf16[24,256,256]{2,1,0:T(8,128)(2,1)} %near_ref.1) | copy-start | bytes 9437188

commit v9 on v8

--- a/solution.py
+++ b/solution.py
@@ -65,8 +65,20 @@
     return main[0:128] + (main[128:256] + rest)
 
 
-def gram(left, right):
-    return fold(lax.dot_general(left, right, NT, precision=HIGHEST, preferred_element_type=F32))
+def local_grams(field, image):
+    high, low = pieces(field)
+    image_high, image_low = pieces(image)
+    main = lax.dot_general(
+        jnp.concatenate([high, low], axis=0),
+        jnp.concatenate([image_high, high], axis=0),
+        NT,
+        preferred_element_type=F32,
+    )
+    rest = lax.dot_general(
+        high, jnp.concatenate([image_low, low], axis=0), NT, preferred_element_type=F32
+    )
+    both = main[0:128] + (main[128:256] + rest)
+    return fold(both[:, 0:128]), fold(both[:, 128:256])
 
 
 def columns(matrix):
@@ -302,8 +314,7 @@
 def finish(x_ref, acc_ref, field_ref, base_ref, out_ref):
     slots = x_ref.shape[0]
     fields = field_ref[...].reshape(128, 256)
-    curve = gram(fields, base_ref[...].reshape(128, 256))
-    norm = gram(fields, fields)
+    curve, norm = local_grams(fields, base_ref[...].reshape(128, 256))
     products = jnp.zeros((128, 128), F32)
     for at in range(slots // 16):
         here = slice(at * 16, at * 16 + 16)

time: 120 us -> 120 us (level)
  no operation moved by 1% of the time
where the time goes in v9:
time: 120 us
  blocking collectives  105 us (88%)
  Pallas kernels  13.7 us (11%)
    all_to_all x4, blocking collectives, swap(): return lax.all_to_all(values, AXES, split_axis=0, concat_axis=0, tiled=True)  105 us
    pallas_call x5, Pallas kernels, placed(): run(*(pltpu.with_memory_space_constraint(value, spec.memory_space) if spe...  13.7 us

profile of v9, /device:TPU:1, one launch (start us, length us, event | category | flops | bytes accessed | tf_op | source)
XLA Modules:
  0.0 119.8 jit_solution(16325555764776151722)
XLA Ops:
  0.6 0.0 copy-start.2
  0.6 1.3 %send.1 = (bf16[128,16,256]{2,1,0:T(8,128)(2,1)S(1)}, s32[128]{0:T(128)S(4)}, s32[96]{0:T(128)S(4)}, s32[2,120]{1,0:T(2,128)S(4)}, bf16[4,256,256]{2,1,0:T(8,128)(2,1)S(1)}) custom-call(s32[128]{0:T(128)} %bitcast.1, s32[96]{0:T(128)} %rank_hbm.1, s32[2,120]{1,0:T(2,128)} %at_hbm.1, f32[8,16,256]{2,1,0:T(8,128)} %field_ref.5, bf16[24,256,256]{2,1,0:T(8,128)(2,1)} %near_ref.1), custom_call_target="tpu_custom_call" | custom-call | tf_op jit(solution)/shard_map/send/pallas_call | solution.py:423
  1.9 0.0 copy-start.1
  1.9 0.0 copy-start.4
  1.9 0.0 copy-start.5
  2.0 30.7 %all_to_all.20.x_ref = bf16[128,16,256]{2,1,0:T(8,128)(2,1)S(1)} all-to-all(bf16[128,16,256]{2,1,0:T(8,128)(2,1)S(1)} %get-tuple-element.19), channel_id=1, replica_groups=mesh['clus'=32,'grp'=4] {'clus','grp'}, dimensions={0} | all-to-all | bytes 2097152 | tf_op jit(solution)/shard_map/all_to_all | solution.py:436
  32.7 0.0 copy-done.2
  32.7 0.0 copy-done.1
  32.7 0.0 copy-done.4
  32.7 0.0 copy-done.5
  32.7 4.6 %owner.2 = (bf16[128,40,128]{2,1,0:T(8,128)(2,1)S(1)}, f32[8,16,256]{2,1,0:T(8,128)S(1)}) custom-call(s32[96]{0:T(128)S(4)} %get-tuple-element.17.rank_ref, s32[2,120]{1,0:T(2,128)S(4)} %get-tuple-element.18.at_ref, bf16[128,16,256]{2,1,0:T(8,128)(2,1)S(1)} %all_to_all.20.x_ref, bf16[4,256,256]{2,1,0:T(8,128)(2,1)S(1)} %get-tuple-element.20.kept_ref, ...), custom_call_target="tpu_custom_call" | custom-call | tf_op jit(solution)/shard_map/owner/pallas_call | solution.py:423
  37.3 0.0 copy-start.3
  37.3 25.8 %all_to_all.21.sums_ref = bf16[128,40,128]{2,1,0:T(8,128)(2,1)S(1)} all-to-all(bf16[128,40,128]{2,1,0:T(8,128)(2,1)S(1)} %get-tuple-element.21), channel_id=1, replica_groups=mesh['clus'=32,'grp'=4] {'clus','grp'}, dimensions={0} | all-to-all | bytes 2621440 | tf_op jit(solution)/shard_map/all_to_all | solution.py:436
  63.1 0.0 copy-start
  63.1 1.1 leaf.1
  64.3 23.1 %all_to_all.22.x_ref = bf16[128,16,256]{2,1,0:T(8,128)(2,1)S(1)} all-to-all(bf16[128,16,256]{2,1,0:T(8,128)(2,1)S(1)} %get-tuple-element.23), channel_id=1, replica_groups=mesh['clus'=32,'grp'=4] {'clus','grp'}, dimensions={0} | all-to-all | bytes 2097152 | tf_op jit(solution)/shard_map/all_to_all | solution.py:436
  87.3 0.0 copy-done.3
  87.3 0.0 copy-done
  87.3 4.5 %owner.3 = (bf16[128,40,128]{2,1,0:T(8,128)(2,1)S(1)}, f32[8,16,256]{2,1,0:T(8,128)S(1)}, f32[17,16,128]{2,1,0:T(8,128)S(1)}) custom-call(s32[96]{0:T(128)S(4)} %get-tuple-element.17.rank_ref, s32[2,120]{1,0:T(2,128)S(4)} %get-tuple-element.18.at_ref, bf16[128,16,256]{2,1,0:T(8,128)(2,1)S(1)} %all_to_all.22.x_ref, bf16[24,256,256]{2,1,0:T(8,128)(2,1)S(1)} %copy-done, ...), custom_call_target="tpu_custom_call" | custom-call | tf_op jit(solution)/shard_map/owner/pallas_call | solution.py:423
  91.8 25.8 %all_to_all.23.sums_ref = bf16[128,40,128]{2,1,0:T(8,128)(2,1)S(1)} all-to-all(bf16[128,40,128]{2,1,0:T(8,128)(2,1)S(1)} %get-tuple-element.26), channel_id=1, replica_groups=mesh['clus'=32,'grp'=4] {'clus','grp'}, dimensions={0} | all-to-all | bytes 2621440 | tf_op jit(solution)/shard_map/all_to_all | solution.py:436
  117.6 2.2 %final.1 = (f32[8,16,256]{2,1,0:T(8,128)}, f32[8,16,256]{2,1,0:T(8,128)}) custom-call(s32[128]{0:T(128)S(4)} %get-tuple-element.16.leaf_ref, bf16[128,40,128]{2,1,0:T(8,128)(2,1)S(1)} %all_to_all.23.sums_ref, f32[8,16,256]{2,1,0:T(8,128)S(1)} %get-tuple-element.27.base_ref, f32[8,16,256]{2,1,0:T(8,128)S(1)} %copy-done.4, ...), custom_call_target="tpu_custom_call" | custom-call | tf_op jit(solution)/shard_map/final/pallas_call | solution.py:423
Async XLA Ops:
  0.6 32.1 %copy-start.2 = (bf16[96,32,256]{2,1,0:T(8,128)(2,1)S(1)}, bf16[96,32,256]{2,1,0:T(8,128)(2,1)}, u32[]{:S(2)}) copy-start(bf16[96,32,256]{2,1,0:T(8,128)(2,1)} %right_ref.3) | copy-start | bytes 4718596
  1.9 30.8 %copy-start.1 = (bf16[96,32,256]{2,1,0:T(8,128)(2,1)S(1)}, bf16[96,32,256]{2,1,0:T(8,128)(2,1)}, u32[]{:S(2)}) copy-start(bf16[96,32,256]{2,1,0:T(8,128)(2,1)} %left_ref.3) | copy-start | bytes 4718596
  1.9 30.8 %copy-start.4 = (f32[8,16,256]{2,1,0:T(8,128)S(1)}, f32[8,16,256]{2,1,0:T(8,128)}, u32[]{:S(2)}) copy-start(f32[8,16,256]{2,1,0:T(8,128)} %field_ref.5) | copy-start | bytes 393220
  1.9 30.7 %copy-start.5 = (f32[8,256]{1,0:T(8,128)S(1)}, f32[8,256]{1,0:T(8,128)}, u32[]{:S(2)}) copy-start(f32[8,256]{1,0:T(8,128)} %shift_ref.3) | copy-start | bytes 24580
  37.3 50.0 %copy-start.3 = (bf16[8,256,256]{2,1,0:T(8,128)(2,1)S(1)}, bf16[8,256,256]{2,1,0:T(8,128)(2,1)}, u32[]{:S(2)}) copy-start(bf16[8,256,256]{2,1,0:T(8,128)(2,1)} %self_ref.1) | copy-start | bytes 3145732
  63.1 24.2 %copy-start = (bf16[24,256,256]{2,1,0:T(8,128)(2,1)S(1)}, bf16[24,256,256]{2,1,0:T(8,128)(2,1)}, u32[]{:S(2)}) copy-start(bf16[24,256,256]{2,1,0:T(8,128)(2,1)} %near_ref.1) | copy-start | bytes 9437188
